TPU v7x, 32 devices: a whole 2x2x4 slice. The times are simulated.
32 devices in a mesh: seq: 8 (over z, y), fsdp: 4 (over x, core).
Axes of the slice: x: 2, y: 2, z: 4, core: 2. Of those that a mesh axis runs over, the one named last changes fastest.
Arguments:
- tokens: bfloat16 [8, 1024, 1024], P('fsdp', 'seq'), may hold values from -6 to 6
- doc_bounds: int32 [8, 2], P('fsdp'), may hold values from 1 to 1024, as said below
- w_qkv: bfloat16 [2, 1024, 3072], P(None, ('seq', 'fsdp')), may hold values from -0.1875 to 0.1875
- w_out: bfloat16 [2, 1024, 1024], P(None, ('seq', 'fsdp')), may hold values from -1.5 to 1.5
- w_gate: bfloat16 [2, 1024, 2816], P(None, ('seq', 'fsdp')), may hold values from -0.1875 to 0.1875
- w_up: bfloat16 [2, 1024, 2816], P(None, ('seq', 'fsdp')), may hold values from -0.1875 to 0.1875
- w_down: bfloat16 [2, 2816, 1024], P(None, ('seq', 'fsdp')), may hold values from -0.109375 to 0.109375
- norm_attn: bfloat16 [2, 1024], P(None, ('seq', 'fsdp')), may hold values from 0.5 to 1.5
- norm_mlp: bfloat16 [2, 1024], P(None, ('seq', 'fsdp')), may hold values from 0.5 to 1.5
- out_grad: bfloat16 [8, 1024, 1024], P('fsdp', 'seq'), may hold values from -6 to 6
Outputs:
- hidden_out: float32 [8, 1024, 1024], P('fsdp', 'seq')
- in_grad: float32 [8, 1024, 1024], P('fsdp', 'seq')
- grad_qkv: float32 [2, 1024, 3072], P(None, ('seq', 'fsdp'))
- grad_out: float32 [2, 1024, 1024], P(None, ('seq', 'fsdp'))
- grad_gate: float32 [2, 1024, 2816], P(None, ('seq', 'fsdp'))
- grad_up: float32 [2, 1024, 2816], P(None, ('seq', 'fsdp'))
- grad_down: float32 [2, 2816, 1024], P(None, ('seq', 'fsdp'))
- grad_norm_attn: float32 [2, 1024], P(None, ('seq', 'fsdp'))
- grad_norm_mlp: float32 [2, 1024], P(None, ('seq', 'fsdp'))
- v1_grad: float32 [8, 1024, 1024], P('fsdp', 'seq')
Inputs may be any that keep to these rules, and one draw needn't show every extreme that they name: `doc_bounds`: per slot, column 0 is the first position of the slot's long document, 1 to 64; positions before it form a short document. Column 1 is the end of the valid tokens, 897 to 1024; positions from it on are padding.
All inputs are finite; a program needn't handle non-finite values.
Results may differ from a plain program's by a relative error of at most 0.033.
Values may be sent and summed in bfloat16 or wider, within the bound.
No kernel may reach another device: no remote copies, remote signals or barrier semaphores. Data moves between devices by JAX's collectives and lax.ppermute only.
A program may use at most 384 MiB of HBM per device.

v0:
```python
import jax
import jax.numpy as jnp
from jax import lax
from jax.sharding import PartitionSpec as P

H = 16
HD = 64
LAYERS = 2


epsilon = 1e-05
masked_score = -1e30


def as_sent(shard):

    def short(part):
        return part.astype(jnp.bfloat16) if part.dtype == jnp.float32 else part

    return jax.tree.map(short, shard)


def labels(position_index, bounds):
    start_at = bounds[:, 0:1]
    end_at = bounds[:, 1:2]
    index_row = position_index[None, :]
    segment = jnp.where(index_row < start_at, 0, jnp.where(index_row < end_at, 1, 2)).astype(
        jnp.int32
    )
    doc_base = jnp.where(index_row < start_at, 0, jnp.where(index_row < end_at, start_at, end_at))
    return (segment, index_row - doc_base)


def rotary(positions):
    frequency = 10000.0 ** (-jnp.arange(HD // 2, dtype=jnp.float32) * 2.0 / HD)
    angles = positions.astype(jnp.float32)[..., None] * frequency
    return (jnp.cos(angles)[:, :, None, :], jnp.sin(angles)[:, :, None, :])


def rotate(rows_in, cosine_table, sine_table):
    half_size = rows_in.shape[-1] // 2
    first_half = rows_in[..., :half_size]
    second_half = rows_in[..., half_size:]
    return jnp.concatenate(
        [
            first_half * cosine_table - second_half * sine_table,
            second_half * cosine_table + first_half * sine_table,
        ],
        axis=-1,
    )


def normalize(hidden):
    inverse = lax.rsqrt(jnp.mean(hidden * hidden, axis=-1, keepdims=True) + epsilon)
    return (hidden * inverse, inverse)


def norm_back(upstream, normed, inverse, gain_row):
    scaled = upstream * gain_row
    inner_mean = jnp.mean(scaled * normed, axis=-1, keepdims=True)
    return (inverse * (scaled - normed * inner_mean), jnp.sum(upstream * normed, axis=0))


def allowed_mask(query_index, query_segment, key_index, key_segment):
    causal = key_index[None, :] <= query_index[:, None]
    same = key_segment[:, None, :] == query_segment[:, :, None]
    return (causal[None] & same)[:, :, None, :]


def block_size():
    return 512


def block_of(array, start, block_rows, head_count):
    piece = lax.dynamic_slice_in_dim(array, start, block_rows, 1)
    return piece.reshape(piece.shape[0], block_rows, head_count, HD)


def forward_block(
    running, queries, query_index, query_segment, key_block, value_block, key_index, key_segment
):
    row_max, row_total, summed = running
    raw_scores = jnp.einsum(
        "sqhd,skhd->sqhk", queries, key_block, preferred_element_type=jnp.float32
    )
    allowed = allowed_mask(query_index, query_segment, key_index, key_segment)
    scores = jnp.where(allowed, raw_scores * 0.125, masked_score)
    new_max = jnp.maximum(row_max, jnp.max(scores, axis=-1))
    rescale = jnp.exp(row_max - new_max)
    weights = jnp.where(allowed, jnp.exp(scores - new_max[..., None]), 0.0)
    row_total = row_total * rescale + jnp.sum(weights, axis=-1)
    summed = summed * rescale[..., None] + jnp.einsum(
        "sqhk,skhd->sqhd",
        weights.astype(jnp.bfloat16),
        value_block,
        preferred_element_type=jnp.float32,
    )
    return (new_max, row_total, summed)


def block_grads(
    queries,
    grads_heads,
    logsum,
    row_delta,
    query_index,
    query_segment,
    key_block,
    value_block,
    key_index,
    key_segment,
):
    raw_scores = jnp.einsum(
        "sqhd,skhd->sqhk", queries, key_block, preferred_element_type=jnp.float32
    )
    allowed = allowed_mask(query_index, query_segment, key_index, key_segment)
    probability = jnp.where(allowed, jnp.exp(raw_scores * 0.125 - logsum[..., None]), 0.0)
    prob_grad = jnp.einsum(
        "sqhd,skhd->sqhk", grads_heads, value_block, preferred_element_type=jnp.float32
    )
    score_grad = (probability * (prob_grad - row_delta[..., None]) * 0.125).astype(jnp.bfloat16)
    return (score_grad, probability.astype(jnp.bfloat16))


def shards(tokens, doc_bounds, w_qkv, w_out, w_gate, w_up, w_down, norm_attn, norm_mlp, out_grad):
    head_count = H
    slot_count, local_rows, width = tokens.shape
    rows_all = slot_count * local_rows
    offset = lax.axis_index("seq") * local_rows
    token_index = offset + jnp.arange(local_rows, dtype=jnp.int32)
    token_segment, token_position = labels(token_index, doc_bounds)
    cosine_table, sine_table = rotary(token_position)
    valid = (token_segment < 2).astype(jnp.float32)[..., None]
    hidden = tokens.reshape(rows_all, width).astype(jnp.float32)

    def heads(flat):
        return flat.reshape(slot_count, local_rows, head_count, HD)

    def layer_shards(layer_number):
        return (
            w_qkv[layer_number],
            w_out[layer_number],
            w_gate[layer_number],
            w_up[layer_number],
            w_down[layer_number],
            norm_attn[layer_number],
            norm_mlp[layer_number],
        )

    saved = []
    first_values = None
    for layer_number in range(LAYERS):
        gathered = lax.all_gather(
            as_sent(layer_shards(layer_number)), ("seq", "fsdp"), axis=0, tiled=True
        )
        qkv_w, out_w, gate_w, up_w, down_w, attn_gain, mlp_gain = gathered
        normed_attn, inverse_attn = normalize(hidden)
        attn_in = (normed_attn * attn_gain.astype(jnp.float32)).astype(jnp.bfloat16)
        projected = jnp.dot(attn_in, qkv_w, preferred_element_type=jnp.float32)
        queries = rotate(heads(projected[:, :width]), cosine_table, sine_table).astype(jnp.bfloat16)
        key_heads = rotate(heads(projected[:, width : 2 * width]), cosine_table, sine_table).astype(
            jnp.bfloat16
        )
        own_values = projected[:, 2 * width :]
        if first_values is None:
            first_values = own_values
            blended = own_values
        else:
            blended = 0.5 * own_values + 0.5 * first_values
        value_rows = blended.astype(jnp.bfloat16)
        initial = (
            jnp.full((slot_count, local_rows, head_count), masked_score, jnp.float32),
            jnp.zeros((slot_count, local_rows, head_count), jnp.float32),
            jnp.zeros((slot_count, local_rows, head_count, HD), jnp.float32),
        )
        key_piece_rows = lax.all_gather(
            key_heads.reshape(slot_count, local_rows, width), "seq", axis=1, tiled=True
        )
        value_piece_rows = lax.all_gather(
            value_rows.reshape(slot_count, local_rows, width), "seq", axis=1, tiled=True
        )
        attend_block_rows = block_size()

        def step(number, state):
            start = number * attend_block_rows
            key_block = block_of(key_piece_rows, start, attend_block_rows, head_count)
            value_block = block_of(value_piece_rows, start, attend_block_rows, head_count)
            key_index = start + jnp.arange(attend_block_rows, dtype=jnp.int32)
            key_segment, unused = labels(key_index, doc_bounds)

            def step_work(inner_state):
                return forward_block(
                    inner_state,
                    queries,
                    token_index,
                    token_segment,
                    key_block,
                    value_block,
                    key_index,
                    key_segment,
                )

            return lax.cond(
                key_index[0] <= token_index[-1], step_work, lambda inner_state: inner_state, state
            )

        row_max, row_total, summed = lax.fori_loop(
            0, key_piece_rows.shape[1] // attend_block_rows, step, initial
        )
        attn_out = summed / row_total[..., None]
        logsum = row_max + jnp.log(row_total)
        attn_bf = attn_out.reshape(rows_all, width).astype(jnp.bfloat16)
        middle = hidden + jnp.dot(attn_bf, out_w, preferred_element_type=jnp.float32)
        normed_mlp, inverse_mlp = normalize(middle)
        mlp_in = (normed_mlp * mlp_gain.astype(jnp.float32)).astype(jnp.bfloat16)
        gate_pre = jnp.dot(mlp_in, gate_w, preferred_element_type=jnp.float32)
        up_pre = jnp.dot(mlp_in, up_w, preferred_element_type=jnp.float32)
        activated = (jax.nn.silu(gate_pre) * up_pre).astype(jnp.bfloat16)
        kept_weights = None
        saved.append(
            (
                normed_attn,
                inverse_attn,
                attn_in,
                queries,
                key_heads,
                value_rows,
                attn_out,
                attn_bf,
                logsum,
                normed_mlp,
                inverse_mlp,
                mlp_in,
                gate_pre,
                up_pre,
                activated,
                kept_weights,
            )
        )
        hidden = middle + jnp.dot(activated, down_w, preferred_element_type=jnp.float32)
    hidden_out = hidden.reshape(slot_count, local_rows, width) * valid
    upstream = (out_grad.astype(jnp.float32) * valid).reshape(rows_all, width)
    value_carry = jnp.zeros((rows_all, width), jnp.float32)
    first_grad = value_carry
    grads_per_layer = [None] * LAYERS
    for layer_number in reversed(range(LAYERS)):
        (
            normed_attn,
            inverse_attn,
            attn_in,
            queries,
            key_heads,
            value_rows,
            attn_out,
            attn_bf,
            logsum,
            normed_mlp,
            inverse_mlp,
            mlp_in,
            gate_pre,
            up_pre,
            activated,
            kept_weights,
        ) = saved[layer_number]
        gathered = lax.all_gather(
            as_sent(layer_shards(layer_number)), ("seq", "fsdp"), axis=0, tiled=True
        )
        qkv_w, out_w, gate_w, up_w, down_w, attn_gain, mlp_gain = gathered
        attn_gain = attn_gain.astype(jnp.float32)
        mlp_gain = mlp_gain.astype(jnp.float32)
        mlp_grad_out = upstream.astype(jnp.bfloat16)
        grad_down = jnp.einsum(
            "tf,td->fd", activated, mlp_grad_out, preferred_element_type=jnp.float32
        )
        act_grad = jnp.einsum("td,fd->tf", mlp_grad_out, down_w, preferred_element_type=jnp.float32)
        sigmoid = jax.nn.sigmoid(gate_pre)
        gate_grad = (act_grad * up_pre * sigmoid * (1.0 + gate_pre * (1.0 - sigmoid))).astype(
            jnp.bfloat16
        )
        up_grad = (act_grad * (gate_pre * sigmoid)).astype(jnp.bfloat16)
        grad_gate = jnp.einsum("td,tf->df", mlp_in, gate_grad, preferred_element_type=jnp.float32)
        grad_up = jnp.einsum("td,tf->df", mlp_in, up_grad, preferred_element_type=jnp.float32)
        mlp_in_grad = jnp.einsum(
            "tf,df->td", gate_grad, gate_w, preferred_element_type=jnp.float32
        ) + jnp.einsum("tf,df->td", up_grad, up_w, preferred_element_type=jnp.float32)
        norm_part, grad_mlp_gain = norm_back(mlp_in_grad, normed_mlp, inverse_mlp, mlp_gain)
        upstream = upstream + norm_part
        attn_grad_out = upstream.astype(jnp.bfloat16)
        grad_outw = jnp.einsum(
            "te,td->ed", attn_bf, attn_grad_out, preferred_element_type=jnp.float32
        )
        grads_rows = jnp.einsum(
            "td,ed->te", attn_grad_out, out_w, preferred_element_type=jnp.float32
        ).astype(jnp.bfloat16)
        grads_heads = heads(grads_rows)
        row_delta = jnp.sum(grads_heads.astype(jnp.float32) * attn_out, axis=-1)
        key_flat = key_heads.reshape(slot_count, local_rows, width)
        value_flat = value_rows.reshape(slot_count, local_rows, width)
        all_keys, all_values = (
            lax.all_gather(key_flat, "seq", axis=1, tiled=True),
            lax.all_gather(value_flat, "seq", axis=1, tiled=True),
        )
        total_rows = all_keys.shape[1]
        block_rows = block_size()

        def back_step(number, carry):
            start = number * block_rows
            key_block = block_of(all_keys, start, block_rows, head_count)
            value_block = block_of(all_values, start, block_rows, head_count)
            key_index = start + jnp.arange(block_rows, dtype=jnp.int32)
            key_segment, unused = labels(key_index, doc_bounds)

            def back_work(inner):
                inner_grad, inner_terms = inner
                score_grad, prob_bf = block_grads(
                    queries,
                    grads_heads,
                    logsum,
                    row_delta,
                    token_index,
                    token_segment,
                    key_block,
                    value_block,
                    key_index,
                    key_segment,
                )
                inner_grad = inner_grad + jnp.einsum(
                    "sqhk,skhd->sqhd", score_grad, key_block, preferred_element_type=jnp.float32
                )
                key_part = jnp.einsum(
                    "sqhk,sqhd->skhd", score_grad, queries, preferred_element_type=jnp.float32
                )
                value_part = jnp.einsum(
                    "sqhk,sqhd->skhd", prob_bf, grads_heads, preferred_element_type=jnp.float32
                )
                joined = jnp.concatenate(
                    [
                        key_part.reshape(slot_count, block_rows, width),
                        value_part.reshape(slot_count, block_rows, width),
                    ],
                    axis=2,
                )
                return (inner_grad, lax.dynamic_update_slice_in_dim(inner_terms, joined, start, 1))

            return lax.cond(key_index[0] <= token_index[-1], back_work, lambda inner: inner, carry)

        query_grad, terms = lax.fori_loop(
            0,
            total_rows // block_rows,
            back_step,
            (
                jnp.zeros((slot_count, local_rows, head_count, HD), jnp.float32),
                jnp.zeros((slot_count, total_rows, 2 * width), jnp.float32),
            ),
        )
        kv_grad = lax.psum_scatter(
            terms.astype(jnp.bfloat16), "seq", scatter_dimension=1, tiled=True
        ).astype(jnp.float32)
        key_grad = kv_grad[..., :width].reshape(slot_count, local_rows, head_count, HD)
        value_grad = kv_grad[..., width:].reshape(rows_all, width)
        if layer_number > 0:
            value_carry = 0.5 * value_grad
            value_total = 0.5 * value_grad
        else:
            value_total = value_grad + value_carry
            first_grad = value_total
        query_back = rotate(query_grad, cosine_table, -sine_table).reshape(rows_all, width)
        key_back = rotate(key_grad, cosine_table, -sine_table).reshape(rows_all, width)
        qkv_grad = jnp.concatenate([query_back, key_back, value_total], axis=1).astype(jnp.bfloat16)
        grad_qkv = jnp.einsum("td,te->de", attn_in, qkv_grad, preferred_element_type=jnp.float32)
        attn_in_grad = jnp.einsum("te,de->td", qkv_grad, qkv_w, preferred_element_type=jnp.float32)
        norm_part, grad_attn_gain = norm_back(attn_in_grad, normed_attn, inverse_attn, attn_gain)
        upstream = upstream + norm_part
        local_grads = (
            grad_qkv,
            grad_outw,
            grad_gate,
            grad_up,
            grad_down,
            grad_attn_gain,
            grad_mlp_gain,
        )
        grads_per_layer[layer_number] = (
            lax.psum_scatter(local_grads[0], ("seq", "fsdp"), scatter_dimension=0, tiled=True),
            lax.psum_scatter(local_grads[1], ("seq", "fsdp"), scatter_dimension=0, tiled=True),
            lax.psum_scatter(local_grads[2], ("seq", "fsdp"), scatter_dimension=0, tiled=True),
            lax.psum_scatter(local_grads[3], ("seq", "fsdp"), scatter_dimension=0, tiled=True),
            lax.psum_scatter(local_grads[4], ("seq", "fsdp"), scatter_dimension=0, tiled=True),
            lax.psum_scatter(local_grads[5], ("seq", "fsdp"), scatter_dimension=0, tiled=True),
            lax.psum_scatter(local_grads[6], ("seq", "fsdp"), scatter_dimension=0, tiled=True),
        )
    stacked = tuple(
        (
            jnp.stack([grads_per_layer[layer_number][member] for layer_number in range(LAYERS)])
            for member in range(7)
        )
    )
    return (
        hidden_out,
        upstream.reshape(slot_count, local_rows, width),
        stacked[0],
        stacked[1],
        stacked[2],
        stacked[3],
        stacked[4],
        stacked[5],
        stacked[6],
        first_grad.reshape(slot_count, local_rows, width),
    )


def solution(mesh):
    in_specs = (
        P("fsdp", "seq", None),
        P("fsdp", None),
        P(None, ("seq", "fsdp"), None),
        P(None, ("seq", "fsdp"), None),
        P(None, ("seq", "fsdp"), None),
        P(None, ("seq", "fsdp"), None),
        P(None, ("seq", "fsdp"), None),
        P(None, ("seq", "fsdp")),
        P(None, ("seq", "fsdp")),
        P("fsdp", "seq", None),
    )
    out_specs = (
        P("fsdp", "seq", None),
        P("fsdp", "seq", None),
        P(None, ("seq", "fsdp"), None),
        P(None, ("seq", "fsdp"), None),
        P(None, ("seq", "fsdp"), None),
        P(None, ("seq", "fsdp"), None),
        P(None, ("seq", "fsdp"), None),
        P(None, ("seq", "fsdp")),
        P(None, ("seq", "fsdp")),
        P("fsdp", "seq", None),
    )
    return jax.shard_map(shards, mesh=mesh, in_specs=in_specs, out_specs=out_specs, check_vma=False)
```

profile of v0, /device:TPU:11, one launch (start us, length us, event | category | flops | bytes accessed | tf_op | source)
XLA Modules:
  0.0 3024.5 jit_solution(8959772564908393232)
XLA Ops:
  11.4 39.9 %all-reduce.9 = (bf16[1024]{0:T(1024)(128)(2,1)S(1)}, bf16[1024]{0:T(1024)(128)(2,1)S(1)}, bf16[1024]{0:T(1024)(128)(2,1)S(1)}, bf16[1024]{0:T(1024)(128)(2,1)S(1)}) all-reduce(bf16[1024]{0:T(1024)(128)(2,1)S(1)} %dynamic-update-slice, bf16[1024]{0:T(1024)(128)(2,1)S(1)} %dynamic-update-slice.1, ...), channel_id=2, replica_groups=mesh['seq'=8,'fsdp'=4] {'seq','fsdp'}, use_global_device_ids=true, to_apply=%add | all-reduce | flops 4096 | bytes 16384
  56.9 25.8 all-gather.37.cloned.1.call-done
  82.6 4.8 fusion.74
  117.7 57.9 %all-gather.29.cloned.1.call-done = bf16[2,1024,1024]{1,2,0:T(8,128)(2,1)} async-done(((bf16[2,128,1024]{1,2,0:T(8,128)(2,1)}), bf16[2,1024,1024]{1,2,0:T(8,128)(2,1)}) %all-gather.29.cloned.1.call-update) | async-done | bytes 4194320 | tf_op jit(solution)/shard_map/all_gather | solution.py:176
  175.5 75.9 %all-gather.31.cloned.1.call-done = bf16[2,1024,1024]{1,2,0:T(8,128)(2,1)} async-done(((bf16[2,128,1024]{1,2,0:T(8,128)(2,1)}), bf16[2,1024,1024]{1,2,0:T(8,128)(2,1)}) %all-gather.31.cloned.1.call-update) | async-done | bytes 4194320 | tf_op jit(solution)/shard_map/all_gather | solution.py:179
  251.5 14.9 while.72
  254.0 9.8 conditional.16
  269.1 41.3 %all-gather.39.cloned.1.call-done = bf16[1,1024,1024]{2,1,0:T(8,128)(2,1)} async-done(((bf16[1,32,1024]{2,1,0:T(8,128)(2,1)}), bf16[1,1024,1024]{2,1,0:T(8,128)(2,1)}) %all-gather.39.cloned.1.call-update) | async-done | bytes 2097168 | tf_op jit(solution)/shard_map/all_gather | solution.py:153
  313.1 68.0 %all-gather.41.cloned.1.call-done = bf16[1,1024,2816]{2,1,0:T(8,128)(2,1)} async-done(((bf16[1,32,2816]{2,1,0:T(8,128)(2,1)}), bf16[1,1024,2816]{2,1,0:T(8,128)(2,1)}) %all-gather.41.cloned.1.call-update) | async-done | bytes 5767184 | tf_op jit(solution)/shard_map/all_gather | solution.py:153
  381.1 5.8 fusion.98
  386.9 63.7 %all-gather.43.cloned.1.call-done = bf16[1,1024,2816]{2,1,0:T(8,128)(2,1)} async-done(((bf16[1,32,2816]{2,1,0:T(8,128)(2,1)}), bf16[1,1024,2816]{2,1,0:T(8,128)(2,1)}) %all-gather.43.cloned.1.call-update) | async-done | bytes 5767184 | tf_op jit(solution)/shard_map/all_gather | solution.py:153
  450.6 7.3 multiply_convert_fusion.5
  457.9 62.4 %all-gather.45.cloned.1.call-done = bf16[1,2816,1024]{2,1,0:T(8,128)(2,1)} async-done(((bf16[1,88,1024]{2,1,0:T(8,128)(2,1)}), bf16[1,2816,1024]{2,1,0:T(8,128)(2,1)}) %all-gather.45.cloned.1.call-update) | async-done | bytes 5767184 | tf_op jit(solution)/shard_map/all_gather | solution.py:153
  520.3 4.8 multiply_reduce_fusion.11
  525.2 66.2 %all-gather.47.cloned.1.call-done = bf16[1,1024,3072]{2,1,0:T(8,128)(2,1)} async-done(((bf16[1,32,3072]{2,1,0:T(8,128)(2,1)}), bf16[1,1024,3072]{2,1,0:T(8,128)(2,1)}) %all-gather.47.cloned.1.call-update) | async-done | bytes 6291472 | tf_op jit(solution)/shard_map/all_gather | solution.py:153
  591.4 4.6 fusion.70
  615.5 44.8 %all-gather.55.cloned.1.call-done = bf16[1,2816,1024]{2,1,0:T(8,128)(2,1)} async-done(((bf16[1,88,1024]{2,1,0:T(8,128)(2,1)}), bf16[1,2816,1024]{2,1,0:T(8,128)(2,1)}) %all-gather.55.cloned.1.call-update) | async-done | bytes 5767184 | tf_op jit(solution)/shard_map/all_gather | solution.py:153
  660.4 5.9 fusion.76
  667.1 66.8 %all-gather.33.cloned.1.call-done = bf16[2,1024,1024]{1,2,0:T(8,128)(2,1)} async-done(((bf16[2,128,1024]{1,2,0:T(8,128)(2,1)}), bf16[2,1024,1024]{1,2,0:T(8,128)(2,1)}) %all-gather.33.cloned.1.call-update) | async-done | bytes 4194320 | tf_op jit(solution)/shard_map/all_gather | solution.py:176
  733.9 75.9 %all-gather.35.cloned.1.call-done = bf16[2,1024,1024]{1,2,0:T(8,128)(2,1)} async-done(((bf16[2,128,1024]{1,2,0:T(8,128)(2,1)}), bf16[2,1024,1024]{1,2,0:T(8,128)(2,1)}) %all-gather.35.cloned.1.call-update) | async-done | bytes 4194320 | tf_op jit(solution)/shard_map/all_gather | solution.py:179
  809.8 14.7 while.73
  812.3 9.8 conditional.17
  826.7 42.1 %all-gather.49.cloned.1.call-done = bf16[1,1024,1024]{2,1,0:T(8,128)(2,1)} async-done(((bf16[1,32,1024]{2,1,0:T(8,128)(2,1)}), bf16[1,1024,1024]{2,1,0:T(8,128)(2,1)}) %all-gather.49.cloned.1.call-update) | async-done | bytes 2097168 | tf_op jit(solution)/shard_map/all_gather | solution.py:153
  871.4 67.6 %all-gather.53.cloned.1.call-done = bf16[1,1024,2816]{2,1,0:T(8,128)(2,1)} async-done(((bf16[1,32,2816]{2,1,0:T(8,128)(2,1)}), bf16[1,1024,2816]{2,1,0:T(8,128)(2,1)}) %all-gather.53.cloned.1.call-update) | async-done | bytes 5767184 | tf_op jit(solution)/shard_map/all_gather | solution.py:153
  939.0 5.8 fusion.82
  944.9 63.1 %all-gather.51.cloned.1.call-done = bf16[1,1024,2816]{2,1,0:T(8,128)(2,1)} async-done(((bf16[1,32,2816]{2,1,0:T(8,128)(2,1)}), bf16[1,1024,2816]{2,1,0:T(8,128)(2,1)}) %all-gather.51.cloned.1.call-update) | async-done | bytes 5767184 | tf_op jit(solution)/shard_map/all_gather | solution.py:153
  1008.0 7.5 multiply_convert_fusion.3
  1026.6 4.4 broadcast.562.clone
  1031.0 20.0 while.74
  1033.5 15.1 conditional.18
  1037.9 3.5 fusion.40
  1051.0 21.7 copy.192
  1072.7 12.1 copy.204
  1087.4 158.4 %reduce-scatter.37.cloned.1.call-done = bf16[128,4096]{1,0:T(8,128)(2,1)} async-done(((bf16[1024,4096]{1,0:T(8,128)(2,1)}), bf16[128,4096]{1,0:T(8,128)(2,1)}) %reduce-scatter.37.cloned.1.call-update) | async-done | bytes 1048592
  1255.9 6.2 multiply_reduce_fusion.2
  1262.4 5.5 multiply_convert_fusion.1
  1276.5 4.4 broadcast.562
  1280.9 19.9 while.75
  1283.3 15.1 conditional.19
  1300.8 21.7 copy.194
  1322.5 12.1 copy.207
  1338.4 4.0 fusion.142
  1342.5 6.0 fusion.181
  1349.7 7.2 fusion.151
  1358.6 6.0 fusion.178
  1366.1 6.0 fusion.177
  1373.5 6.0 fusion.180
  1380.8 5.9 fusion.179
  1388.0 8.1 fusion.161
  1398.1 99.7 %reduce-scatter.39.cloned.1.call-done = bf16[128,4096]{1,0:T(8,128)(2,1)} async-done(((bf16[1024,4096]{1,0:T(8,128)(2,1)}), bf16[128,4096]{1,0:T(8,128)(2,1)}) %reduce-scatter.39.cloned.1.call-update) | async-done | bytes 1048592
  1512.1 6.5 fusion.137
  1519.8 4.8 fusion.125
  1525.8 86.1 %reduce-scatter.23.cloned.1.call-done = f32[32,1024]{1,0:T(8,128)} async-done(((f32[1024,1024]{1,0:T(8,128)}), f32[32,1024]{1,0:T(8,128)}) %reduce-scatter.23.cloned.1.call-update) | async-done | bytes 131088 | tf_op jit(solution)/shard_map/reduce_scatter | solution.py:385
  1611.9 139.2 %reduce-scatter.21.cloned.1.call-done = f32[32,1024]{1,0:T(8,128)} async-done(((f32[1024,1024]{1,0:T(8,128)}), f32[32,1024]{1,0:T(8,128)}) %reduce-scatter.21.cloned.1.call-update) | async-done | bytes 131088 | tf_op jit(solution)/shard_map/reduce_scatter | solution.py:385
  1754.1 5.2 multiply_reduce_fusion.3
  1759.4 70.0 %all-reduce.8 = (f32[1024]{0:T(1024)S(1)}, f32[1024]{0:T(1024)S(1)}, f32[1024]{0:T(1024)S(1)}, f32[1024]{0:T(1024)S(1)}) all-reduce(f32[1024]{0:T(1024)S(1)} %copy-done.78, f32[1024]{0:T(1024)S(1)} %get-tuple-element.2348, f32[1024]{0:T(1024)S(1)} %copy-done.77, ...), channel_id=29, replica_groups=mesh['seq'=8,'fsdp'=4] {'seq','fsdp'}, use_global_device_ids=true, to_apply=%region_45.46.clone | all-reduce | flops 4096 | bytes 32768
  1832.1 76.9 %reduce-scatter.35.cloned.1.call-done = f32[88,1024]{1,0:T(8,128)} async-done(((f32[2816,1024]{1,0:T(8,128)}), f32[88,1024]{1,0:T(8,128)}) %reduce-scatter.35.cloned.1.call-update) | async-done | bytes 360464 | tf_op jit(solution)/shard_map/reduce_scatter | solution.py:388
  1908.9 159.7 %reduce-scatter.33.cloned.1.call-done = f32[88,1024]{1,0:T(8,128)} async-done(((f32[2816,1024]{1,0:T(8,128)}), f32[88,1024]{1,0:T(8,128)}) %reduce-scatter.33.cloned.1.call-update) | async-done | bytes 360464 | tf_op jit(solution)/shard_map/reduce_scatter | solution.py:388
  2070.7 151.2 %reduce-scatter.27.cloned.1.call-done = f32[32,2816]{1,0:T(8,128)} async-done(((f32[1024,2816]{1,0:T(8,128)}), f32[32,2816]{1,0:T(8,128)}) %reduce-scatter.27.cloned.1.call-update) | async-done | bytes 360464 | tf_op jit(solution)/shard_map/reduce_scatter | solution.py:386
  2221.9 153.0 %reduce-scatter.25.cloned.1.call-done = f32[32,2816]{1,0:T(8,128)} async-done(((f32[1024,2816]{1,0:T(8,128)}), f32[32,2816]{1,0:T(8,128)}) %reduce-scatter.25.cloned.1.call-update) | async-done | bytes 360464 | tf_op jit(solution)/shard_map/reduce_scatter | solution.py:386
  2376.9 150.9 %reduce-scatter.31.cloned.1.call-done = f32[32,2816]{1,0:T(8,128)} async-done(((f32[1024,2816]{1,0:T(8,128)}), f32[32,2816]{1,0:T(8,128)}) %reduce-scatter.31.cloned.1.call-update) | async-done | bytes 360464 | tf_op jit(solution)/shard_map/reduce_scatter | solution.py:387
  2527.8 153.0 %reduce-scatter.29.cloned.1.call-done = f32[32,2816]{1,0:T(8,128)} async-done(((f32[1024,2816]{1,0:T(8,128)}), f32[32,2816]{1,0:T(8,128)}) %reduce-scatter.29.cloned.1.call-update) | async-done | bytes 360464 | tf_op jit(solution)/shard_map/reduce_scatter | solution.py:387
  2682.8 171.4 %reduce-scatter.19.cloned.1.call-done = f32[32,3072]{1,0:T(8,128)} async-done(((f32[1024,3072]{1,0:T(8,128)}), f32[32,3072]{1,0:T(8,128)}) %reduce-scatter.19.cloned.1.call-update) | async-done | bytes 393232 | tf_op jit(solution)/shard_map/reduce_scatter | solution.py:384
  2854.2 161.5 %reduce-scatter.17.cloned.1.call-done = f32[32,3072]{1,0:T(8,128)} async-done(((f32[1024,3072]{1,0:T(8,128)}), f32[32,3072]{1,0:T(8,128)}) %reduce-scatter.17.cloned.1.call-update) | async-done | bytes 393232 | tf_op jit(solution)/shard_map/reduce_scatter | solution.py:384
  (452 shorter events, 201.8 us)
Async XLA Ops:
  7.2 75.4 %all-gather.37.cloned.1.call-start = ((), (), s32[]{:S(2)}) async-start(), calls=%async_computation.26 | async-start | bytes 6488064 | tf_op jit(solution)/shard_map/all_gather | solution.py:153
  9.0 166.5 %all-gather.29.cloned.1.call-start = ((), (), s32[]{:S(2)}) async-start(), calls=%async_computation.12 | async-start | bytes 4718592 | tf_op jit(solution)/shard_map/all_gather | solution.py:176
  51.4 36.0 %copy-start.65 = (f32[1024]{0:T(1024)}, f32[1024]{0:T(1024)S(1)}, u32[]{:S(2)}) copy-start(f32[1024]{0:T(1024)S(1)} %convert_element_type.271) | copy-start | bytes 12292
  54.8 552.1 %copy-start.54 = (f32[2,128,32]{1,0,2:T(2,128)}, f32[2,128,32]{1,0,2:T(2,128)S(1)}, u32[]{:S(2)}) copy-start(f32[2,128,32]{1,0,2:T(2,128)S(1)} %get-tuple-element.2536) | copy-start | bytes 98308
  87.4 17.2 copy-start.29
  102.9 13.8 copy-start.70
  104.5 146.9 %all-gather.31.cloned.1.call-start = ((), (), s32[]{:S(2)}) async-start(), calls=%async_computation.13 | async-start | bytes 4718592 | tf_op jit(solution)/shard_map/all_gather | solution.py:179
  105.4 11.4 copy-start.51
  107.5 202.9 %all-gather.39.cloned.1.call-start = ((), (), s32[]{:S(2)}) async-start(), calls=%async_computation.27 | async-start | bytes 2162688 | tf_op jit(solution)/shard_map/all_gather | solution.py:153
  109.1 272.0 %all-gather.41.cloned.1.call-start = ((), (), s32[]{:S(2)}) async-start(), calls=%async_computation.28 | async-start | bytes 5947392 | tf_op jit(solution)/shard_map/all_gather | solution.py:153
  111.0 339.7 %all-gather.43.cloned.1.call-start = ((), (), s32[]{:S(2)}) async-start(), calls=%async_computation.29 | async-start | bytes 5947392 | tf_op jit(solution)/shard_map/all_gather | solution.py:153
  112.9 407.5 %all-gather.45.cloned.1.call-start = ((), (), s32[]{:S(2)}) async-start(), calls=%async_computation.30 | async-start | bytes 5947392 | tf_op jit(solution)/shard_map/all_gather | solution.py:153
  114.7 476.6 %all-gather.47.cloned.1.call-start = ((), (), s32[]{:S(2)}) async-start(), calls=%async_computation.31 | async-start | bytes 6488064 | tf_op jit(solution)/shard_map/all_gather | solution.py:153
  115.5 544.9 %all-gather.55.cloned.1.call-start = ((), (), s32[]{:S(2)}) async-start(), calls=%async_computation.35 | async-start | bytes 5947392 | tf_op jit(solution)/shard_map/all_gather | solution.py:153
  116.2 617.7 %all-gather.33.cloned.1.call-start = ((), (), s32[]{:S(2)}) async-start(), calls=%async_computation.14 | async-start | bytes 4718592 | tf_op jit(solution)/shard_map/all_gather | solution.py:176
  116.8 196.1 %copy-start.63 = (f32[1024]{0:T(1024)}, f32[1024]{0:T(1024)S(1)}, u32[]{:S(2)}) copy-start(f32[1024]{0:T(1024)S(1)} %convert_element_type.272) | copy-start | bytes 12292
  116.8 474.5 %copy-start.60 = (f32[1024]{0:T(1024)}, f32[1024]{0:T(1024)S(1)}, u32[]{:S(2)}) copy-start(f32[1024]{0:T(1024)S(1)} %convert_element_type.273) | copy-start | bytes 12292
  251.5 58.9 %copy-start.19 = (bf16[2,128,1024]{2,1,0:T(8,128)(2,1)S(1)}, bf16[2,128,1024]{2,1,0:T(8,128)(2,1)}, u32[]{:S(2)}) copy-start(bf16[2,128,1024]{2,1,0:T(8,128)(2,1)} %param.26) | copy-start | bytes 1572868
  266.4 46.6 %copy-start = (bf16[2,128,16,64]{1,3,2,0:T(8,128)(2,1)}, bf16[2,128,16,64]{1,3,2,0:T(8,128)(2,1)S(1)}, u32[]{:S(2)}) copy-start(bf16[2,128,16,64]{1,3,2,0:T(8,128)(2,1)S(1)} %get-tuple-element.3085) | copy-start | bytes 1572868
  269.1 117.8 %copy-start.25 = (bf16[2,128,16,64]{1,0,3,2:T(2,128)(2,1)}, bf16[2,128,16,64]{1,0,3,2:T(2,128)(2,1)S(1)}, u32[]{:S(2)}) copy-start(bf16[2,128,16,64]{1,0,3,2:T(2,128)(2,1)S(1)} %get-tuple-element.2464) | copy-start | bytes 1572868
  312.9 207.5 %copy-start.11 = (f32[256,1024]{1,0:T(8,128)}, f32[256,1024]{1,0:T(8,128)S(1)}, u32[]{:S(2)}) copy-start(f32[256,1024]{1,0:T(8,128)S(1)} %get-tuple-element.2542) | copy-start | bytes 3145732
  312.9 74.1 %copy-start.73 = (f32[256]{0:T(256)}, f32[256]{0:T(256)S(1)}, u32[]{:S(2)}) copy-start(f32[256]{0:T(256)S(1)} %add_rsqrt_fusion.2) | copy-start | bytes 3076
  313.1 137.6 %copy-start.21 = (bf16[256,1024]{1,0:T(8,128)(2,1)}, bf16[256,1024]{1,0:T(8,128)(2,1)S(1)}, u32[]{:S(2)}) copy-start(bf16[256,1024]{1,0:T(8,128)(2,1)S(1)} %multiply_convert_fusion.8) | copy-start | bytes 1572868
  525.2 343.6 %copy-start.4 = (f32[256,1024]{1,0:T(8,128)}, f32[256,1024]{1,0:T(8,128)S(1)}, u32[]{:S(2)}) copy-start(f32[256,1024]{1,0:T(8,128)S(1)} %get-tuple-element.2546) | copy-start | bytes 3145732
  525.2 70.8 %copy-start.67 = (f32[256]{0:T(256)}, f32[256]{0:T(256)S(1)}, u32[]{:S(2)}) copy-start(f32[256]{0:T(256)S(1)} %add_rsqrt_fusion.1) | copy-start | bytes 3076
  609.2 5.1 copy-start.57
  610.8 198.9 %all-gather.35.cloned.1.call-start = ((), (), s32[]{:S(2)}) async-start(), calls=%async_computation.15 | async-start | bytes 4718592 | tf_op jit(solution)/shard_map/all_gather | solution.py:179
  611.9 256.9 %all-gather.49.cloned.1.call-start = ((), (), s32[]{:S(2)}) async-start(), calls=%async_computation.32 | async-start | bytes 2162688 | tf_op jit(solution)/shard_map/all_gather | solution.py:153
  612.4 326.6 %all-gather.53.cloned.1.call-start = ((), (), s32[]{:S(2)}) async-start(), calls=%async_computation.34 | async-start | bytes 5947392 | tf_op jit(solution)/shard_map/all_gather | solution.py:153
  613.2 394.8 %all-gather.51.cloned.1.call-start = ((), (), s32[]{:S(2)}) async-start(), calls=%async_computation.33 | async-start | bytes 5947392 | tf_op jit(solution)/shard_map/all_gather | solution.py:153
  613.8 632.0 %reduce-scatter.37.cloned.1.call-start = ((), (), s32[]{:S(2)}) async-start(), calls=%async_computation.36 | async-start | bytes 9437184
  614.3 52.0 %copy-start.71 = (f32[2,128]{1,0:T(2,128)}, f32[2,128]{1,0:T(2,128)S(1)}, u32[]{:S(2)}) copy-start(f32[2,128]{1,0:T(2,128)S(1)} %compare_convert_fusion) | copy-start | bytes 3076
  615.5 50.8 %copy-start.38 = (bf16[256,1024]{1,0:T(8,128)(2,1)}, bf16[256,1024]{1,0:T(8,128)(2,1)S(1)}, u32[]{:S(2)}) copy-start(bf16[256,1024]{1,0:T(8,128)(2,1)S(1)} %bitcast_convert_fusion) | copy-start | bytes 1572868
  826.7 118.2 %copy-start.27 = (bf16[2,128,16,64]{1,0,3,2:T(2,128)(2,1)}, bf16[2,128,16,64]{1,0,3,2:T(2,128)(2,1)S(1)}, u32[]{:S(2)}) copy-start(bf16[2,128,16,64]{1,0,3,2:T(2,128)(2,1)S(1)} %get-tuple-element.2462) | copy-start | bytes 1572868
  871.2 146.0 %copy-start.9 = (f32[256,1024]{1,0:T(8,128)}, f32[256,1024]{1,0:T(8,128)S(1)}, u32[]{:S(2)}) copy-start(f32[256,1024]{1,0:T(8,128)S(1)} %get-tuple-element.2548) | copy-start | bytes 3145732
  871.4 136.6 %copy-start.23 = (bf16[256,1024]{1,0:T(8,128)(2,1)}, bf16[256,1024]{1,0:T(8,128)(2,1)S(1)}, u32[]{:S(2)}) copy-start(bf16[256,1024]{1,0:T(8,128)(2,1)S(1)} %multiply_convert_fusion.6) | copy-start | bytes 1572868
  1008.0 7.5 copy-start.80
  1084.9 412.9 %reduce-scatter.39.cloned.1.call-start = ((), (), s32[]{:S(2)}) async-start(), calls=%async_computation.37 | async-start | bytes 9437184
  1251.4 11.0 slice-start.4
  1255.7 6.7 slice-start.5
  1255.8 6.2 copy-start.34
  1255.8 12.1 slice-start.2
  1255.8 13.8 slice-start
  1262.4 10.0 copy-start.7
  1262.4 5.5 slice-start.3
  1262.4 7.3 slice-start.1
  1334.6 277.3 %reduce-scatter.23.cloned.1.call-start = ((), (), s32[]{:S(2)}) async-start(), calls=%async_computation.19 | async-start | bytes 4325376 | tf_op jit(solution)/shard_map/reduce_scatter | solution.py:385
  1338.3 412.7 %reduce-scatter.21.cloned.1.call-start = ((), (), s32[]{:S(2)}) async-start(), calls=%async_computation.18 | async-start | bytes 4325376 | tf_op jit(solution)/shard_map/reduce_scatter | solution.py:385
  1342.4 566.5 %reduce-scatter.35.cloned.1.call-start = ((), (), s32[]{:S(2)}) async-start(), calls=%async_computation.25 | async-start | bytes 11894784 | tf_op jit(solution)/shard_map/reduce_scatter | solution.py:388
  1348.5 720.2 %reduce-scatter.33.cloned.1.call-start = ((), (), s32[]{:S(2)}) async-start(), calls=%async_computation.24 | async-start | bytes 11894784 | tf_op jit(solution)/shard_map/reduce_scatter | solution.py:388
  1356.9 865.0 %reduce-scatter.27.cloned.1.call-start = ((), (), s32[]{:S(2)}) async-start(), calls=%async_computation.21 | async-start | bytes 11894784 | tf_op jit(solution)/shard_map/reduce_scatter | solution.py:386
  1364.6 1010.3 %reduce-scatter.25.cloned.1.call-start = ((), (), s32[]{:S(2)}) async-start(), calls=%async_computation.20 | async-start | bytes 11894784 | tf_op jit(solution)/shard_map/reduce_scatter | solution.py:386
  1372.1 1155.7 %reduce-scatter.31.cloned.1.call-start = ((), (), s32[]{:S(2)}) async-start(), calls=%async_computation.23 | async-start | bytes 11894784 | tf_op jit(solution)/shard_map/reduce_scatter | solution.py:387
  1379.5 1301.3 %reduce-scatter.29.cloned.1.call-start = ((), (), s32[]{:S(2)}) async-start(), calls=%async_computation.22 | async-start | bytes 11894784 | tf_op jit(solution)/shard_map/reduce_scatter | solution.py:387
  1386.8 1467.5 %reduce-scatter.19.cloned.1.call-start = ((), (), s32[]{:S(2)}) async-start(), calls=%async_computation.17 | async-start | bytes 12976128 | tf_op jit(solution)/shard_map/reduce_scatter | solution.py:384
  1396.1 1619.6 %reduce-scatter.17.cloned.1.call-start = ((), (), s32[]{:S(2)}) async-start(), calls=%async_computation.16 | async-start | bytes 12976128 | tf_op jit(solution)/shard_map/reduce_scatter | solution.py:384
  1519.8 232.9 %copy-start.30 = (f32[2,128,1024]{1,2,0:T(8,128)S(1)}, f32[2,128,1024]{1,2,0:T(8,128)}, u32[]{:S(2)}) copy-start(f32[2,128,1024]{1,2,0:T(8,128)} %get-tuple-element.2461) | copy-start | bytes 3145732
  1524.7 229.4 %copy-start.20 = (bf16[2,128,1024]{2,1,0:T(8,128)(2,1)S(1)}, bf16[2,128,1024]{2,1,0:T(8,128)(2,1)}, u32[]{:S(2)}) copy-start(bf16[2,128,1024]{2,1,0:T(8,128)(2,1)} %param.26) | copy-start | bytes 1572868
  1524.7 229.4 %copy-start.66 = (f32[1024]{0:T(1024)S(1)}, f32[1024]{0:T(1024)}, u32[]{:S(2)}) copy-start(f32[1024]{0:T(1024)} %copy-done.65) | copy-start | bytes 12292
  1524.7 229.4 %copy-start.76 = (f32[256]{0:T(256)S(1)}, f32[256]{0:T(256)}, u32[]{:S(2)}) copy-start(f32[256]{0:T(256)} %copy-done.75) | copy-start | bytes 3076
  1754.1 5.3 copy-start.77
  1754.1 5.3 copy-start.78
  1754.1 5.3 copy-start.79
  1754.1 76.7 %copy-start.3 = (f32[256,1024]{1,0:T(8,128)S(1)}, f32[256,1024]{1,0:T(8,128)}, u32[]{:S(2)}) copy-start(f32[256,1024]{1,0:T(8,128)} %copy-done.2) | copy-start | bytes 3145732
  (50 other events, 105.7 us)
Sparse Core Ops, SparseCore 0:
  11.4 71.1 all-gather.36
  104.6 70.8 all-gather.28
  178.2 73.1 all-gather.30
  254.1 56.2 all-gather.38
  313.7 67.3 all-gather.40
  384.4 66.2 all-gather.42
  454.1 66.2 all-gather.44
  523.2 68.1 all-gather.46
  594.2 66.1 all-gather.54
  662.8 70.9 all-gather.32
  736.5 73.1 all-gather.34
  812.4 56.2 all-gather.48
  871.6 67.3 all-gather.52
  941.7 66.2 all-gather.50
  1085.0 160.7 reduce-scatter.36
  1334.7 163.0 reduce-scatter.38
  1499.9 111.8 reduce-scatter.22
  1614.0 136.9 reduce-scatter.20
  1753.4 155.5 reduce-scatter.34
  1911.1 157.5 reduce-scatter.32
  2071.0 150.8 reduce-scatter.26
  2224.2 150.6 reduce-scatter.24
  2377.2 150.4 reduce-scatter.30
  2529.9 150.8 reduce-scatter.28
  2686.8 167.3 reduce-scatter.18
  2861.1 154.5 reduce-scatter.16
where the time goes:
time: 3040 us; the launch traced here: 3020 us
  waiting for transfers between devices  2490 us (82%)
  local copies, waits for them, and re-layouts  174 us (6%)
  matrix products  170 us (6%)
  blocking collectives  110 us (4%)
  other arithmetic  56.3 us (2%)
    all_gather x10, waiting for transfers between devices, shards(): lax.all_gather(as_sent(layer_shards(layer_number)), ('seq', 'fsdp'), axis...  545 us
    reduce_scatter x2, waiting for transfers between devices, shards(): lax.psum_scatter(local_grads[0], ('seq', 'fsdp'), scatter_dimension=0, ti...  333 us
    reduce_scatter x2, waiting for transfers between devices, shards(): lax.psum_scatter(local_grads[2], ('seq', 'fsdp'), scatter_dimension=0, ti...  304 us
    reduce_scatter x2, waiting for transfers between devices, shards(): lax.psum_scatter(local_grads[3], ('seq', 'fsdp'), scatter_dimension=0, ti...  304 us
    unnamed x28, waiting for transfers between devices  262 us
    reduce_scatter x2, waiting for transfers between devices, shards(): lax.psum_scatter(local_grads[4], ('seq', 'fsdp'), scatter_dimension=0, ti...  237 us
    reduce_scatter x2, waiting for transfers between devices, shards(): lax.psum_scatter(local_grads[1], ('seq', 'fsdp'), scatter_dimension=0, ti...  225 us
    all_gather x2, waiting for transfers between devices, shards(): lax.all_gather(value_rows.reshape(slot_count, local_rows, width), 'seq',...  152 us
  transfers between devices with their start and end apart: 26, of which 26 were waited for; matrix products, arithmetic and copies ran while one was open for 7% of the time, Pallas kernels for 0%

commit v1 on v0

v1 whole, which is shorter than its diff:
```python
import functools

import jax
import jax.numpy as jnp
from jax import lax
from jax.experimental import pallas as pl
from jax.experimental.pallas import tpu as pltpu
from jax.sharding import Mesh, PartitionSpec as P

HD = 64
LAYERS = 2
epsilon = 1e-05
masked_score = -1e30
bf16 = jnp.bfloat16
f32 = jnp.float32

ALL = ("sz", "sy", "fx", "fc")
SWAP = ((0, 1), (1, 0))
VMEM_LIMIT = 48 * 1024 * 1024


def dot(left, right):
    return jnp.dot(left, right, preferred_element_type=f32)


def dot_rows(left, right):
    return lax.dot_general(left, right, (((0,), (0,)), ((), ())), preferred_element_type=f32)


def dot_cols(left, right):
    return lax.dot_general(left, right, (((1,), (1,)), ((), ())), preferred_element_type=f32)


def swap_core(value):
    return lax.ppermute(value, "fc", SWAP)


def swap_x(value):
    return lax.ppermute(value, "fx", SWAP)


def swap_y(value):
    return lax.ppermute(value, "sy", SWAP)


def pick(array, index, axis=0):
    return lax.dynamic_index_in_dim(array, index, axis, keepdims=False)


def in_order(flag, first, second, axis):
    return jnp.where(
        flag == 0, jnp.stack([first, second], axis), jnp.stack([second, first], axis)
    )


def exchange(pieces):
    fx, fc = lax.axis_index("fx"), lax.axis_index("fc")
    pieces = pieces.reshape((2, 2) + pieces.shape[1:])
    got = swap_x(pick(pieces, 1 - fx))
    both = in_order(fx, pick(pieces, fx), got, 0)
    got = swap_core(pick(both, 1 - fc, 1))
    both = in_order(fc, pick(both, fc, 1), got, 1)
    return both.reshape((4,) + both.shape[2:])


def join_y(own):
    full = in_order(lax.axis_index("sy"), own, swap_y(own), 1)
    return full.reshape(-1, own.shape[-1])


def reduce_rows(grad, rows):
    sy = lax.axis_index("sy")
    grad = grad.reshape(-1, 2, rows, grad.shape[-1])
    got = swap_y(pick(grad, 1 - sy, 1))
    total = (pick(grad, sy, 1).astype(f32) + got.astype(f32)).astype(bf16)
    return lax.psum_scatter(total, "sz", scatter_dimension=0, tiled=False)


def spread(value):
    over = swap_x(value)
    return (
        jnp.concatenate([value, swap_core(value)]),
        jnp.concatenate([over, swap_core(over)]),
    )


def gather_sum(near, far):
    rows = near.shape[0] // 2
    out = far[:rows] + swap_core(far[rows:].astype(bf16)).astype(f32)
    out = swap_x(out.astype(bf16)).astype(f32)
    own = near[:rows] + swap_core(near[rows:].astype(bf16)).astype(f32)
    return own + out


def normalize(hidden):
    inverse = lax.rsqrt(jnp.mean(hidden * hidden, axis=-1, keepdims=True) + epsilon)
    return (hidden * inverse, inverse)


def norm_back(upstream, normed, inverse, gain_row):
    scaled = upstream * gain_row
    inner_mean = jnp.mean(scaled * normed, axis=-1, keepdims=True)
    return (inverse * (scaled - normed * inner_mean), jnp.sum(upstream * normed, axis=0))


def partner(rows):
    lane = lax.broadcasted_iota(jnp.int32, rows.shape, 1)
    return jnp.where(lane % 64 < 32, pltpu.roll(rows, 96, 1), pltpu.roll(rows, 32, 1))


def block_mask(block, rows, start, end):
    shape = (rows, (block + 1) * rows)
    query = block * rows + lax.broadcasted_iota(jnp.int32, (rows, 1), 0)
    lowest = jnp.where(query < start, 0, jnp.where(query < end, start, end))
    key = lax.broadcasted_iota(jnp.int32, shape, 1)
    return (key <= query) & (key >= lowest)


def softmax_rows(scores, allowed):
    scores = jnp.where(allowed, scores * 0.125, masked_score)
    weights = jnp.exp(scores - jnp.max(scores, axis=-1, keepdims=True))
    return weights * (1.0 / jnp.sum(weights, axis=-1, keepdims=True))


def attention_kernel(blend, scalars, cos_ref, sin_ref, *refs):
    if blend:
        part_ref, first_ref, q_ref, k_ref, v_ref, o_ref = refs
    else:
        part_ref, q_ref, k_ref, v_ref, o_ref = refs
    me, start, end = scalars[0], scalars[1], scalars[2]
    total, width = q_ref.shape
    rows = total // 4
    for i in range(4):
        here = slice(i * rows, (i + 1) * rows)
        there = pl.ds(pl.multiple_of((me ^ i) * rows, rows), rows)
        cosine, sine = cos_ref[here, :], sin_ref[here, :]
        for j in range(width // 128):
            for into, at in ((q_ref, 0), (k_ref, width)):
                piece = part_ref[here, at + j * 128 : at + (j + 1) * 128]
                turned = piece * cosine + partner(piece) * sine
                into[there, j * 128 : (j + 1) * 128] = turned.astype(bf16)
        value = part_ref[here, 2 * width : 3 * width]
        if blend:
            value = 0.5 * value + 0.5 * first_ref[here, 2 * width : 3 * width]
        v_ref[there, :] = value.astype(bf16)
    lane = lax.broadcasted_iota(jnp.int32, (rows, 128), 1)
    for b in range(4):
        allowed = block_mask(b, rows, start, end)
        there = pl.ds(pl.multiple_of((me ^ b) * rows, rows), rows)
        for j in range(width // 128):
            columns = slice(j * 128, (j + 1) * 128)
            query = q_ref[b * rows : (b + 1) * rows, columns]
            keys = k_ref[: (b + 1) * rows, columns]
            values = v_ref[: (b + 1) * rows, columns]
            outs = []
            for h in range(2):
                one = jnp.where(lane // 64 == h, query, jnp.zeros_like(query))
                chance = softmax_rows(dot_cols(one, keys), allowed)
                outs.append(dot(chance.astype(bf16), values))
            o_ref[there, columns] = jnp.where(lane < 64, outs[0], outs[1]).astype(bf16)


def attention_back_kernel(last, scalars, cos_ref, sin_ref, *refs):
    if last:
        q_ref, k_ref, v_ref, up_ref, carry_ref, d_ref, dv_ref, dk_sum, dv_sum = refs
    else:
        q_ref, k_ref, v_ref, up_ref, d_ref, dv_ref, dk_sum, dv_sum = refs
    me, start, end = scalars[0], scalars[1], scalars[2]
    total, width = q_ref.shape
    rows = total // 4
    lane = lax.broadcasted_iota(jnp.int32, (rows, 128), 1)
    dk_sum[...] = jnp.zeros_like(dk_sum)
    dv_sum[...] = jnp.zeros_like(dv_sum)
    for b in range(4):
        allowed = block_mask(b, rows, start, end)
        there = pl.ds(pl.multiple_of((me ^ b) * rows, rows), rows)
        upto = slice(0, (b + 1) * rows)
        cosine, sine = cos_ref[there, :], sin_ref[there, :]
        for j in range(width // 128):
            columns = slice(j * 128, (j + 1) * 128)
            query = q_ref[b * rows : (b + 1) * rows, columns]
            keys, values = k_ref[upto, columns], v_ref[upto, columns]
            up = up_ref[there, columns]
            dq, dk, dv = [], [], []
            for h in range(2):
                mine = lane // 64 == h
                one = jnp.where(mine, query, jnp.zeros_like(query))
                one_up = jnp.where(mine, up, jnp.zeros_like(up))
                chance = softmax_rows(dot_cols(one, keys), allowed)
                back = dot_cols(one_up, values)
                delta = jnp.sum(chance * back, axis=-1, keepdims=True)
                score = (chance * (back - delta) * 0.125).astype(bf16)
                dq.append(dot(score, keys))
                dk.append(dot_rows(score, one))
                dv.append(dot_rows(chance.astype(bf16), one_up))
            dk_sum[upto, columns] += dk[0] + dk[1]
            dv_sum[upto, columns] += dv[0] + dv[1]
            dq = jnp.where(lane < 64, dq[0], dq[1])
            d_ref[there, columns] = (dq * cosine - partner(dq) * sine).astype(bf16)
    for b in range(4):
        there = pl.ds(pl.multiple_of((me ^ b) * rows, rows), rows)
        here = slice(b * rows, (b + 1) * rows)
        cosine, sine = cos_ref[there, :], sin_ref[there, :]
        for j in range(width // 128):
            dk = dk_sum[here, j * 128 : (j + 1) * 128]
            dk = dk * cosine - partner(dk) * sine
            d_ref[there, width + j * 128 : width + (j + 1) * 128] = dk.astype(bf16)
        dv = dv_sum[here, :]
        dv = dv + carry_ref[there, :] if last else 0.5 * dv
        dv_ref[there, :] = dv
        d_ref[there, 2 * width : 3 * width] = dv.astype(bf16)


def kernel_call(body, out_shape, operands, scratch=(), flops=0):
    return pl.pallas_call(
        body,
        out_shape=out_shape,
        in_specs=[pl.BlockSpec(memory_space=pltpu.SMEM)]
        + [pl.BlockSpec(memory_space=pltpu.VMEM)] * (len(operands) - 1),
        out_specs=[pl.BlockSpec(memory_space=pltpu.VMEM)] * len(out_shape),
        scratch_shapes=list(scratch),
        compiler_params=pltpu.CompilerParams(vmem_limit_bytes=VMEM_LIMIT),
        cost_estimate=pl.CostEstimate(flops=flops, bytes_accessed=1 << 22, transcendentals=1 << 20),
    )(*operands)


def turn(rows, cosine, sine):
    total, width = rows.shape
    halves = rows.reshape(total, width // HD, 2, HD // 2)
    cosine = cosine[:, :HD].reshape(total, 1, 2, HD // 2)
    sine = sine[:, :HD].reshape(total, 1, 2, HD // 2)
    return (halves * cosine + halves[:, :, ::-1] * sine).reshape(total, width)


class Attention:
    def __init__(self, me, part, parts, total, bounds):
        self.parts, self.part, self.total = parts, part, total
        rows = total // 4
        blocks = (me ^ jnp.arange(4, dtype=jnp.int32)) * rows
        inner = (blocks[:, None] + jnp.arange(rows, dtype=jnp.int32)[None, :]).reshape(total)
        start, end = bounds[0], bounds[1]
        self.start, self.end = start, end
        self.inner = inner
        index = part * total + inner
        base = jnp.where(index < start, 0, jnp.where(index < end, start, end))
        self.index = index
        self.scalars = jnp.stack([me.astype(jnp.int32), start, end])
        frequency = 10000.0 ** (-jnp.arange(HD // 2, dtype=f32) * 2.0 / HD)
        angles = (index - base).astype(f32)[:, None] * frequency[None, :]
        cosine, sine = jnp.cos(angles), jnp.sin(angles)
        self.cosine = jnp.concatenate([cosine] * 4, axis=1)
        self.sine = jnp.concatenate([-sine, sine] * 2, axis=1)

    def valid(self, rows):
        return (self.index[:rows] < self.end).astype(f32)[:, None]

    def rotate_parts(self, value, shift):
        if shift % self.parts == 0:
            return value
        total = lax.axis_size(("sz", "sy"))
        pairs = []
        for t in range(total):
            head = t - t % self.parts
            pairs.append((head + (t + shift) % self.parts, t))
        return lax.ppermute(value, ("sz", "sy"), pairs)

    def forward(self, part, first):
        total, width = self.total, part.shape[1] // 3
        if self.parts == 1:
            operands = [self.scalars, self.cosine, self.sine, part]
            if first is not None:
                operands.append(first)
            shape = jax.ShapeDtypeStruct((total, width), bf16)
            return kernel_call(
                functools.partial(attention_kernel, first is not None),
                [shape] * 4,
                operands,
                flops=3 * total * total * width,
            )
        query = turn(part[:, :width], self.cosine, self.sine).astype(bf16)
        key = turn(part[:, width : 2 * width], self.cosine, self.sine).astype(bf16)
        value = part[:, 2 * width :]
        if first is not None:
            value = 0.5 * value + 0.5 * first[:, 2 * width :]
        value = value.astype(bf16)
        keys, values = self.slot(key), self.slot(value)

        def one(items):
            q, k, v = items
            return dot(softmax_rows(dot_cols(q, k), self.allowed()).astype(bf16), v)

        out = lax.map(one, (self.heads(query), self.heads(keys), self.heads(values)))
        return (query, key, value, self.rows(out).astype(bf16))

    def slot(self, value):
        return jnp.concatenate([self.rotate_parts(value, r) for r in range(self.parts)])

    def heads(self, rows):
        return rows.reshape(rows.shape[0], -1, HD).transpose(1, 0, 2)

    def rows(self, heads):
        return heads.transpose(1, 0, 2).reshape(heads.shape[1], -1)

    def allowed(self):
        key = jnp.concatenate(
            [(self.part + r) % self.parts * self.total + self.inner for r in range(self.parts)]
        )
        query = self.index[:, None]
        lowest = jnp.where(
            query < self.start, 0, jnp.where(query < self.end, self.start, self.end)
        )
        return (key[None, :] <= query) & (key[None, :] >= lowest)

    def backward(self, saved, up, carry, last):
        query, key, value = saved
        total, width = query.shape
        if self.parts == 1:
            operands = [self.scalars, self.cosine, self.sine, query, key, value, up]
            if last:
                operands.append(carry)
            return kernel_call(
                functools.partial(attention_back_kernel, last),
                [
                    jax.ShapeDtypeStruct((total, 3 * width), bf16),
                    jax.ShapeDtypeStruct((total, width), f32),
                ],
                operands,
                [pltpu.VMEM((total, width), f32)] * 2,
                flops=7 * total * total * width,
            )
        keys, values = self.slot(key), self.slot(value)

        def one(items):
            q, k, v, u = items
            chance = softmax_rows(dot_cols(q, k), self.allowed())
            back = dot_cols(u, v)
            delta = jnp.sum(chance * back, axis=-1, keepdims=True)
            score = (chance * (back - delta) * 0.125).astype(bf16)
            return (dot(score, k), dot_rows(score, q), dot_rows(chance.astype(bf16), u))

        dq, dk, dv = lax.map(
            one, (self.heads(query), self.heads(keys), self.heads(values), self.heads(up))
        )
        dk, dv = self.collect(self.rows(dk)), self.collect(self.rows(dv))
        dv = dv + carry if last else 0.5 * dv
        back_turn = functools.partial(turn, cosine=self.cosine, sine=-self.sine)
        joined = jnp.concatenate([back_turn(self.rows(dq)), back_turn(dk), dv], axis=1)
        return (joined.astype(bf16), dv)

    def collect(self, slot_rows):
        pieces = slot_rows.reshape(self.parts, self.total, -1)
        result = pieces[0]
        for r in range(1, self.parts):
            result = result + self.rotate_parts(pieces[r].astype(bf16), -r).astype(f32)
        return result


def routes(seq_size, group_size, slots_here):
    slots = slots_here * group_size
    parts = seq_size // slots
    result = []
    for r in range(slots_here):
        pairs = []
        for s in range(seq_size):
            for f in range(group_size):
                slot = slots_here * f + (s + r) % slots_here
                t = slot * parts + s // slots
                k = s % slots // slots_here
                pairs.append((s * group_size + f, t * group_size + k))
        result.append(pairs)
    return result


def shards(tokens, doc_bounds, w_qkv, w_out, w_gate, w_up, w_down, norm_attn, norm_mlp, out_grad):
    slots_here, block, model = tokens.shape
    seq_size = lax.axis_size(("sz", "sy"))
    group_size = lax.axis_size(("fx", "fc"))
    sz_size = seq_size // 2
    seq_at = lax.axis_index(("sz", "sy"))
    me = lax.axis_index(("fx", "fc"))
    parts = seq_size // (slots_here * group_size)
    local = slots_here * block
    total = local * group_size
    width = model // group_size
    in_rows = w_qkv.shape[1]
    group_rows = in_rows * group_size
    hidden_rows = w_down.shape[1]
    hidden_here = hidden_rows * seq_size
    paths = routes(seq_size, group_size, slots_here)
    backs = [[(target, source) for source, target in pairs] for pairs in paths]

    def to_group(array):
        got = [
            lax.ppermute(pick(array, (seq_at + r) % 2), ALL, paths[r]) for r in range(slots_here)
        ]
        return in_order(seq_at // parts % 2, got[0], got[1], 0).reshape(local, model)

    def from_group(rows):
        rows = rows.astype(bf16).reshape(slots_here, block, model)
        at = seq_at // parts % 2
        got = [lax.ppermute(pick(rows, (at + r) % 2), ALL, backs[r]) for r in range(slots_here)]
        return in_order(seq_at % 2, got[0], got[1], 0).astype(f32)

    bounds = lax.ppermute(pick(doc_bounds, seq_at % 2), ALL, paths[0])
    hidden = to_group(tokens).astype(f32)
    attention = Attention(me, seq_at % parts, parts, total, bounds)
    valid = attention.valid(local)

    gains = jnp.stack([norm_attn[0], norm_mlp[0], norm_attn[1], norm_mlp[1]], axis=1)
    gains = jnp.pad(gains, ((0, 0), (0, 124)))

    def gathered(own):
        return lax.all_gather(own, "sz", axis=0, tiled=False)

    def attention_weights(layer):
        pieces = w_qkv[layer].reshape(in_rows, 3, group_size, width).transpose(2, 0, 1, 3)
        pieces = pieces.reshape(group_size, in_rows, 3 * width)
        if layer == 0:
            extra = jnp.broadcast_to(gains[None], (group_size, in_rows, 128))
            pieces = jnp.concatenate([pieces, extra], axis=2)
        mine = exchange(pieces).reshape(group_rows, -1)
        outs = w_out[layer].reshape(in_rows, group_size, width).transpose(1, 0, 2)
        own = gathered(jnp.concatenate([mine, outs.reshape(group_rows, width)], axis=1))
        wide = mine.shape[1]
        into = join_y(own[:, :, :wide])
        outs = own[:, :, wide:].reshape(group_size, -1, group_size, in_rows, width)
        outs = exchange(outs.transpose(0, 1, 3, 2, 4).reshape(group_size, -1, in_rows, model))
        outs = in_order(lax.axis_index("sy"), outs, swap_y(outs), 0)
        outs = outs.transpose(2, 0, 1, 3, 4).reshape(width, model)
        return (into, outs)

    def mlp_weights(layer):
        def cut(weight):
            weight = weight[layer].reshape(in_rows, seq_size, group_size, hidden_rows)
            return weight.transpose(2, 0, 1, 3).reshape(group_size, in_rows, hidden_here)

        mine = exchange(jnp.stack([cut(w_gate), cut(w_up)], axis=1))
        mine = mine.transpose(1, 0, 2, 3).reshape(2 * group_rows, hidden_here)
        own = gathered(mine)
        return (join_y(own[:, :group_rows]), join_y(own[:, group_rows:]))

    weights = []
    in_first, out_first = attention_weights(0)
    gain_rows = in_first[:, 3 * width : 3 * width + 4].astype(f32).T
    weights.append((in_first[:, : 3 * width], out_first) + mlp_weights(0))
    downs = gathered(jnp.concatenate([w_down[0], w_down[1]]))
    downs = [join_y(downs[:, :hidden_rows]), join_y(downs[:, hidden_rows:])]
    weights.append(attention_weights(1) + mlp_weights(1))

    saved = []
    first = None
    for layer in range(LAYERS):
        qkv_w, out_w, gate_w, up_w = weights[layer]
        normed_attn, inverse_attn = normalize(hidden)
        attn_in = spread((normed_attn * gain_rows[2 * layer]).astype(bf16))
        part = jnp.concatenate([dot(rows, qkv_w) for rows in attn_in])
        query, key, value, out = attention.forward(part, first)
        if first is None:
            first = part
        outs = (out[: total // 2], out[total // 2 :])
        middle = hidden + gather_sum(dot(outs[0], out_w), dot(outs[1], out_w))
        normed_mlp, inverse_mlp = normalize(middle)
        mlp_in = spread((normed_mlp * gain_rows[2 * layer + 1]).astype(bf16))
        gates = [dot(rows, gate_w) for rows in mlp_in]
        ups = [dot(rows, up_w) for rows in mlp_in]
        active = [(jax.nn.silu(g) * u).astype(bf16) for g, u in zip(gates, ups)]
        hidden = middle + gather_sum(dot(active[0], downs[layer]), dot(active[1], downs[layer]))
        saved.append(
            (normed_attn, inverse_attn, attn_in, (query, key, value), outs)
            + (normed_mlp, inverse_mlp, mlp_in, gates, ups, active)
        )
    hidden_out = from_group(hidden * valid)

    upstream = to_group(out_grad).astype(f32) * valid
    carry = None
    grads = [None] * LAYERS
    for layer in reversed(range(LAYERS)):
        qkv_w, out_w, gate_w, up_w = weights[layer]
        (normed_attn, inverse_attn, attn_in, attn_saved, outs) = saved[layer][:5]
        (normed_mlp, inverse_mlp, mlp_in, gates, ups, active) = saved[layer][5:]
        mlp_up = spread(upstream.astype(bf16))
        gate_grads, up_grads = [], []
        for rows, gate, up in zip(mlp_up, gates, ups):
            act_grad = dot_cols(rows, downs[layer])
            sigmoid = jax.nn.sigmoid(gate)
            gate_grads.append(
                (act_grad * up * sigmoid * (1.0 + gate * (1.0 - sigmoid))).astype(bf16)
            )
            up_grads.append((act_grad * (gate * sigmoid)).astype(bf16))
        mlp_in_grad = gather_sum(
            *[dot_cols(g, gate_w) + dot_cols(u, up_w) for g, u in zip(gate_grads, up_grads)]
        )

        def sum_dots(lefts, rights):
            return (dot_rows(lefts[0], rights[0]) + dot_rows(lefts[1], rights[1])).astype(bf16)

        grad_down = reduce_rows(sum_dots(active, mlp_up), hidden_rows)
        grad_gate = sum_dots(mlp_in, gate_grads).reshape(sz_size, 2, group_rows, hidden_here)
        grad_up = sum_dots(mlp_in, up_grads).reshape(sz_size, 2, group_rows, hidden_here)
        pair = reduce_rows(jnp.concatenate([grad_gate, grad_up], axis=2), 2 * group_rows)
        pair = pair.reshape(2, group_size, in_rows, hidden_here).transpose(1, 0, 2, 3)
        pair = exchange(pair).reshape(group_size, 2, in_rows, seq_size, hidden_rows)
        pair = pair.transpose(1, 2, 3, 0, 4).reshape(2, in_rows, -1)

        norm_part, mlp_gain = norm_back(
            mlp_in_grad, normed_mlp, inverse_mlp, gain_rows[2 * layer + 1]
        )
        upstream = upstream + norm_part
        attn_up = spread(upstream.astype(bf16))
        out_back = jnp.concatenate([dot_cols(rows, out_w).astype(bf16) for rows in attn_up])
        joined, value_grad = attention.backward(attn_saved, out_back, carry, layer == 0)
        if layer > 0:
            carry = value_grad if carry is None else carry + value_grad
        halves = (joined[: total // 2], joined[total // 2 :])
        attn_in_grad = gather_sum(*[dot_cols(rows, qkv_w) for rows in halves])
        norm_part, attn_gain = norm_back(
            attn_in_grad, normed_attn, inverse_attn, gain_rows[2 * layer]
        )
        upstream = upstream + norm_part

        grad_qkv = sum_dots(attn_in, halves)
        extra = jnp.stack([attn_gain, mlp_gain], axis=1).astype(bf16)
        grad_qkv = jnp.concatenate([grad_qkv, jnp.pad(extra, ((0, 0), (0, 126)))], axis=1)
        grad_outw = sum_dots(outs, attn_up).reshape(-1, 2, group_size, in_rows, model)
        grad_outw = exchange(grad_outw.transpose(2, 0, 1, 3, 4))
        grad_outw = grad_outw.reshape(seq_size, in_rows, group_size, width)
        grad_outw = grad_outw.transpose(0, 2, 1, 3).reshape(model, width)
        mixed = reduce_rows(jnp.concatenate([grad_qkv, grad_outw], axis=1), group_rows)
        wide = grad_qkv.shape[1]
        outw = mixed[:, wide:].reshape(group_size, in_rows, width)
        outw = outw.transpose(1, 0, 2).reshape(in_rows, model)
        mixed = exchange(mixed[:, :wide].reshape(group_size, in_rows, wide)).astype(f32)
        gain_sums = jnp.sum(mixed[:, :, 3 * width : 3 * width + 2], axis=0)
        qkv = mixed[:, :, : 3 * width].reshape(group_size, in_rows, 3, width)
        qkv = qkv.transpose(1, 2, 0, 3).reshape(in_rows, 3 * model)
        grads[layer] = (qkv, outw, pair[0], pair[1], grad_down, gain_sums[:, 0], gain_sums[:, 1])

    pieces = value_grad.astype(bf16).reshape(group_size, local, width)
    order = me ^ jnp.arange(group_size, dtype=jnp.int32)
    pieces = jnp.take(pieces, order, axis=0)
    first_grad = exchange(pieces).transpose(1, 0, 2).reshape(local, model)
    stacked = [
        jnp.stack([grads[layer][member].astype(f32) for layer in range(LAYERS)])
        for member in range(7)
    ]
    return (hidden_out, from_group(upstream), *stacked, from_group(first_grad))


def solution(mesh):
    seq, fsdp = mesh.shape["seq"], mesh.shape["fsdp"]
    inner = Mesh(mesh.devices.reshape(seq // 2, 2, fsdp // 2, 2), ALL)
    rows = P(("fx", "fc"), ("sz", "sy"), None)
    weight, gain = P(None, ALL, None), P(None, ALL)
    in_specs = (rows, P(("fx", "fc"), None)) + (weight,) * 5 + (gain,) * 2 + (rows,)
    out_specs = (rows, rows) + (weight,) * 5 + (gain,) * 2 + (rows,)
    return jax.shard_map(
        shards, mesh=inner, in_specs=in_specs, out_specs=out_specs, check_vma=False
    )
```

time: 3040 us -> 861 us (0.28)
  waiting for transfers between devices: 2490 us -> 293 us
  blocking collectives: 110 us -> 0 us
  starting transfers between devices: 2.51 us -> 112 us
  matrix products: 170 us -> 96.4 us
  Pallas kernels: 0 us -> 53.7 us
  other arithmetic: 56.3 us -> 108 us
    reduce_scatter x10 -> x6, waiting for transfers between devices: 1400 us -> 0.03 us  [reduce_rows(): return lax.psum_scatter(total, 'sz', scatter_dimension=0, tiled=False)]
    all_gather x14 -> x5, waiting for transfers between devices: 821 us -> 45.5 us  [gathered(): return lax.all_gather(own, 'sz', axis=0, tiled=False)]
    unnamed x28 -> x11, waiting for transfers between devices: 262 us -> 0.18 us
    ppermute x0 -> x101, waiting for transfers between devices: none -> 248 us  [the longest x29 99.5 us: swap_x(): return lax.ppermute(value, 'fx', SWAP)]
    ppermute x0 -> x101, starting transfers between devices: none -> 110 us  [the longest x45 44.8 us: swap_core(): return lax.ppermute(value, 'fc', SWAP)]
    unnamed x2 -> x0, blocking collectives: 110 us -> none
    dot_general x44 -> x60, matrix products: 170 us -> 96.4 us  [the longest x20 39.5 us: dot_rows(): lax.dot_general(left, right, (((0,), (0,)), ((), ())), preferred_element_...]
    unnamed x206 -> x282, local copies, waits for them, and re-layouts: 101 us -> 30.1 us
  transfers between devices with their start and end apart: 26 -> 112, of which waited for: 26 -> 35; matrix products, arithmetic and copies ran while one was open for 7% -> 41% of each run, Pallas kernels for 0% -> 6%
where the time goes in v1:
time: 861 us; the launch traced here: 847 us
  waiting for transfers between devices  293 us (34%)
  local copies, waits for them, and re-layouts  165 us (19%)
  starting transfers between devices  112 us (13%)
  other arithmetic  108 us (13%)
  matrix products  96.4 us (11%)
  Pallas kernels  53.7 us (6%)
  between operations  17.6 us (2%)
    ppermute x29, waiting for transfers between devices, swap_x(): return lax.ppermute(value, 'fx', SWAP)  99.5 us
    ppermute x16, waiting for transfers between devices, swap_y(): return lax.ppermute(value, 'sy', SWAP)  83.7 us
    ppermute x6, waiting for transfers between devices, from_group(): lax.ppermute(pick(rows, (at + r) % 2), ALL, backs[r])  64 us
    pallas_call x4, Pallas kernels, kernel_call(): pl.pallas_call(body, out_shape=out_shape, in_specs=[pl.BlockSpec(memory_s...  53.7 us
    all_gather x5, waiting for transfers between devices, gathered(): return lax.all_gather(own, 'sz', axis=0, tiled=False)  45.5 us
    ppermute x45, starting transfers between devices, swap_core(): return lax.ppermute(value, 'fc', SWAP)  44.8 us
    dot_general x20, matrix products, dot_rows(): lax.dot_general(left, right, (((0,), (0,)), ((), ())), preferred_element_...  39.5 us
    select_n x16, local copies, waits for them, and re-layouts, in_order(): jnp.where(flag == 0, jnp.stack([first, second], axis), jnp.stack([second,...  35.1 us
  transfers between devices with their start and end apart: 112, of which 35 were waited for; matrix products, arithmetic and copies ran while one was open for 41% of the time, Pallas kernels for 6%

profile of v1, /device:TPU:11, one launch (start us, length us, event | category | flops | bytes accessed | tf_op | source)
XLA Modules:
  0.0 846.7 jit_solution(3557938898395368700)
XLA Ops:
  7.9 4.2 collective-permute-start.2
  14.7 4.8 collective-permute-done.3
  32.8 3.7 collective-permute-start
  41.3 27.1 %all-gather.13.cloned.1.call-done = bf16[512,1152]{1,0:T(8,128)(2,1)} async-done(((bf16[128,1152]{1,0:T(8,128)(2,1)}), bf16[512,1152]{1,0:T(8,128)(2,1)}) %all-gather.13.cloned.1.call-update) | async-done | bytes 1179664 | tf_op jit(solution)/shard_map/all_gather | solution.py:413
  78.7 5.2 collective-permute-done.9
  85.3 7.9 collective-permute-done.5
  103.0 6.1 collective-permute-done.7
  116.3 11.0 %shard_map.177 = (bf16[1024,256]{1,0:T(8,128)(2,1)S(1)}, bf16[1024,256]{1,0:T(8,128)(2,1)S(1)}, bf16[1024,256]{1,0:T(8,128)(2,1)S(1)}, bf16[1024,256]{1,0:T(8,128)(2,1)S(1)}) custom-call(s32[3]{0:T(128)S(1)} %pad_add_fusion.scalars, f32[1024,128]{1,0:T(8,128)S(1)} %get-tuple-element.184.cos_ref, f32[1024,128]{1,0:T(8,128)S(1)} %get-tuple-element.185.sin_ref, ...), custom_call_target="tpu_custom_call" | custom-call | flops 805306368 | bytes 4194304 | tf_op jit(solution)/shard_map/pallas_call | solution.py:215
  137.7 3.1 slice_bitcast_fusion.6
  142.8 3.2 slice_bitcast_fusion.11
  147.6 3.9 collective-permute-done.14
  155.4 6.2 collective-permute-start.51
  163.0 17.5 %all-gather.17.cloned.1.call-done = bf16[512,1024]{1,0:T(8,128)(2,1)} async-done(((bf16[128,1024]{1,0:T(8,128)(2,1)}), bf16[512,1024]{1,0:T(8,128)(2,1)}) %all-gather.17.cloned.1.call-update) | async-done | bytes 1048592 | tf_op jit(solution)/shard_map/all_gather | solution.py:413
  184.0 3.2 maximum_select_fusion.4
  191.4 4.6 select_n.644
  203.1 4.8 select_n.642
  218.2 3.2 multiply_convert_fusion.11
  226.9 14.0 %collective-permute-done.32 = bf16[2,1,32,1024]{3,2,0,1:T(8,128)(2,1)S(1)} collective-permute-done((bf16[2,1,32,1024]{3,2,0,1:T(8,128)(2,1)S(1)}, bf16[2,1,32,1024]{3,2,0,1:T(8,128)(2,1)S(1)}, u32[]{:S(2)}, u32[]{:S(2)}) %collective-permute-start.32) | collective-permute-done | bytes 131104 | tf_op jit(solution)/shard_map/ppermute | solution.py:39
  252.8 13.9 %collective-permute-done.34 = bf16[4,1,32,1024]{3,2,0,1:T(8,128)(2,1)} collective-permute-done((bf16[4,1,32,1024]{3,2,0,1:T(8,128)(2,1)}, bf16[4,1,32,1024]{3,2,0,1:T(8,128)(2,1)}, u32[]{:S(2)}, u32[]{:S(2)}) %collective-permute-start.34) | collective-permute-done | bytes 262176 | tf_op jit(solution)/shard_map/ppermute | solution.py:43
  270.5 2.8 fusion.74
  277.4 12.0 %shard_map.178 = (bf16[1024,256]{1,0:T(8,128)(2,1)S(1)}, bf16[1024,256]{1,0:T(8,128)(2,1)S(1)}, bf16[1024,256]{1,0:T(8,128)(2,1)S(1)}, bf16[1024,256]{1,0:T(8,128)(2,1)S(1)}) custom-call(s32[3]{0:T(128)S(1)} %pad_add_fusion.scalars, f32[1024,128]{1,0:T(8,128)S(1)} %get-tuple-element.184.cos_ref, f32[1024,128]{1,0:T(8,128)S(1)} %get-tuple-element.185.sin_ref, ...), custom_call_target="tpu_custom_call" | custom-call | flops 805306368 | bytes 4194304 | tf_op jit(solution)/shard_map/pallas_call | solution.py:215
  297.7 7.8 collective-permute-done.55
  309.3 3.3 slice_bitcast_fusion.8
  313.8 2.9 collective-permute-done.37
  323.0 4.1 collective-permute-done.43
  330.0 12.5 %collective-permute-done.42 = bf16[4,128,704]{1,2,0:T(8,128)(2,1)S(1)} collective-permute-done((bf16[4,128,704]{1,2,0:T(8,128)(2,1)S(1)}, bf16[4,128,704]{1,2,0:T(8,128)(2,1)S(1)}, u32[]{:S(2)}, u32[]{:S(2)}) %collective-permute-start.42) | collective-permute-done | bytes 720928 | tf_op jit(solution)/shard_map/ppermute | solution.py:43
  345.3 4.6 select_n.668
  349.8 8.1 collective-permute-done.41
  362.8 4.7 select_n.666
  385.8 3.7 fusion.109
  402.3 4.7 reshape.876
  407.0 4.4 add_convert_fusion.5
  411.4 4.7 reshape.875
  425.4 7.8 collective-permute-done.58
  434.7 9.7 %collective-permute-done.48 = bf16[256,1024]{1,0:T(8,128)(2,1)S(1)} collective-permute-done((bf16[256,1024]{1,0:T(8,128)(2,1)S(1)}, bf16[256,1024]{1,0:T(8,128)(2,1)S(1)}, u32[]{:S(2)}, u32[]{:S(2)}) %collective-permute-start.48) | collective-permute-done | bytes 524320 | tf_op jit(solution)/shard_map/ppermute | solution.py:39
  444.4 3.3 fusion.119
  448.7 5.8 collective-permute-done.92
  454.5 3.2 fusion
  468.6 14.7 %shard_map.179 = (bf16[1024,768]{1,0:T(8,128)(2,1)S(1)}, f32[1024,256]{1,0:T(8,128)S(1)}) custom-call(s32[3]{0:T(128)S(1)} %pad_add_fusion.scalars, f32[1024,128]{1,0:T(8,128)S(1)} %get-tuple-element.184.cos_ref, f32[1024,128]{1,0:T(8,128)S(1)} %get-tuple-element.185.sin_ref, bf16[1024,256]{1,0:T(8,128)(2,1)S(1)} %copy-done.5, ...), custom_call_target="tpu_custom_call" | custom-call | flops 1879048192 | bytes 4194304 | tf_op jit(solution)/shard_map/pallas_call | solution.py:215
  490.2 3.4 collective-permute-done.84
  501.2 5.9 collective-permute-done.64
  511.4 25.1 %collective-permute-done.86 = bf16[4,128,1152]{2,1,0:T(8,128)(2,1)S(1)} collective-permute-done((bf16[4,128,1152]{2,1,0:T(8,128)(2,1)S(1)}, bf16[4,128,1152]{2,1,0:T(8,128)(2,1)S(1)}, u32[]{:S(2)}, u32[]{:S(2)}) %collective-permute-start.86) | collective-permute-done | bytes 1179680 | tf_op jit(solution)/shard_map/ppermute | solution.py:43
  545.3 3.2 collective-permute-start.65
  549.2 2.8 collective-permute-start.49
  557.3 23.4 %collective-permute-done.49 = bf16[128,1024]{1,0:T(8,128)(2,1)} collective-permute-done((bf16[128,1024]{1,0:T(8,128)(2,1)}, bf16[128,1024]{1,0:T(8,128)(2,1)}, u32[]{:S(2)}, u32[]{:S(2)}) %collective-permute-start.49) | collective-permute-done | bytes 262176 | tf_op jit(solution)/shard_map/ppermute | solution.py:401
  580.8 5.5 collective-permute-done.50
  588.5 3.5 multiply_convert_fusion.2
  596.7 3.5 collective-permute-start.66
  619.7 5.1 reshape.872
  627.6 4.7 reshape.873
  647.2 7.7 collective-permute-done.70
  657.3 3.1 fusion.117
  665.8 5.7 collective-permute-done.89
  671.4 3.2 fusion.1
  682.8 15.9 %shard_map.180 = (bf16[1024,768]{1,0:T(8,128)(2,1)}, f32[1024,256]{1,0:T(8,128)S(1)}) custom-call(s32[3]{0:T(128)S(1)} %pad_add_fusion.scalars, f32[1024,128]{1,0:T(8,128)S(1)} %get-tuple-element.184.cos_ref, f32[1024,128]{1,0:T(8,128)S(1)} %get-tuple-element.185.sin_ref, bf16[1024,256]{1,0:T(8,128)(2,1)S(1)} %get-tuple-element.28.refs_0_, ...), custom_call_target="tpu_custom_call" | custom-call | flops 1879048192 | bytes 4194304 | tf_op jit(solution)/shard_map/pallas_call | solution.py:215
  710.6 8.4 collective-permute-done.79
  728.0 6.9 collective-permute-done.76
  756.0 3.7 collective-permute-start.99
  772.5 3.8 collective-permute-start.90
  780.3 3.3 collective-permute-start.78
  786.5 3.4 collective-permute-done.100
  792.1 24.4 %collective-permute-done.77 = bf16[128,1024]{1,0:T(8,128)(2,1)S(1)} collective-permute-done((bf16[128,1024]{1,0:T(8,128)(2,1)S(1)}, bf16[128,1024]{1,0:T(8,128)(2,1)S(1)}, u32[]{:S(2)}, u32[]{:S(2)}) %collective-permute-start.77) | collective-permute-done | bytes 262176 | tf_op jit(solution)/shard_map/ppermute | solution.py:401
  816.6 7.3 collective-permute-done.78
  832.5 3.1 collective-permute-start.83
  (809 shorter events, 370.8 us)
Async XLA Ops:
  7.2 61.2 %all-gather.13.cloned.1.call-start = ((), (), s32[]{:S(2)}) async-start(), calls=%async_computation.14 | async-start | bytes 1474560 | tf_op jit(solution)/shard_map/all_gather | solution.py:413
  7.9 24.9 %collective-permute-start.2 = (s32[2]{0:T(128)S(1)}, s32[2]{0:T(128)S(1)}, u32[]{:S(2)}, u32[]{:S(2)}) collective-permute-start(s32[2]{0:T(128)S(1)} %fusion.96), channel_id=1, source_target_pairs={{0,0},{1,8},{2,16},{3,24},{4,4},{5,12},{6,20},{7,28},{8,1},{9,9},{... | collective-permute-start | bytes 32 | tf_op jit(solution)/shard_map/ppermute | solution.py:404
  21.7 115.9 %all-gather.15.cloned.1.call-start = ((), (), s32[]{:S(2)}) async-start(), calls=%async_computation.15 | async-start | bytes 1802240 | tf_op jit(solution)/shard_map/all_gather | solution.py:413
  23.4 47.3 %collective-permute-start.39 = (bf16[2,2,32,704]{3,2,0,1:T(8,128)(2,1)}, bf16[2,2,32,704]{3,2,0,1:T(8,128)(2,1)S(1)}, u32[]{:S(2)}, u32[]{:S(2)}) collective-permute-start(bf16[2,2,32,704]{3,2,0,1:T(8,128)(2,1)} %get-tuple-element.126), channel_id=1, source_target_pairs={{0,2},{2,0},{1,3},{3,1},{4,6},{6,4},{5,7},{7,5},{8,10},{10,8},{9,1... | collective-permute-start | bytes 540680 | tf_op jit(solution)/shard_map/ppermute | solution.py:39
  25.9 47.7 %collective-permute-start.16 = (bf16[2,2,32,704]{3,2,0,1:T(8,128)(2,1)}, bf16[2,2,32,704]{3,2,0,1:T(8,128)(2,1)}, u32[]{:S(2)}, u32[]{:S(2)}) collective-permute-start(bf16[2,2,32,704]{3,2,0,1:T(8,128)(2,1)} %get-tuple-element.132), channel_id=1, source_target_pairs={{0,2},{2,0},{1,3},{3,1},{4,6},{6,4},{5,7},{7,5},{8,10},{10,8},{9,1... | collective-permute-start | bytes 540680 | tf_op jit(solution)/shard_map/ppermute | solution.py:39
  28.5 73.3 %collective-permute-start.27 = (bf16[2,32,768]{2,1,0:T(8,128)(2,1)}, bf16[2,32,768]{2,1,0:T(8,128)(2,1)}, u32[]{:S(2)}, u32[]{:S(2)}) collective-permute-start(bf16[2,32,768]{2,1,0:T(8,128)(2,1)} %get-tuple-element.162), channel_id=1, source_target_pairs={{0,2},{2,0},{1,3},{3,1},{4,6},{6,4},{5,7},{7,5},{8,10},{10,8},{9,1... | collective-permute-start | bytes 294920 | tf_op jit(solution)/shard_map/ppermute | solution.py:39
  29.4 47.6 %collective-permute-start.1 = (bf16[128,1024]{1,0:T(8,128)(2,1)}, bf16[128,1024]{1,0:T(8,128)(2,1)S(1)}, u32[]{:S(2)}, u32[]{:S(2)}) collective-permute-start(bf16[128,1024]{1,0:T(8,128)(2,1)} %get-tuple-element.113), channel_id=1, source_target_pairs={{0,4},{1,12},{2,20},{3,28},{4,0},{5,8},{6,16},{7,24},{8,5},{9,13},... | collective-permute-start | bytes 786440 | tf_op jit(solution)/shard_map/ppermute | solution.py:394
  32.6 110.3 %all-gather.9.cloned.1.call-start = ((), (), s32[]{:S(2)}) async-start(), calls=%async_computation.6 | async-start | bytes 1802240 | tf_op jit(solution)/shard_map/all_gather | solution.py:413
  32.8 44.1 %collective-permute-start = (bf16[128,1024]{1,0:T(8,128)(2,1)}, bf16[128,1024]{1,0:T(8,128)(2,1)S(1)}, u32[]{:S(2)}, u32[]{:S(2)}) collective-permute-start(bf16[128,1024]{1,0:T(8,128)(2,1)} %get-tuple-element.114), channel_id=1, source_target_pairs={{0,0},{1,8},{2,16},{3,24},{4,4},{5,12},{6,20},{7,28},{8,1},{9,9},{... | collective-permute-start | bytes 786440 | tf_op jit(solution)/shard_map/ppermute | solution.py:394
  70.8 22.4 %collective-permute-start.5 = (bf16[4,128,896]{2,1,0:T(8,128)(2,1)}, bf16[4,128,896]{2,1,0:T(8,128)(2,1)}, u32[]{:S(2)}, u32[]{:S(2)}) collective-permute-start(bf16[4,128,896]{2,1,0:T(8,128)(2,1)} %get-tuple-element.85), channel_id=1, source_target_pairs={{0,4},{4,0},{1,5},{5,1},{2,6},{6,2},{3,7},{7,3},{8,12},{12,8},{9,1... | collective-permute-start | bytes 2752520 | tf_op jit(solution)/shard_map/ppermute | solution.py:43
  76.2 20.3 %collective-permute-start.17 = (bf16[2,2,32,704]{3,2,1,0:T(8,128)(2,1)}, bf16[2,2,32,704]{3,2,1,0:T(8,128)(2,1)}, u32[]{:S(2)}, u32[]{:S(2)}) collective-permute-start(bf16[2,2,32,704]{3,2,1,0:T(8,128)(2,1)} %bitcast.475), channel_id=1, source_target_pairs={{0,1},{1,0},{2,3},{3,2},{4,5},{5,4},{6,7},{7,6},{8,9},{9,8},{10,11... | collective-permute-start | bytes 540680 | tf_op jit(solution)/shard_map/ppermute | solution.py:35
  98.7 81.8 %all-gather.17.cloned.1.call-start = ((), (), s32[]{:S(2)}) async-start(), calls=%async_computation.16 | async-start | bytes 1310720 | tf_op jit(solution)/shard_map/all_gather | solution.py:413
  102.9 27.1 %collective-permute-start.28 = (bf16[2,32,768]{2,1,0:T(8,128)(2,1)S(1)}, bf16[2,32,768]{2,1,0:T(8,128)(2,1)S(1)}, u32[]{:S(2)}, u32[]{:S(2)}) collective-permute-start(bf16[2,32,768]{2,1,0:T(8,128)(2,1)S(1)} %get-tuple-element.160), channel_id=1, source_target_pairs={{0,1},{1,0},{2,3},{3,2},{4,5},{5,4},{6,7},{7,6},{8,9},{9,8},{10,11... | collective-permute-start | bytes 294920 | tf_op jit(solution)/shard_map/ppermute | solution.py:35
  130.8 178.5 %all-gather.11.cloned.1.call-start = ((), (), s32[]{:S(2)}) async-start(), calls=%async_computation.7 | async-start | bytes 1802240 | tf_op jit(solution)/shard_map/all_gather | solution.py:413
  140.8 42.8 %collective-permute-start.20 = (bf16[4,88,1024]{2,1,0:T(8,128)(2,1)}, bf16[4,88,1024]{2,1,0:T(8,128)(2,1)}, u32[]{:S(2)}, u32[]{:S(2)}) collective-permute-start(bf16[4,88,1024]{2,1,0:T(8,128)(2,1)} %get-tuple-element.75), channel_id=1, source_target_pairs={{0,4},{4,0},{1,5},{5,1},{2,6},{6,2},{3,7},{7,3},{8,12},{12,8},{9,1... | collective-permute-start | bytes 2162696 | tf_op jit(solution)/shard_map/ppermute | solution.py:43
  146.1 41.2 %collective-permute-start.19 = (bf16[4,128,704]{1,2,0:T(8,128)(2,1)}, bf16[4,128,704]{1,2,0:T(8,128)(2,1)}, u32[]{:S(2)}, u32[]{:S(2)}) collective-permute-start(bf16[4,128,704]{1,2,0:T(8,128)(2,1)} %get-tuple-element.82), channel_id=1, source_target_pairs={{0,4},{4,0},{1,5},{5,1},{2,6},{6,2},{3,7},{7,3},{8,12},{12,8},{9,1... | collective-permute-start | bytes 2162696 | tf_op jit(solution)/shard_map/ppermute | solution.py:43
  147.3 51.0 %collective-permute-start.18 = (bf16[4,128,704]{1,2,0:T(8,128)(2,1)}, bf16[4,128,704]{1,2,0:T(8,128)(2,1)}, u32[]{:S(2)}, u32[]{:S(2)}) collective-permute-start(bf16[4,128,704]{1,2,0:T(8,128)(2,1)} %get-tuple-element.83), channel_id=1, source_target_pairs={{0,4},{4,0},{1,5},{5,1},{2,6},{6,2},{3,7},{7,3},{8,12},{12,8},{9,1... | collective-permute-start | bytes 2162696 | tf_op jit(solution)/shard_map/ppermute | solution.py:43
  154.3 41.7 %collective-permute-start.22 = (bf16[256,1024]{1,0:T(8,128)(2,1)S(1)}, bf16[256,1024]{1,0:T(8,128)(2,1)}, u32[]{:S(2)}, u32[]{:S(2)}) collective-permute-start(bf16[256,1024]{1,0:T(8,128)(2,1)S(1)} %multiply_convert_fusion.14), channel_id=1, source_target_pairs={{0,2},{2,0},{1,3},{3,1},{4,6},{6,4},{5,7},{7,5},{8,10},{10,8},{9,1... | collective-permute-start | bytes 1572872 | tf_op jit(solution)/shard_map/ppermute | solution.py:39
  155.4 90.3 %collective-permute-start.51 = (bf16[128,1024]{1,0:T(8,128)(2,1)}, bf16[128,1024]{1,0:T(8,128)(2,1)}, u32[]{:S(2)}, u32[]{:S(2)}) collective-permute-start(bf16[128,1024]{1,0:T(8,128)(2,1)} %get-tuple-element.109), channel_id=1, source_target_pairs={{0,0},{1,8},{2,16},{3,24},{4,4},{5,12},{6,20},{7,28},{8,1},{9,9},{... | collective-permute-start | bytes 786440 | tf_op jit(solution)/shard_map/ppermute | solution.py:394
  183.5 25.4 %collective-permute-start.15 = (bf16[256,1024]{1,0:T(8,128)(2,1)S(1)}, bf16[256,1024]{1,0:T(8,128)(2,1)}, u32[]{:S(2)}, u32[]{:S(2)}) collective-permute-start(bf16[256,1024]{1,0:T(8,128)(2,1)S(1)} %multiply_convert_fusion.14), channel_id=1, source_target_pairs={{0,1},{1,0},{2,3},{3,2},{4,5},{5,4},{6,7},{7,6},{8,9},{9,8},{10,11... | collective-permute-start | bytes 1572872 | tf_op jit(solution)/shard_map/ppermute | solution.py:35
  187.3 59.6 %collective-permute-start.52 = (bf16[128,1024]{1,0:T(8,128)(2,1)}, bf16[128,1024]{1,0:T(8,128)(2,1)}, u32[]{:S(2)}, u32[]{:S(2)}) collective-permute-start(bf16[128,1024]{1,0:T(8,128)(2,1)} %get-tuple-element.110), channel_id=1, source_target_pairs={{0,4},{1,12},{2,20},{3,28},{4,0},{5,8},{6,16},{7,24},{8,5},{9,13},... | collective-permute-start | bytes 786440 | tf_op jit(solution)/shard_map/ppermute | solution.py:394
  222.5 19.0 %collective-permute-start.21 = (bf16[256,1024]{1,0:T(8,128)(2,1)S(1)}, bf16[256,1024]{1,0:T(8,128)(2,1)S(1)}, u32[]{:S(2)}, u32[]{:S(2)}) collective-permute-start(bf16[256,1024]{1,0:T(8,128)(2,1)S(1)} %slice.628), channel_id=1, source_target_pairs={{0,1},{1,0},{2,3},{3,2},{4,5},{5,4},{6,7},{7,6},{8,9},{9,8},{10,11... | collective-permute-start | bytes 1572872 | tf_op jit(solution)/shard_map/ppermute | solution.py:35
  223.2 18.6 %collective-permute-start.25 = (bf16[256,1024]{1,0:T(8,128)(2,1)S(1)}, bf16[256,1024]{1,0:T(8,128)(2,1)S(1)}, u32[]{:S(2)}, u32[]{:S(2)}) collective-permute-start(bf16[256,1024]{1,0:T(8,128)(2,1)S(1)} %fusion.28), channel_id=1, source_target_pairs={{0,2},{2,0},{1,3},{3,1},{4,6},{6,4},{5,7},{7,5},{8,10},{10,8},{9,1... | collective-permute-start | bytes 1572872 | tf_op jit(solution)/shard_map/ppermute | solution.py:39
  241.5 27.3 %collective-permute-start.29 = (bf16[4,128,768]{2,1,0:T(8,128)(2,1)}, bf16[4,128,768]{2,1,0:T(8,128)(2,1)}, u32[]{:S(2)}, u32[]{:S(2)}) collective-permute-start(bf16[4,128,768]{2,1,0:T(8,128)(2,1)} %get-tuple-element.88), channel_id=1, source_target_pairs={{0,4},{4,0},{1,5},{5,1},{2,6},{6,2},{3,7},{7,3},{8,12},{12,8},{9,1... | collective-permute-start | bytes 2359304 | tf_op jit(solution)/shard_map/ppermute | solution.py:43
  243.5 24.5 %collective-permute-start.30 = (bf16[256,1024]{1,0:T(8,128)(2,1)}, bf16[256,1024]{1,0:T(8,128)(2,1)}, u32[]{:S(2)}, u32[]{:S(2)}) collective-permute-start(bf16[256,1024]{1,0:T(8,128)(2,1)} %multiply_convert_fusion.13), channel_id=1, source_target_pairs={{0,2},{2,0},{1,3},{3,1},{4,6},{6,4},{5,7},{7,5},{8,10},{10,8},{9,1... | collective-permute-start | bytes 1572872 | tf_op jit(solution)/shard_map/ppermute | solution.py:39
  245.7 21.0 %collective-permute-start.34 = (bf16[4,1,32,1024]{3,2,0,1:T(8,128)(2,1)}, bf16[4,1,32,1024]{3,2,0,1:T(8,128)(2,1)}, u32[]{:S(2)}, u32[]{:S(2)}) collective-permute-start(bf16[4,1,32,1024]{3,2,0,1:T(8,128)(2,1)} %bitcast.75), channel_id=1, source_target_pairs={{0,4},{4,0},{1,5},{5,1},{2,6},{6,2},{3,7},{7,3},{8,12},{12,8},{9,1... | collective-permute-start | bytes 786440 | tf_op jit(solution)/shard_map/ppermute | solution.py:43
  248.9 21.6 %collective-permute-start.26 = (bf16[256,1024]{1,0:T(8,128)(2,1)}, bf16[256,1024]{1,0:T(8,128)(2,1)}, u32[]{:S(2)}, u32[]{:S(2)}) collective-permute-start(bf16[256,1024]{1,0:T(8,128)(2,1)} %multiply_convert_fusion.13), channel_id=1, source_target_pairs={{0,1},{1,0},{2,3},{3,2},{4,5},{5,4},{6,7},{7,6},{8,9},{9,8},{10,11... | collective-permute-start | bytes 1572872 | tf_op jit(solution)/shard_map/ppermute | solution.py:35
  252.5 379.8 %reduce-scatter.13.cloned.1.call-start = ((), (), s32[]{:S(2)}) async-start(), calls=%async_computation.11 | async-start | bytes 1802240 | tf_op jit(solution)/shard_map/reduce_scatter | solution.py:76
  295.9 16.7 %collective-permute-start.35 = (bf16[256,1024]{1,0:T(8,128)(2,1)}, bf16[256,1024]{1,0:T(8,128)(2,1)}, u32[]{:S(2)}, u32[]{:S(2)}) collective-permute-start(bf16[256,1024]{1,0:T(8,128)(2,1)} %slice.626), channel_id=1, source_target_pairs={{0,1},{1,0},{2,3},{3,2},{4,5},{5,4},{6,7},{7,6},{8,9},{9,8},{10,11... | collective-permute-start | bytes 1572872 | tf_op jit(solution)/shard_map/ppermute | solution.py:35
  297.4 19.3 %collective-permute-start.37 = (bf16[256,1024]{1,0:T(8,128)(2,1)}, bf16[256,1024]{1,0:T(8,128)(2,1)}, u32[]{:S(2)}, u32[]{:S(2)}) collective-permute-start(bf16[256,1024]{1,0:T(8,128)(2,1)} %fusion.25), channel_id=1, source_target_pairs={{0,2},{2,0},{1,3},{3,1},{4,6},{6,4},{5,7},{7,5},{8,10},{10,8},{9,1... | collective-permute-start | bytes 1572872 | tf_op jit(solution)/shard_map/ppermute | solution.py:39
  297.4 76.6 %collective-permute-start.53 = (bf16[256,1024]{1,0:T(8,128)(2,1)}, bf16[256,1024]{1,0:T(8,128)(2,1)}, u32[]{:S(2)}, u32[]{:S(2)}) collective-permute-start(bf16[256,1024]{1,0:T(8,128)(2,1)} %fusion.35), channel_id=1, source_target_pairs={{0,1},{1,0},{2,3},{3,2},{4,5},{5,4},{6,7},{7,6},{8,9},{9,8},{10,11... | collective-permute-start | bytes 1572872 | tf_op jit(solution)/shard_map/ppermute | solution.py:35
  309.0 18.1 %collective-permute-start.43 = (bf16[4,88,1024]{2,1,0:T(8,128)(2,1)}, bf16[4,88,1024]{2,1,0:T(8,128)(2,1)}, u32[]{:S(2)}, u32[]{:S(2)}) collective-permute-start(bf16[4,88,1024]{2,1,0:T(8,128)(2,1)} %get-tuple-element.74), channel_id=1, source_target_pairs={{0,4},{4,0},{1,5},{5,1},{2,6},{6,2},{3,7},{7,3},{8,12},{12,8},{9,1... | collective-permute-start | bytes 2162696 | tf_op jit(solution)/shard_map/ppermute | solution.py:43
  312.6 29.8 %collective-permute-start.42 = (bf16[4,128,704]{1,2,0:T(8,128)(2,1)S(1)}, bf16[4,128,704]{1,2,0:T(8,128)(2,1)S(1)}, u32[]{:S(2)}, u32[]{:S(2)}) collective-permute-start(bf16[4,128,704]{1,2,0:T(8,128)(2,1)S(1)} %get-tuple-element.78), channel_id=1, source_target_pairs={{0,4},{4,0},{1,5},{5,1},{2,6},{6,2},{3,7},{7,3},{8,12},{12,8},{9,1... | collective-permute-start | bytes 2162696 | tf_op jit(solution)/shard_map/ppermute | solution.py:43
  316.7 41.3 %collective-permute-start.41 = (bf16[4,128,704]{1,2,0:T(8,128)(2,1)}, bf16[4,128,704]{1,2,0:T(8,128)(2,1)}, u32[]{:S(2)}, u32[]{:S(2)}) collective-permute-start(bf16[4,128,704]{1,2,0:T(8,128)(2,1)} %get-tuple-element.79), channel_id=1, source_target_pairs={{0,4},{4,0},{1,5},{5,1},{2,6},{6,2},{3,7},{7,3},{8,12},{12,8},{9,1... | collective-permute-start | bytes 2162696 | tf_op jit(solution)/shard_map/ppermute | solution.py:43
  320.6 48.5 %collective-permute-start.38 = (bf16[256,1024]{1,0:T(8,128)(2,1)}, bf16[256,1024]{1,0:T(8,128)(2,1)}, u32[]{:S(2)}, u32[]{:S(2)}) collective-permute-start(bf16[256,1024]{1,0:T(8,128)(2,1)} %multiply_convert_fusion.12), channel_id=1, source_target_pairs={{0,1},{1,0},{2,3},{3,2},{4,5},{5,4},{6,7},{7,6},{8,9},{9,8},{10,11... | collective-permute-start | bytes 1572872 | tf_op jit(solution)/shard_map/ppermute | solution.py:35
  378.7 56.0 %collective-permute-start.44 = (bf16[256,1024]{1,0:T(8,128)(2,1)}, bf16[256,1024]{1,0:T(8,128)(2,1)}, u32[]{:S(2)}, u32[]{:S(2)}) collective-permute-start(bf16[256,1024]{1,0:T(8,128)(2,1)} %slice.624), channel_id=1, source_target_pairs={{0,1},{1,0},{2,3},{3,2},{4,5},{5,4},{6,7},{7,6},{8,9},{9,8},{10,11... | collective-permute-start | bytes 1572872 | tf_op jit(solution)/shard_map/ppermute | solution.py:35
  383.1 42.2 %collective-permute-start.54 = (bf16[256,1024]{1,0:T(8,128)(2,1)}, bf16[256,1024]{1,0:T(8,128)(2,1)}, u32[]{:S(2)}, u32[]{:S(2)}) collective-permute-start(bf16[256,1024]{1,0:T(8,128)(2,1)} %slice.622), channel_id=1, source_target_pairs={{0,1},{1,0},{2,3},{3,2},{4,5},{5,4},{6,7},{7,6},{8,9},{9,8},{10,11... | collective-permute-start | bytes 1572872 | tf_op jit(solution)/shard_map/ppermute | solution.py:35
  395.3 26.3 %collective-permute-start.47 = (bf16[256,1024]{1,0:T(8,128)(2,1)}, bf16[256,1024]{1,0:T(8,128)(2,1)}, u32[]{:S(2)}, u32[]{:S(2)}) collective-permute-start(bf16[256,1024]{1,0:T(8,128)(2,1)} %slice.623), channel_id=1, source_target_pairs={{0,1},{1,0},{2,3},{3,2},{4,5},{5,4},{6,7},{7,6},{8,9},{9,8},{10,11... | collective-permute-start | bytes 1572872 | tf_op jit(solution)/shard_map/ppermute | solution.py:35
  399.8 18.0 %collective-permute-start.57 = (bf16[256,1024]{1,0:T(8,128)(2,1)}, bf16[256,1024]{1,0:T(8,128)(2,1)}, u32[]{:S(2)}, u32[]{:S(2)}) collective-permute-start(bf16[256,1024]{1,0:T(8,128)(2,1)} %slice.621), channel_id=1, source_target_pairs={{0,1},{1,0},{2,3},{3,2},{4,5},{5,4},{6,7},{7,6},{8,9},{9,8},{10,11... | collective-permute-start | bytes 1572872 | tf_op jit(solution)/shard_map/ppermute | solution.py:35
  421.3 33.2 %collective-permute-start.92 = (bf16[4,256,704]{1,2,0:T(8,128)(2,1)}, bf16[4,256,704]{1,2,0:T(8,128)(2,1)}, u32[]{:S(2)}, u32[]{:S(2)}) collective-permute-start(bf16[4,256,704]{1,2,0:T(8,128)(2,1)} %dynamic-slice_bitcast_fusion), channel_id=1, source_target_pairs={{0,4},{4,0},{1,5},{5,1},{2,6},{6,2},{3,7},{7,3},{8,12},{12,8},{9,1... | collective-permute-start | bytes 4325384 | tf_op jit(solution)/shard_map/ppermute | solution.py:43
  423.9 20.5 %collective-permute-start.48 = (bf16[256,1024]{1,0:T(8,128)(2,1)S(1)}, bf16[256,1024]{1,0:T(8,128)(2,1)S(1)}, u32[]{:S(2)}, u32[]{:S(2)}) collective-permute-start(bf16[256,1024]{1,0:T(8,128)(2,1)S(1)} %fusion.20), channel_id=1, source_target_pairs={{0,2},{2,0},{1,3},{3,1},{4,6},{6,4},{5,7},{7,5},{8,10},{10,8},{9,1... | collective-permute-start | bytes 1572872 | tf_op jit(solution)/shard_map/ppermute | solution.py:39
  447.7 15.7 %collective-permute-start.59 = (bf16[256,1024]{1,0:T(8,128)(2,1)}, bf16[256,1024]{1,0:T(8,128)(2,1)}, u32[]{:S(2)}, u32[]{:S(2)}) collective-permute-start(bf16[256,1024]{1,0:T(8,128)(2,1)} %get-tuple-element.54), channel_id=1, source_target_pairs={{0,1},{1,0},{2,3},{3,2},{4,5},{5,4},{6,7},{7,6},{8,9},{9,8},{10,11... | collective-permute-start | bytes 1572872 | tf_op jit(solution)/shard_map/ppermute | solution.py:35
  457.8 285.2 %reduce-scatter.9.cloned.1.call-start = ((), (), s32[]{:S(2)}) async-start(), calls=%async_computation.9 | async-start | bytes 1474560 | tf_op jit(solution)/shard_map/reduce_scatter | solution.py:76
  511.2 25.3 %collective-permute-start.86 = (bf16[4,128,1152]{2,1,0:T(8,128)(2,1)S(1)}, bf16[4,128,1152]{2,1,0:T(8,128)(2,1)S(1)}, u32[]{:S(2)}, u32[]{:S(2)}) collective-permute-start(bf16[4,128,1152]{2,1,0:T(8,128)(2,1)S(1)} %dynamic-slice_bitcast_fusion.2), channel_id=1, source_target_pairs={{0,4},{4,0},{1,5},{5,1},{2,6},{6,2},{3,7},{7,3},{8,12},{12,8},{9,1... | collective-permute-start | bytes 3538952 | tf_op jit(solution)/shard_map/ppermute | solution.py:43
  537.8 206.7 %reduce-scatter.17.cloned.1.call-start = ((), (), s32[]{:S(2)}) async-start(), calls=%async_computation.13 | async-start | bytes 901120 | tf_op jit(solution)/shard_map/reduce_scatter | solution.py:76
  545.3 43.2 %collective-permute-start.65 = (bf16[256,1024]{1,0:T(8,128)(2,1)S(1)}, bf16[256,1024]{1,0:T(8,128)(2,1)}, u32[]{:S(2)}, u32[]{:S(2)}) collective-permute-start(bf16[256,1024]{1,0:T(8,128)(2,1)S(1)} %get-tuple-element.52), channel_id=1, source_target_pairs={{0,1},{1,0},{2,3},{3,2},{4,5},{5,4},{6,7},{7,6},{8,9},{9,8},{10,11... | collective-permute-start | bytes 1572872 | tf_op jit(solution)/shard_map/ppermute | solution.py:35
  549.2 31.5 %collective-permute-start.49 = (bf16[128,1024]{1,0:T(8,128)(2,1)}, bf16[128,1024]{1,0:T(8,128)(2,1)}, u32[]{:S(2)}, u32[]{:S(2)}) collective-permute-start(bf16[128,1024]{1,0:T(8,128)(2,1)} %get-tuple-element.111), channel_id=1, source_target_pairs={{0,0},{8,1},{16,2},{24,3},{4,4},{12,5},{20,6},{28,7},{1,8},{9,9},{... | collective-permute-start | bytes 786440 | tf_op jit(solution)/shard_map/ppermute | solution.py:401
  552.0 34.2 %collective-permute-start.50 = (bf16[128,1024]{1,0:T(8,128)(2,1)S(1)}, bf16[128,1024]{1,0:T(8,128)(2,1)}, u32[]{:S(2)}, u32[]{:S(2)}) collective-permute-start(bf16[128,1024]{1,0:T(8,128)(2,1)S(1)} %get-tuple-element.112), channel_id=1, source_target_pairs={{4,0},{12,1},{20,2},{28,3},{0,4},{8,5},{16,6},{24,7},{5,8},{13,9},... | collective-permute-start | bytes 786440 | tf_op jit(solution)/shard_map/ppermute | solution.py:401
  557.0 187.4 %reduce-scatter.15.cloned.1.call-start = ((), (), s32[]{:S(2)}) async-start(), calls=%async_computation.12 | async-start | bytes 901120 | tf_op jit(solution)/shard_map/reduce_scatter | solution.py:76
  596.7 50.6 %collective-permute-start.66 = (bf16[256,1024]{1,0:T(8,128)(2,1)}, bf16[256,1024]{1,0:T(8,128)(2,1)}, u32[]{:S(2)}, u32[]{:S(2)}) collective-permute-start(bf16[256,1024]{1,0:T(8,128)(2,1)} %slice.618), channel_id=1, source_target_pairs={{0,1},{1,0},{2,3},{3,2},{4,5},{5,4},{6,7},{7,6},{8,9},{9,8},{10,11... | collective-permute-start | bytes 1572872 | tf_op jit(solution)/shard_map/ppermute | solution.py:35
  610.4 33.7 %collective-permute-start.95 = (bf16[4,88,1024]{2,1,0:T(8,128)(2,1)}, bf16[4,88,1024]{2,1,0:T(8,128)(2,1)}, u32[]{:S(2)}, u32[]{:S(2)}) collective-permute-start(bf16[4,88,1024]{2,1,0:T(8,128)(2,1)} %dynamic-slice_bitcast_fusion.5), channel_id=1, source_target_pairs={{0,4},{4,0},{1,5},{5,1},{2,6},{6,2},{3,7},{7,3},{8,12},{12,8},{9,1... | collective-permute-start | bytes 2162696 | tf_op jit(solution)/shard_map/ppermute | solution.py:43
  613.8 26.6 %collective-permute-start.69 = (bf16[256,1024]{1,0:T(8,128)(2,1)S(1)}, bf16[256,1024]{1,0:T(8,128)(2,1)}, u32[]{:S(2)}, u32[]{:S(2)}) collective-permute-start(bf16[256,1024]{1,0:T(8,128)(2,1)S(1)} %slice.617), channel_id=1, source_target_pairs={{0,1},{1,0},{2,3},{3,2},{4,5},{5,4},{6,7},{7,6},{8,9},{9,8},{10,11... | collective-permute-start | bytes 1572872 | tf_op jit(solution)/shard_map/ppermute | solution.py:35
  639.1 32.4 %collective-permute-start.89 = (bf16[4,256,704]{1,2,0:T(8,128)(2,1)}, bf16[4,256,704]{1,2,0:T(8,128)(2,1)}, u32[]{:S(2)}, u32[]{:S(2)}) collective-permute-start(bf16[4,256,704]{1,2,0:T(8,128)(2,1)} %dynamic-slice_bitcast_fusion.1), channel_id=1, source_target_pairs={{0,4},{4,0},{1,5},{5,1},{2,6},{6,2},{3,7},{7,3},{8,12},{12,8},{9,1... | collective-permute-start | bytes 4325384 | tf_op jit(solution)/shard_map/ppermute | solution.py:43
  646.4 124.9 %reduce-scatter.11.cloned.1.call-start = ((), (), s32[]{:S(2)}) async-start(), calls=%async_computation.10 | async-start | bytes 1802240 | tf_op jit(solution)/shard_map/reduce_scatter | solution.py:76
  661.3 16.7 %collective-permute-start.71 = (bf16[256,1024]{1,0:T(8,128)(2,1)}, bf16[256,1024]{1,0:T(8,128)(2,1)}, u32[]{:S(2)}, u32[]{:S(2)}) collective-permute-start(bf16[256,1024]{1,0:T(8,128)(2,1)} %get-tuple-element.50), channel_id=1, source_target_pairs={{0,1},{1,0},{2,3},{3,2},{4,5},{5,4},{6,7},{7,6},{8,9},{9,8},{10,11... | collective-permute-start | bytes 1572872 | tf_op jit(solution)/shard_map/ppermute | solution.py:35
  674.7 153.0 %reduce-scatter.7.cloned.1.call-start = ((), (), s32[]{:S(2)}) async-start(), calls=%async_computation.8 | async-start | bytes 1474560 | tf_op jit(solution)/shard_map/reduce_scatter | solution.py:76
  705.5 19.2 %collective-permute-start.97 = (bf16[2,256,256]{2,1,0:T(8,128)(2,1)S(1)}, bf16[2,256,256]{2,1,0:T(8,128)(2,1)S(1)}, u32[]{:S(2)}, u32[]{:S(2)}) collective-permute-start(bf16[2,256,256]{2,1,0:T(8,128)(2,1)S(1)} %get-tuple-element.94), channel_id=1, source_target_pairs={{0,2},{2,0},{1,3},{3,1},{4,6},{6,4},{5,7},{7,5},{8,10},{10,8},{9,1... | collective-permute-start | bytes 786440 | tf_op jit(solution)/shard_map/ppermute | solution.py:39
  708.0 20.0 %collective-permute-start.74 = (bf16[256,1024]{1,0:T(8,128)(2,1)}, bf16[256,1024]{1,0:T(8,128)(2,1)}, u32[]{:S(2)}, u32[]{:S(2)}) collective-permute-start(bf16[256,1024]{1,0:T(8,128)(2,1)} %slice.616), channel_id=1, source_target_pairs={{0,1},{1,0},{2,3},{3,2},{4,5},{5,4},{6,7},{7,6},{8,9},{9,8},{10,11... | collective-permute-start | bytes 1572872 | tf_op jit(solution)/shard_map/ppermute | solution.py:35
  739.9 27.5 %collective-permute-start.81 = (bf16[4,128,1152]{2,1,0:T(8,128)(2,1)}, bf16[4,128,1152]{2,1,0:T(8,128)(2,1)}, u32[]{:S(2)}, u32[]{:S(2)}) collective-permute-start(bf16[4,128,1152]{2,1,0:T(8,128)(2,1)} %dynamic-slice_bitcast_fusion.3), channel_id=1, source_target_pairs={{0,4},{4,0},{1,5},{5,1},{2,6},{6,2},{3,7},{7,3},{8,12},{12,8},{9,1... | collective-permute-start | bytes 3538952 | tf_op jit(solution)/shard_map/ppermute | solution.py:43
  756.0 30.5 %collective-permute-start.99 = (bf16[128,1024]{1,0:T(8,128)(2,1)}, bf16[128,1024]{1,0:T(8,128)(2,1)}, u32[]{:S(2)}, u32[]{:S(2)}) collective-permute-start(bf16[128,1024]{1,0:T(8,128)(2,1)} %get-tuple-element.89), channel_id=1, source_target_pairs={{0,0},{8,1},{16,2},{24,3},{4,4},{12,5},{20,6},{28,7},{1,8},{9,9},{... | collective-permute-start | bytes 786440 | tf_op jit(solution)/shard_map/ppermute | solution.py:401
  759.7 30.2 %collective-permute-start.100 = (bf16[128,1024]{1,0:T(8,128)(2,1)}, bf16[128,1024]{1,0:T(8,128)(2,1)}, u32[]{:S(2)}, u32[]{:S(2)}) collective-permute-start(bf16[128,1024]{1,0:T(8,128)(2,1)} %get-tuple-element.90), channel_id=1, source_target_pairs={{4,0},{12,1},{20,2},{28,3},{0,4},{8,5},{16,6},{24,7},{5,8},{13,9},... | collective-permute-start | bytes 786440 | tf_op jit(solution)/shard_map/ppermute | solution.py:401
  778.4 38.2 %collective-permute-start.77 = (bf16[128,1024]{1,0:T(8,128)(2,1)S(1)}, bf16[128,1024]{1,0:T(8,128)(2,1)S(1)}, u32[]{:S(2)}, u32[]{:S(2)}) collective-permute-start(bf16[128,1024]{1,0:T(8,128)(2,1)S(1)} %get-tuple-element.107), channel_id=1, source_target_pairs={{0,0},{8,1},{16,2},{24,3},{4,4},{12,5},{20,6},{28,7},{1,8},{9,9},{... | collective-permute-start | bytes 786440 | tf_op jit(solution)/shard_map/ppermute | solution.py:401
  780.3 43.5 %collective-permute-start.78 = (bf16[128,1024]{1,0:T(8,128)(2,1)S(1)}, bf16[128,1024]{1,0:T(8,128)(2,1)S(1)}, u32[]{:S(2)}, u32[]{:S(2)}) collective-permute-start(bf16[128,1024]{1,0:T(8,128)(2,1)S(1)} %get-tuple-element.108), channel_id=1, source_target_pairs={{4,0},{12,1},{20,2},{28,3},{0,4},{8,5},{16,6},{24,7},{5,8},{13,9},... | collective-permute-start | bytes 786440 | tf_op jit(solution)/shard_map/ppermute | solution.py:401
  783.8 41.2 %collective-permute-start.91 = (bf16[2,2,32,704]{3,2,1,0:T(8,128)(2,1)S(1)}, bf16[2,2,32,704]{3,2,1,0:T(8,128)(2,1)S(1)}, u32[]{:S(2)}, u32[]{:S(2)}) collective-permute-start(bf16[2,2,32,704]{3,2,1,0:T(8,128)(2,1)S(1)} %bitcast.585), channel_id=1, source_target_pairs={{0,1},{1,0},{2,3},{3,2},{4,5},{5,4},{6,7},{7,6},{8,9},{9,8},{10,11... | collective-permute-start | bytes 540680 | tf_op jit(solution)/shard_map/ppermute | solution.py:35
  (181 other events, 1406.2 us)
Sparse Core Ops, SparseCore 0:
  21.9 46.5 all-gather.12
  70.6 36.2 all-gather.14
  109.0 33.8 all-gather.8
  144.3 36.1 all-gather.16
  252.6 31.4 all-gather.10
  457.9 30.7 reduce-scatter.12
  537.9 42.9 reduce-scatter.8
  583.8 21.9 reduce-scatter.16
  646.5 20.1 reduce-scatter.14
  674.8 32.4 reduce-scatter.10
  770.2 51.0 reduce-scatter.6

commit v2 on v1

v2 whole, which is shorter than its diff:
```python
import functools

import jax
import jax.numpy as jnp
from jax import lax
from jax.experimental import pallas as pl
from jax.experimental.pallas import tpu as pltpu
from jax.sharding import Mesh, PartitionSpec as P

HD = 64
LAYERS = 2
epsilon = 1e-05
masked_score = -1e30
bf16 = jnp.bfloat16
f32 = jnp.float32

ALL = ("sz", "sy", "fx", "fc")
SWAP = ((0, 1), (1, 0))
VMEM_LIMIT = 24 * 1024 * 1024


def dot(left, right):
    return jnp.dot(left, right, preferred_element_type=f32)


def dot_rows(left, right):
    return lax.dot_general(left, right, (((0,), (0,)), ((), ())), preferred_element_type=f32)


def dot_cols(left, right):
    return lax.dot_general(left, right, (((1,), (1,)), ((), ())), preferred_element_type=f32)


def swap_core(value):
    return lax.ppermute(value, "fc", SWAP)


def swap_x(value):
    return lax.ppermute(value, "fx", SWAP)


def swap_y(value):
    return lax.ppermute(value, "sy", SWAP)


def pick(array, index, axis=0):
    return lax.dynamic_index_in_dim(array, index, axis, keepdims=False)


def in_order(flag, first, second, axis):
    return jnp.where(
        flag == 0, jnp.stack([first, second], axis), jnp.stack([second, first], axis)
    )


def exchange(pieces):
    fx, fc = lax.axis_index("fx"), lax.axis_index("fc")
    pieces = pieces.reshape((2, 2) + pieces.shape[1:])
    got = swap_x(pick(pieces, 1 - fx))
    both = in_order(fx, pick(pieces, fx), got, 0)
    got = swap_core(pick(both, 1 - fc, 1))
    both = in_order(fc, pick(both, fc, 1), got, 1)
    return both.reshape((4,) + both.shape[2:])


def sum_near(value):
    value = value + swap_x(value)
    value = value + swap_core(value)
    half = value.shape[1] // 2
    got = swap_y(value)
    return value[:, :half] + got[:, half:]


def steps_z():
    size = lax.axis_size("sz")
    return [(d, [(i, i ^ d) for i in range(size)]) for d in range(1, size)]


def gather_near(block):
    return [block] + [lax.ppermute(block, "sz", pairs) for _, pairs in steps_z()]


def scatter_near(blocks):
    total = blocks[0].astype(f32)
    for d, pairs in steps_z():
        total = total + lax.ppermute(blocks[d], "sz", pairs).astype(f32)
    return total


def by_distance(rows):
    at = lax.axis_index("sz")
    return [pick(rows, at ^ d) for d in range(rows.shape[0])]


def scattered(total):
    return lax.psum_scatter(total, "sz", scatter_dimension=0, tiled=False)


def spread(value):
    over = swap_x(value)
    return (value, swap_core(value), over, swap_core(over))


def kernel_call(body, results, scalars, operands, scratch, after, flops):
    count, extra = len(operands), len(after)

    def whole(scalars_ref, *refs):
        body(scalars_ref, *refs[:count], *refs[count + extra :])

    vmem = pl.BlockSpec(memory_space=pltpu.VMEM)
    return pl.pallas_call(
        whole,
        out_shape=[shape_of(*one) for one in results],
        in_specs=[pl.BlockSpec(memory_space=pltpu.SMEM)]
        + [vmem] * count
        + [pl.BlockSpec(memory_space=pl.ANY)] * extra,
        out_specs=[vmem] * len(results),
        scratch_shapes=list(scratch),
        compiler_params=pltpu.CompilerParams(vmem_limit_bytes=VMEM_LIMIT),
        cost_estimate=pl.CostEstimate(
            flops=1, bytes_accessed=1, transcendentals=0
        ),
    )(scalars, *operands, *after)


def shape_of(shape, dtype):
    return jax.ShapeDtypeStruct(shape, dtype)


def block_pairs(scalars, width):
    half, me_y = width // 256, scalars[3]
    for i in range(half):
        yield (i * 128, pl.multiple_of((2 * i + me_y) * 128, 128))
        yield ((half + i) * 128, pl.multiple_of((2 * i + 1 - me_y) * 128, 128))


def norm_kernel(added, scalars, *refs):
    inputs, (gain_ref, sum_ref, out_ref) = refs[:added], refs[added:]
    total = inputs[0][...].astype(f32)
    for ref in inputs[1:]:
        total += (ref[...] if len(ref.shape) == 2 else ref[0]).astype(f32)
    sum_ref[...] = total
    inverse = lax.rsqrt(jnp.mean(total * total, axis=-1, keepdims=True) + epsilon)
    for local, natural in block_pairs(scalars, sum_ref.shape[1]):
        normed = sum_ref[:, pl.ds(natural, 128)] * inverse
        out_ref[:, local : local + 128] = (normed * gain_ref[:, local : local + 128]).astype(bf16)


def norm_back_kernel(scalars, up_ref, d0, d1, d2, z_ref, gain_ref, up_out, low_out, gain_out, work):
    z = z_ref[...]
    inverse = lax.rsqrt(jnp.mean(z * z, axis=-1, keepdims=True) + epsilon)
    for local, natural in block_pairs(scalars, z.shape[1]):
        here = slice(local, local + 128)
        core = d1[:, here] if len(d1.shape) == 2 else d1[0, :, here]
        dy = d0[:, here] + core.astype(f32) + d2[:, here].astype(f32)
        normed = z_ref[:, pl.ds(natural, 128)] * inverse
        gain_out[:, here] = jnp.sum(dy * normed, axis=0, keepdims=True)
        work[:, pl.ds(natural, 128)] = dy * gain_ref[:, here]
    scaled = work[...]
    normed = z * inverse
    mean = jnp.mean(scaled * normed, axis=-1, keepdims=True)
    up = up_ref[...] + inverse * (scaled - normed * mean)
    up_out[...] = up
    low_out[...] = up.astype(bf16)


def add_kernel(scalars, left, right, out_ref):
    out_ref[...] = (left[...].astype(f32) + right[...].astype(f32)).astype(out_ref.dtype)


def add_second_kernel(scalars, left, right, out_ref):
    out_ref[...] = (left[...] + right[1].astype(f32)).astype(out_ref.dtype)


def add_pair_kernel(scalars, left, right, second_left, second_right, out_ref):
    size = left.shape[2]
    out_ref[:, :, :size] = (left[...].astype(f32) + right[...].astype(f32)).astype(bf16)
    out_ref[:, :, size:] = (second_left[...].astype(f32) + second_right[...].astype(f32)).astype(bf16)


def hold_kernel(scalars, value, out_ref):
    out_ref[...] = value[...]


def partner(rows):
    lane = lax.broadcasted_iota(jnp.int32, rows.shape, 1)
    return jnp.where(lane % 64 < 32, pltpu.roll(rows, 96, 1), pltpu.roll(rows, 32, 1))


def block_mask(block, rows, start, end):
    shape = (rows, (block + 1) * rows)
    query = block * rows + lax.broadcasted_iota(jnp.int32, (rows, 1), 0)
    lowest = jnp.where(query < start, 0, jnp.where(query < end, start, end))
    key = lax.broadcasted_iota(jnp.int32, shape, 1)
    return (key <= query) & (key >= lowest)


def softmax_rows(scores, allowed):
    scores = jnp.where(allowed, scores * 0.125, masked_score)
    weights = jnp.exp(scores - jnp.max(scores, axis=-1, keepdims=True))
    return weights * (1.0 / jnp.sum(weights, axis=-1, keepdims=True))


def flat(ref, first, last):
    value = ref[:, first:last, :]
    return value.reshape(-1, value.shape[-1])


def rows_of(refs, columns):
    values = []
    for ref in refs:
        if len(ref.shape) == 3:
            values.append(ref[:, :, :columns].reshape(-1, columns))
        else:
            values.append(ref[:, :columns])
    return values[0] if len(values) == 1 else jnp.concatenate(values, axis=0)


def place(ref, me_y, own, other):
    half = own.shape[0]
    ref[pl.ds(pl.multiple_of(me_y * half, half), half), :] = own
    ref[pl.ds(pl.multiple_of((1 - me_y) * half, half), half), :] = other


def attention_kernel(blend, count, scalars, a0, a1, a2, a3, *refs):
    own, other, refs = refs[:count], refs[count : 2 * count], refs[2 * count :]
    cos_ref, sin_ref, refs = refs[0], refs[1], refs[2:]
    if blend:
        first_ref, q_ref, k_ref, v_ref, o_ref = refs
    else:
        q_ref, k_ref, v_ref, o_ref, first_ref = refs
    me, start, end = scalars[0], scalars[1], scalars[2]
    total, width = q_ref.shape
    rows = total // 4
    here_w, there_w = rows_of(own, 3 * width), rows_of(other, 3 * width)
    half = here_w.shape[0]
    for i, a_ref in enumerate((a0, a1, a2, a3)):
        part = dot(a_ref[:, :half], here_w) + dot(a_ref[:, half:], there_w)
        here = slice(i * rows, (i + 1) * rows)
        there = pl.ds(pl.multiple_of((me ^ i) * rows, rows), rows)
        cosine, sine = cos_ref[here, :], sin_ref[here, :]
        for j in range(width // 128):
            for into, at in ((q_ref, 0), (k_ref, width)):
                piece = part[:, at + j * 128 : at + (j + 1) * 128]
                turned = piece * cosine + partner(piece) * sine
                into[there, j * 128 : (j + 1) * 128] = turned.astype(bf16)
        value = part[:, 2 * width :]
        if blend:
            value = 0.5 * value + 0.5 * first_ref[there, :]
        else:
            first_ref[there, :] = value
        v_ref[there, :] = value.astype(bf16)
    lane = lax.broadcasted_iota(jnp.int32, (rows, 128), 1)
    for b in range(4):
        allowed = block_mask(b, rows, start, end)
        there = pl.ds(pl.multiple_of((me ^ b) * rows, rows), rows)
        for j in range(width // 128):
            columns = slice(j * 128, (j + 1) * 128)
            query = q_ref[b * rows : (b + 1) * rows, columns]
            keys = k_ref[: (b + 1) * rows, columns]
            values = v_ref[: (b + 1) * rows, columns]
            outs = []
            for h in range(2):
                one = jnp.where(lane // 64 == h, query, jnp.zeros_like(query))
                chance = softmax_rows(dot_cols(one, keys), allowed)
                outs.append(dot(chance.astype(bf16), values))
            o_ref[there, columns] = jnp.where(lane < 64, outs[0], outs[1]).astype(bf16)


def out_kernel(scalars, o_ref, out_w, near, far, cores):
    rows = near.shape[0]
    cores[1] = dot(o_ref[3 * rows :, :], out_w[...]).astype(bf16)
    cores[0] = dot(o_ref[rows : 2 * rows, :], out_w[...]).astype(bf16)
    far[...] = dot(o_ref[2 * rows : 3 * rows, :], out_w[...])
    near[...] = dot(o_ref[:rows, :], out_w[...])


def attention_back_kernel(last, count, scalars, y0, y1, y2, y3, *refs):
    own, other, refs = refs[:count], refs[count : 2 * count], refs[2 * count :]
    out_w, cos_ref, sin_ref, q_ref, k_ref, v_ref = refs[:6]
    refs = refs[6:]
    if last:
        carry_ref, near, far, cores, d_ref, dv_ref, dk_sum, dv_sum, up_ref = refs
    else:
        near, far, cores, d_ref, dv_ref, dk_sum, dv_sum, up_ref = refs
    me, start, end = scalars[0], scalars[1], scalars[2]
    total, width = q_ref.shape
    rows = total // 4
    for i, y_ref in enumerate((y0, y1, y2, y3)):
        there = pl.ds(pl.multiple_of((me ^ i) * rows, rows), rows)
        up_ref[there, :] = dot_cols(y_ref[...], out_w[...]).astype(bf16)
    lane = lax.broadcasted_iota(jnp.int32, (rows, 128), 1)
    dk_sum[...] = jnp.zeros_like(dk_sum)
    dv_sum[...] = jnp.zeros_like(dv_sum)
    for b in range(4):
        allowed = block_mask(b, rows, start, end)
        there = pl.ds(pl.multiple_of((me ^ b) * rows, rows), rows)
        upto = slice(0, (b + 1) * rows)
        cosine, sine = cos_ref[there, :], sin_ref[there, :]
        for j in range(width // 128):
            columns = slice(j * 128, (j + 1) * 128)
            query = q_ref[b * rows : (b + 1) * rows, columns]
            keys, values = k_ref[upto, columns], v_ref[upto, columns]
            up = up_ref[b * rows : (b + 1) * rows, columns]
            dq, dk, dv = [], [], []
            for h in range(2):
                mine = lane // 64 == h
                one = jnp.where(mine, query, jnp.zeros_like(query))
                one_up = jnp.where(mine, up, jnp.zeros_like(up))
                chance = softmax_rows(dot_cols(one, keys), allowed)
                back = dot_cols(one_up, values)
                delta = jnp.sum(chance * back, axis=-1, keepdims=True)
                score = (chance * (back - delta) * 0.125).astype(bf16)
                dq.append(dot(score, keys))
                dk.append(dot_rows(score, one))
                dv.append(dot_rows(chance.astype(bf16), one_up))
            dk_sum[upto, columns] += dk[0] + dk[1]
            dv_sum[upto, columns] += dv[0] + dv[1]
            dq = jnp.where(lane < 64, dq[0], dq[1])
            d_ref[there, columns] = (dq * cosine - partner(dq) * sine).astype(bf16)
    for b in range(4):
        there = pl.ds(pl.multiple_of((me ^ b) * rows, rows), rows)
        here = slice(b * rows, (b + 1) * rows)
        cosine, sine = cos_ref[there, :], sin_ref[there, :]
        for j in range(width // 128):
            dk = dk_sum[here, j * 128 : (j + 1) * 128]
            dk = dk * cosine - partner(dk) * sine
            d_ref[there, width + j * 128 : width + (j + 1) * 128] = dk.astype(bf16)
        dv = dv_sum[here, :]
        dv = dv + carry_ref[here, :] if last else 0.5 * dv
        dv_ref[here, :] = dv
        d_ref[there, 2 * width : 3 * width] = dv.astype(bf16)
    here_w, there_w = rows_of(own, 3 * width), rows_of(other, 3 * width)
    half = here_w.shape[0]
    for at, weight in ((slice(0, half), here_w), (slice(half, 2 * half), there_w)):
        for i in range(4):
            total_d = dot_cols(d_ref[i * rows : (i + 1) * rows, :], weight)
            if i % 2:
                cores[i // 2, :, at] = total_d.astype(bf16)
            else:
                (far if i else near)[:, at] = total_d


def mlp_halves(ref):
    size = ref.shape[2] // 2
    blocks = range(ref.shape[0])
    return [
        jnp.concatenate([ref[z, :, at : at + size] for z in blocks], axis=1) for at in (0, size)
    ]


def mlp_kernel(scalars, m0, m1, own, other, down_own, down_other, p0, p1, g_ref, u_ref, z_ref, down):
    rows = m0.shape[0]
    place(down, scalars[3], down_own[...], down_other[...])
    gate_own, up_own = mlp_halves(own)
    gate_other, up_other = mlp_halves(other)
    half = gate_own.shape[1]
    for i, (m_ref, p_ref) in enumerate(((m0, p0), (m1, p1))):
        here = slice(i * rows, (i + 1) * rows)
        left, right = m_ref[:, :half], m_ref[:, half:]
        gate = dot_cols(left, gate_own) + dot_cols(right, gate_other)
        up = dot_cols(left, up_own) + dot_cols(right, up_other)
        active = (jax.nn.silu(gate) * up).astype(bf16)
        g_ref[here, :] = gate.astype(bf16)
        u_ref[here, :] = up.astype(bf16)
        z_ref[here, :] = active
        p_ref[...] = dot(active, down[...]).astype(p_ref.dtype)


def mlp_back_kernel(scalars, y0, y1, g_ref, u_ref, own, other, down_own, down_other, p0, p1, dg_ref, du_ref, down):
    rows = y0.shape[0]
    place(down, scalars[3], down_own[...], down_other[...])
    gate_own, up_own = mlp_halves(own)
    gate_other, up_other = mlp_halves(other)
    half = gate_own.shape[1]
    for i, (y_ref, p_ref) in enumerate(((y0, p0), (y1, p1))):
        here = slice(i * rows, (i + 1) * rows)
        back = dot_cols(y_ref[...], down[...])
        gate, up = g_ref[here, :].astype(f32), u_ref[here, :].astype(f32)
        sigmoid = jax.nn.sigmoid(gate)
        dg = (back * up * sigmoid * (1.0 + gate * (1.0 - sigmoid))).astype(bf16)
        du = (back * (gate * sigmoid)).astype(bf16)
        dg_ref[here, :] = dg
        du_ref[here, :] = du
        p_ref[:, :half] = (dot(dg, gate_own) + dot(du, up_own)).astype(p_ref.dtype)
        p_ref[:, half:] = (dot(dg, gate_other) + dot(du, up_other)).astype(p_ref.dtype)


def gate_grad_kernel(scalars, m0, m1, m2, m3, near, far, keep, send):
    rows = m0.shape[0]
    blocks, size = keep.shape[0], keep.shape[2]
    half = blocks * size
    for into, columns in ((send, slice(half, 2 * half)), (keep, slice(0, half))):
        total = dot_rows(near[:rows, :], m0[:, columns])
        total += dot_rows(near[rows:, :], m1[:, columns])
        total += dot_rows(far[:rows, :], m2[:, columns])
        total += dot_rows(far[rows:, :], m3[:, columns])
        for z in range(blocks):
            into[z] = total[:, z * size : (z + 1) * size].astype(bf16)


def rows_grad_kernel(scalars, left_near, left_far, y0, y1, y2, y3, keep, send, work):
    rows = y0.shape[0]
    half = keep.shape[0]
    work[...] = dot_rows(left_near[:rows, :], y0[...]) + dot_rows(left_near[rows:, :], y1[...])
    work[...] += dot_rows(left_far[:rows, :], y2[...]) + dot_rows(left_far[rows:, :], y3[...])
    me_y = scalars[3]
    keep[...] = work[pl.ds(pl.multiple_of(me_y * half, half), half), :].astype(bf16)
    send[...] = work[pl.ds(pl.multiple_of((1 - me_y) * half, half), half), :].astype(bf16)


def qkv_grad_kernel(scalars, a0, a1, a2, a3, d_ref, keep, send):
    rows = a0.shape[0]
    blocks, size = keep.shape[0], keep.shape[1]
    half = blocks * size
    for into, columns in ((send, slice(half, 2 * half)), (keep, slice(0, half))):
        total = dot_rows(a0[:, columns], d_ref[:rows, :])
        for i, a_ref in ((1, a1), (2, a2), (3, a3)):
            total += dot_rows(a_ref[:, columns], d_ref[i * rows : (i + 1) * rows, :])
        into[...] = total.astype(bf16).reshape(blocks, size, -1)


def turn(rows, cosine, sine):
    total, width = rows.shape
    halves = rows.reshape(total, width // HD, 2, HD // 2)
    cosine = cosine[:, :HD].reshape(total, 1, 2, HD // 2)
    sine = sine[:, :HD].reshape(total, 1, 2, HD // 2)
    return (halves * cosine + halves[:, :, ::-1] * sine).reshape(total, width)


class Group:
    def __init__(self, local, model, width, parts, bounds):
        self.local, self.model, self.width, self.parts = local, model, width, parts
        self.total = total = 4 * local
        self.me_y = lax.axis_index("sy")
        self.blocks = lax.axis_size("sz")
        me = lax.axis_index(("fx", "fc"))
        self.part = lax.axis_index(("sz", "sy")) % parts
        order = (me ^ jnp.arange(4, dtype=jnp.int32)) * local
        self.inner = (order[:, None] + jnp.arange(local, dtype=jnp.int32)[None, :]).reshape(total)
        self.start, self.end = bounds[0], bounds[1]
        self.index = index = self.part * total + self.inner
        self.me_z = lax.axis_index("sz")
        self.scalars = jnp.stack([me, self.start, self.end, self.me_y, self.me_z]).astype(jnp.int32)
        base = jnp.where(index < self.start, 0, jnp.where(index < self.end, self.start, self.end))
        frequency = 10000.0 ** (-jnp.arange(HD // 2, dtype=f32) * 2.0 / HD)
        angles = (index - base).astype(f32)[:, None] * frequency[None, :]
        cosine, sine = jnp.cos(angles), jnp.sin(angles)
        self.cosine = jnp.concatenate([cosine] * 4, axis=1)
        self.sine = jnp.concatenate([-sine, sine] * 2, axis=1)
        self.block = model // (2 * self.blocks)
        self.latest, self.needed = None, []

    def call(self, body, shapes, operands, scratch=(), micros=1):
        after = self.needed + ([] if self.latest is None else [self.latest])
        self.needed = []
        flops = int(micros * 1e9)
        got = kernel_call(body, shapes, self.scalars, operands, scratch, after, flops)
        self.latest = got[-1]
        return got

    def add(self, left, right):
        return self.call(add_kernel, [(left.shape, bf16)], [left, right])[0]

    def need(self, *values):
        self.needed += values

    def add_pair(self, first, second):
        shape = (*first[0].shape[:2], 2 * first[0].shape[2])
        if self.block % 128:
            sums = [self.add(*one) for one in (first, second)]
            return jnp.concatenate(sums, axis=2)
        return self.call(add_pair_kernel, [(shape, bf16)], [*first, *second])[0]

    def hold(self, value):
        return self.call(hold_kernel, [(value.shape, value.dtype)], [value])[0]

    def reduce_pieces(self, pieces):
        if len(pieces) == 3:
            got = swap_core(pieces[2])
            out = self.call(
                add_second_kernel,
                [(pieces[1].shape, bf16)],
                [pieces[1], got],
            )[0]
            return (pieces[0], got, swap_x(out))
        got = swap_core(pieces[3])
        out = self.call(
            add_kernel, [(got.shape, bf16)], [pieces[2], got]
        )[0]
        return (pieces[0], swap_core(pieces[1]), swap_x(out))

    def sum_y(self, keep, send):
        return self.add(keep, send)

    def valid(self):
        return (self.index[: self.local] < self.end).astype(f32)[:, None]

    def to_local(self, rows):
        cut = rows.reshape(rows.shape[0], self.blocks, 2, self.block)
        pair = in_order(self.me_y, cut[:, :, 0], cut[:, :, 1], 1)
        return pair.reshape(rows.shape[0], self.model)

    def to_natural(self, rows):
        cut = rows.reshape(rows.shape[0], 2, self.blocks, self.block)
        cut = in_order(self.me_y, cut[:, 0], cut[:, 1], 2)
        return cut.reshape(rows.shape[0], self.model)

    def plain_sum(self, pieces):
        return sum((one if one.ndim == 2 else one[0]).astype(f32) for one in pieces)

    def norm(self, pieces, gain):
        if self.block % 128 == 0:
            shape = (self.local, self.model)
            return self.call(
                functools.partial(norm_kernel, len(pieces)),
                [(shape, f32), (shape, bf16)],
                [*pieces, gain],
            )
        total = self.plain_sum(pieces)
        inverse = lax.rsqrt(jnp.mean(total * total, axis=-1, keepdims=True) + epsilon)
        return (total, (self.to_local(total * inverse) * gain).astype(bf16))

    def norm_back(self, up, pieces, z, gain):
        if self.block % 128 == 0:
            shape = (self.local, self.model)
            return self.call(
                norm_back_kernel,
                [(shape, f32), (shape, bf16), ((1, self.model), f32)],
                [up, *pieces, z, gain],
                [pltpu.VMEM(shape, f32)],
            )
        dy = self.plain_sum(pieces)
        inverse = lax.rsqrt(jnp.mean(z * z, axis=-1, keepdims=True) + epsilon)
        normed = z * inverse
        gain_grad = jnp.sum(dy * self.to_local(normed), axis=0, keepdims=True)
        scaled = self.to_natural(dy * gain)
        mean = jnp.mean(scaled * normed, axis=-1, keepdims=True)
        up = up + inverse * (scaled - normed * mean)
        return (up, up.astype(bf16), gain_grad)

    def pieces(self):
        shape = (self.local, self.model)
        return [(shape, f32), (shape, f32), ((2, *shape), bf16)]

    def cut(self, rows):
        cut = rows.reshape(4, self.local, -1)
        return (cut[0], cut[2], cut[1::2].astype(bf16))

    def attend(self, a, weights, first):
        total, width = self.total, self.width
        tables = [self.cosine, self.sine]
        own, other, out_w = weights
        if self.parts == 1:
            results = [((total, width), bf16)] * 4
            operands = [*a, *own, *other, *tables]
            if first is None:
                results += [((total, width), f32)]
            else:
                operands += [first]
            got = self.call(
                functools.partial(attention_kernel, first is not None, len(own)),
                results,
                operands,
                micros=12,
            )
            partial = self.call(out_kernel, self.pieces(), [got[3], out_w], micros=3)
            return (partial, got[:3], got[3], got[4] if first is None else first)
        own, other = self.plain(own), self.plain(other)
        rows = jnp.concatenate(a)
        part = dot(rows[:, : own.shape[0]], own) + dot(rows[:, own.shape[0] :], other)
        query = turn(part[:, :width], *tables).astype(bf16)
        key = turn(part[:, width : 2 * width], *tables).astype(bf16)
        value = part[:, 2 * width :]
        if first is None:
            first = value
        else:
            value = 0.5 * value + 0.5 * first
        value = value.astype(bf16)

        def one(items):
            q, k, v = items
            return dot(softmax_rows(dot_cols(q, k), self.allowed()).astype(bf16), v)

        packed = (self.heads(query), self.heads(self.slot(key)), self.heads(self.slot(value)))
        out = self.rows(lax.map(one, packed)).astype(bf16)
        return (self.cut(dot(out, out_w)), (query, key, value), out, first)

    def attend_back(self, y, weights, saved, carry, last):
        total, width = self.total, self.width
        own, other, out_w = weights
        if self.parts == 1:
            operands = [*y, *own, *other, out_w, self.cosine, self.sine, *saved]
            if last:
                operands += [carry]
            got = self.call(
                functools.partial(attention_back_kernel, last, len(own)),
                self.pieces() + [((total, 3 * width), bf16), ((total, width), f32)],
                operands,
                [pltpu.VMEM((total, width), f32)] * 2 + [pltpu.VMEM((total, width), bf16)],
                micros=20,
            )
            return (got[:3], got[3], got[4])
        own, other = self.plain(own), self.plain(other)
        query, key, value = saved
        up = dot_cols(jnp.concatenate(y), out_w).astype(bf16)

        def one(items):
            q, k, v, u = items
            chance = softmax_rows(dot_cols(q, k), self.allowed())
            back = dot_cols(u, v)
            delta = jnp.sum(chance * back, axis=-1, keepdims=True)
            score = (chance * (back - delta) * 0.125).astype(bf16)
            return (dot(score, k), dot_rows(score, q), dot_rows(chance.astype(bf16), u))

        packed = (query, self.slot(key), self.slot(value), up)
        dq, dk, dv = lax.map(one, tuple(self.heads(rows) for rows in packed))
        dk, dv = self.collect(self.rows(dk)), self.collect(self.rows(dv))
        dv = dv + carry if last else 0.5 * dv
        back_turn = functools.partial(turn, cosine=self.cosine, sine=-self.sine)
        joined = jnp.concatenate([back_turn(self.rows(dq)), back_turn(dk), dv], axis=1)
        joined = joined.astype(bf16)
        sums = jnp.concatenate([dot_cols(joined, own), dot_cols(joined, other)], axis=1)
        return (self.cut(sums), joined, dv)

    def plain(self, blocks):
        wide = 3 * self.width
        return jnp.concatenate([block[..., :wide].reshape(-1, wide) for block in blocks])

    def rotate_parts(self, value, shift):
        if shift % self.parts == 0:
            return value
        pairs = []
        for t in range(lax.axis_size(("sz", "sy"))):
            head = t - t % self.parts
            pairs.append((head + (t + shift) % self.parts, t))
        return lax.ppermute(value, ("sz", "sy"), pairs)

    def slot(self, value):
        return jnp.concatenate([self.rotate_parts(value, r) for r in range(self.parts)])

    def heads(self, rows):
        return rows.reshape(rows.shape[0], -1, HD).transpose(1, 0, 2)

    def rows(self, heads):
        return heads.transpose(1, 0, 2).reshape(heads.shape[1], -1)

    def allowed(self):
        key = jnp.concatenate(
            [(self.part + r) % self.parts * self.total + self.inner for r in range(self.parts)]
        )
        query = self.index[:, None]
        lowest = jnp.where(
            query < self.start, 0, jnp.where(query < self.end, self.start, self.end)
        )
        return (key[None, :] <= query) & (key[None, :] >= lowest)

    def collect(self, slot_rows):
        pieces = slot_rows.reshape(self.parts, self.total, -1)
        result = pieces[0]
        for r in range(1, self.parts):
            result = result + self.rotate_parts(pieces[r].astype(bf16), -r).astype(f32)
        return result

    def mlp(self, m, weights):
        hidden = weights[0].shape[1]
        rows = 2 * self.local
        shape = (self.local, self.model)
        scratch = [pltpu.VMEM((hidden, self.model), bf16)]
        results = [(shape, f32), (shape, bf16)] + [((rows, hidden), bf16)] * 3
        return [
            self.call(mlp_kernel, results, [*pair, *weights], scratch, 6)
            for pair in (m[:2], m[2:])
        ]

    def mlp_back(self, y, saved, weights):
        hidden = weights[0].shape[1]
        rows = 2 * self.local
        shape = (self.local, self.model)
        scratch = [pltpu.VMEM((hidden, self.model), bf16)]
        results = [(shape, f32), (shape, bf16)] + [((rows, hidden), bf16)] * 2
        return [
            self.call(mlp_back_kernel, results, [*pair, *kept, *weights], scratch, 6)
            for pair, kept in ((y[:2], saved[0]), (y[2:], saved[1]))
        ]

    def gate_grads(self, m, near, far):
        hidden = near.shape[-1]
        blocks = self.blocks if self.block % 128 == 0 else 1
        shape = ((blocks, hidden, self.model // 2 // blocks), bf16)
        keep, send = self.call(
            gate_grad_kernel,
            [shape] * 2,
            [*m, near, far],
        )
        if blocks != self.blocks:
            keep, send = [
                rows.reshape(hidden, self.blocks, self.block).transpose(1, 0, 2)
                for rows in (keep, send)
            ]
        return (keep, send)

    def mlp_layout(self, rows):
        if self.block % 128 == 0:
            return rows
        hidden = rows.shape[1]
        cut = rows.reshape(self.blocks, hidden, 2, self.block).transpose(1, 2, 0, 3)
        return cut.reshape(1, hidden, self.model)

    def rows_grads(self, near, far, y):
        size = near.shape[-1]
        return self.call(
            rows_grad_kernel,
            [((size // 2, self.model), bf16)] * 2,
            [near, far, *y],
            [pltpu.VMEM((size, self.model), f32)],
        )

    def qkv_grads(self, a, joined):
        shape = ((self.blocks, self.block, 3 * self.width), bf16)
        return self.call(qkv_grad_kernel, [shape] * 2, [*a, joined], micros=4)


def routes(seq_size, group_size, slots_here):
    slots = slots_here * group_size
    parts = seq_size // slots
    result = []
    for r in range(slots_here):
        pairs = []
        for s in range(seq_size):
            for f in range(group_size):
                slot = slots_here * f + (s + r) % slots_here
                t = slot * parts + s // slots
                k = s % slots // slots_here
                pairs.append((s * group_size + f, t * group_size + k))
        result.append(pairs)
    return result


def shards(tokens, doc_bounds, w_qkv, w_out, w_gate, w_up, w_down, norm_attn, norm_mlp, out_grad):
    slots_here, block, model = tokens.shape
    seq_size = lax.axis_size(("sz", "sy"))
    group_size = lax.axis_size(("fx", "fc"))
    sz_size = seq_size // 2
    seq_at = lax.axis_index(("sz", "sy"))
    me = lax.axis_index(("fx", "fc"))
    parts = seq_size // (slots_here * group_size)
    local = slots_here * block
    width = model // group_size
    in_rows = w_qkv.shape[1]
    group_rows = in_rows * group_size
    hidden_rows = w_down.shape[1]
    hidden_here = hidden_rows * seq_size
    paths = routes(seq_size, group_size, slots_here)
    backs = [[(target, source) for source, target in pairs] for pairs in paths]

    def to_group(array):
        got = [
            lax.ppermute(pick(array, (seq_at + r) % 2), ALL, paths[r]) for r in range(slots_here)
        ]
        return in_order(seq_at // parts % 2, got[0], got[1], 0).reshape(local, model)

    def from_group(rows):
        rows = rows.astype(bf16).reshape(slots_here, block, model)
        at = seq_at // parts % 2
        got = [lax.ppermute(pick(rows, (at + r) % 2), ALL, backs[r]) for r in range(slots_here)]
        return in_order(seq_at % 2, got[0], got[1], 0).astype(f32)

    def gathered(own):
        return lax.all_gather(own, "sz", axis=0, tiled=False)

    def qkv_pieces(layer):
        pieces = w_qkv[layer].reshape(in_rows, 3, group_size, width).transpose(2, 0, 1, 3)
        return pieces.reshape(group_size, in_rows, 3 * width)

    def attention_weights(layer, mine):
        outs = w_out[layer].reshape(in_rows, group_size, width).transpose(1, 0, 2)
        own = gathered(jnp.concatenate([mine, outs.reshape(group_rows, width)], axis=1))
        other = swap_y(own[:, :, : 3 * width])
        outs = own[:, :, 3 * width :].reshape(group_size, -1, group_size, in_rows, width)
        outs = exchange(outs.transpose(0, 1, 3, 2, 4).reshape(group_size, -1, in_rows, model))
        outs = outs.transpose(1, 0, 2, 3)
        outs = in_order(group.me_y, outs, swap_y(outs), 1).reshape(width, model)
        return ([own], [other], outs)

    def mlp_weights(layer):
        def cut(weight):
            weight = weight[layer].reshape(in_rows, sz_size, 2, group_size, hidden_rows)
            return weight.transpose(3, 0, 2, 1, 4).reshape(group_size, in_rows, hidden_here)

        mine = exchange(group.hold(jnp.stack([cut(w_gate), cut(w_up)], axis=1)))
        mine = mine.transpose(1, 0, 2, 3).reshape(2 * group_rows, hidden_here).T
        if layer > 0:
            group.need(mine)
        own = gathered(mine)
        return (group.mlp_layout(own), group.mlp_layout(swap_y(own)))

    bounds = lax.ppermute(pick(doc_bounds, seq_at % 2), ALL, paths[0])
    group = Group(local, model, width, parts, bounds)
    gains = jnp.stack([norm_attn[0], norm_mlp[0], norm_attn[1], norm_mlp[1]])
    sums = (to_group(tokens),)
    first_qkv = exchange(qkv_pieces(0)).reshape(group_rows, 3 * width)
    gains = jnp.stack(by_distance(jnp.stack(gather_near(gains.astype(f32)))))
    gains = gains.transpose(1, 0, 2).reshape(4, sz_size, 1, 1, in_rows)
    gains = in_order(lax.axis_index("fx"), gains, swap_x(gains), 2)[:, :, :, 0]
    gains = in_order(lax.axis_index("fc"), gains, swap_core(gains), 3)
    gains = gains.reshape(4, sz_size * group_rows)
    gains = jnp.concatenate([gains, swap_y(gains)], axis=1)
    gains = [gains[i : i + 1] for i in range(4)]

    attention = [attention_weights(0, first_qkv)]
    mlps, downs = [], None
    upstream = to_group(out_grad)

    saved = []
    first = None
    for layer in range(LAYERS):
        entry, a = group.norm(sums, gains[2 * layer])
        if layer == 0:
            gates = [mlp_weights(0)]
            downs = gathered(jnp.concatenate([w_down[0], w_down[1]]))
            cut = slice(0, hidden_rows), slice(hidden_rows, 2 * hidden_rows)
            downs = [downs[:, at].reshape(-1, model) for at in cut]
            downs = [(own, swap_y(own)) for own in downs]
            next_qkv = exchange(group.hold(qkv_pieces(1))).reshape(group_rows, 3 * width)
        else:
            group.need(gates[1][0], downs[1][1])
        a = spread(a)
        partial, kept, out, first = group.attend(a, attention[layer], first)
        if layer == 0:
            group.need(next_qkv)
            attention.append(attention_weights(1, next_qkv))
        else:
            group.need(gates[1][1])
        middle, m = group.norm((entry, *group.reduce_pieces(partial)), gains[2 * layer + 1])
        m = spread(m)
        if layer == 0:
            gates.append(mlp_weights(1))
        mlps.append(gates[layer] + downs[layer])
        near, far = group.mlp(m, mlps[layer])
        if layer == 0:
            group.need(attention[1][1][0], attention[1][2])
        sums = (middle, *group.reduce_pieces((*near[:2], *far[:2])))
        saved.append((entry, a, kept, out, middle, m, near[2:], far[2:]))
    valid = group.valid()
    hidden_out = from_group(group.plain_sum(sums) * valid)

    upstream = upstream.astype(f32) * valid
    low = upstream.astype(bf16)
    carry = None
    grads = [None] * LAYERS
    gain_grads = [None] * (2 * LAYERS)

    def out_rows(outs):
        if parts == 1:
            rows = group.add(outs[0], outs[1])
        else:
            rows = group.add(*outs)
        rows = rows.reshape(-1, group_size, in_rows, model)
        return exchange(rows.transpose(1, 0, 2, 3)).reshape(sz_size, in_rows, model)

    def swap_outs(keep, send):
        if parts == 1:
            return (keep, swap_y(send))
        both = in_order(group.me_y, keep, send, 0).reshape(-1, 2, group_rows, model)
        return (pick(both, group.me_y, 1), swap_y(pick(both, 1 - group.me_y, 1)))

    def hand_out(layer, pair, down, qkv, rows):
        pair = pair.T.reshape(2, group_size, in_rows, hidden_here).transpose(1, 0, 2, 3)
        pair = exchange(pair)
        pair = pair.reshape(group_size, 2, in_rows, 2, sz_size, hidden_rows)
        pair = pair.transpose(1, 2, 4, 3, 0, 5).reshape(2, in_rows, -1)
        qkv = exchange(qkv.reshape(group_size, in_rows, 3 * width))
        qkv = qkv.reshape(group_size, in_rows, 3, width)
        qkv = qkv.transpose(1, 2, 0, 3).reshape(in_rows, 3 * model)
        grads[layer] = (qkv, rows, pair[0], pair[1], down)

    half = 2 * local
    waiting = None
    for layer in reversed(range(LAYERS)):
        last = layer == 0
        entry, a, kept, out, middle, m, near, far = saved[layer]
        y = spread(low)
        if waiting is not None:
            pair, qkv, down, outs = waiting
            qkv = scattered(group.add(*qkv))
        near_back, far_back = group.mlp_back(y, (near[:2], far[:2]), mlps[layer])
        partial = group.reduce_pieces((*near_back[:2], *far_back[:2]))
        keep, send = group.gate_grads(m, near_back[2], far_back[2])
        gate = (keep, swap_y(send))
        if waiting is not None:
            down = group.add(*down).reshape(sz_size, hidden_rows, model)
            rows = scattered(jnp.concatenate([down, out_rows(outs)], axis=1))
        down_keep, down_send = group.rows_grads(near[2], far[2], y)
        upstream, low, gain_grads[2 * layer + 1] = group.norm_back(
            upstream, partial, middle, gains[2 * layer + 1]
        )
        y2 = spread(low)
        keep, send = group.gate_grads(m, near_back[3], far_back[3])
        up = (keep, swap_y(send))
        group.need(gate[1])
        partial, joined, value_grad = group.attend_back(y2, attention[layer], kept, carry, last)
        if not last:
            carry = value_grad if carry is None else carry + value_grad
        partial = group.reduce_pieces(partial)
        keep, send = group.qkv_grads(a, joined)
        qkv_sums = (keep, swap_y(send))
        down_sums = (down_keep, swap_y(down_send))
        if waiting is not None:
            done = [pair, qkv, rows]
        pair = scattered(group.add_pair(gate, up))
        outs = swap_outs(*group.rows_grads(out[:half], out[half:], y2))
        upstream, low, gain_grads[2 * layer] = group.norm_back(
            upstream, partial, entry, gains[2 * layer]
        )
        waiting = (pair, qkv_sums, down_sums, outs)
    pair, qkv, down, outs = waiting
    qkv = scatter_near(by_distance(group.add(*qkv))).astype(bf16)
    down = group.add(*down).reshape(sz_size, hidden_rows, model)
    rows = out_rows(outs)
    extra = sum_near(jnp.concatenate(gain_grads)).reshape(2 * LAYERS, sz_size, group_rows)
    extra = extra.astype(bf16).transpose(1, 0, 2)
    extra = jnp.pad(extra, ((0, 0), (0, 8 - 2 * LAYERS), (0, model - group_rows)))
    rows = scattered(jnp.concatenate([down, rows, extra], axis=1))
    down, rows = rows[:hidden_rows], rows[hidden_rows:]
    gain_sums = rows[in_rows : in_rows + 2 * LAYERS].astype(f32)
    gain_sums = lax.dynamic_slice(gain_sums, (0, me * in_rows), (2 * LAYERS, in_rows))
    pair_1, qkv_1, rows_1 = [group.hold(one) for one in done]
    value_grad = group.hold(value_grad)
    hand_out(1, pair_1, rows_1[:hidden_rows], qkv_1, rows_1[hidden_rows:])
    hand_out(0, pair, down, qkv, rows[:in_rows])
    pieces = value_grad.astype(bf16).reshape(group_size, local, width)
    if parts != 1:
        order = me ^ jnp.arange(group_size, dtype=jnp.int32)
        pieces = jnp.take(pieces, order, axis=0)
    first_grad = exchange(pieces).transpose(1, 0, 2).reshape(local, model)
    stacked = [
        jnp.stack([grads[layer][member].astype(f32) for layer in range(LAYERS)])
        for member in range(5)
    ]
    return (
        hidden_out,
        from_group(upstream),
        *stacked,
        gain_sums[0::2],
        gain_sums[1::2],
        from_group(first_grad),
    )


def solution(mesh):
    seq, fsdp = mesh.shape["seq"], mesh.shape["fsdp"]
    inner = Mesh(mesh.devices.reshape(seq // 2, 2, fsdp // 2, 2), ALL)
    rows = P(("fx", "fc"), ("sz", "sy"), None)
    weight, gain = P(None, ALL, None), P(None, ALL)
    in_specs = (rows, P(("fx", "fc"), None)) + (weight,) * 5 + (gain,) * 2 + (rows,)
    out_specs = (rows, rows) + (weight,) * 5 + (gain,) * 2 + (rows,)
    return jax.shard_map(
        shards, mesh=inner, in_specs=in_specs, out_specs=out_specs, check_vma=False
    )
```

time: 861 us -> 765 us (0.89)
  Pallas kernels: 53.7 us -> 164 us
  matrix products: 96.4 us -> 0 us
  other arithmetic: 108 us -> 31.2 us
  local copies, waits for them, and re-layouts: 165 us -> 102 us
  starting transfers between devices: 112 us -> 150 us
    pallas_call x4 -> x55, Pallas kernels: 53.7 us -> 164 us  [kernel_call(): pl.pallas_call(whole, out_shape=[shape_of(*one) for one in results], in_s...]
    dot_general x60 -> x0, matrix products: 96.4 us -> none  [the longest x20 39.5 us: dot_rows(): lax.dot_general(left, right, (((0,), (0,)), ((), ())), preferred_element_...]
    convert_element_type x25 -> x5, other arithmetic: 37.5 us -> 2.86 us  [the longest x1 1.4 us: shards(): low = upstream.astype(bf16)]
    select_n x16 -> x8, local copies, waits for them, and re-layouts: 35.1 us -> 2.79 us  [in_order(): jnp.where(flag == 0, jnp.stack([first, second], axis), jnp.stack([second,...]
    all_gather x5, waiting for transfers between devices: 45.5 us -> 14.6 us  [gathered(): return lax.all_gather(own, 'sz', axis=0, tiled=False)]
    unnamed x282 -> x326, local copies, waits for them, and re-layouts: 30.1 us -> 57.2 us
    ppermute x29 -> x31, waiting for transfers between devices: 99.5 us -> 124 us  [swap_x(): return lax.ppermute(value, 'fx', SWAP)]
    ppermute x45 -> x43, starting transfers between devices: 44.8 us -> 67.7 us  [swap_core(): return lax.ppermute(value, 'fc', SWAP)]
  transfers between devices with their start and end apart: 112 -> 121, of which waited for: 35 -> 53; matrix products, arithmetic and copies ran while one was open for 41% -> 9% of each run, Pallas kernels for 6% -> 18%
where the time goes in v2:
time: 765 us; the launch traced here: 757 us
  waiting for transfers between devices  294 us (38%)
  Pallas kernels  164 us (21%)
  starting transfers between devices  150 us (20%)
  local copies, waits for them, and re-layouts  102 us (13%)
  other arithmetic  31.2 us (4%)
  between operations  17.1 us (2%)
    pallas_call x55, Pallas kernels, kernel_call(): pl.pallas_call(whole, out_shape=[shape_of(*one) for one in results], in_s...  164 us
    ppermute x31, waiting for transfers between devices, swap_x(): return lax.ppermute(value, 'fx', SWAP)  124 us
    ppermute x43, starting transfers between devices, swap_core(): return lax.ppermute(value, 'fc', SWAP)  67.7 us
    ppermute x20, waiting for transfers between devices, swap_y(): return lax.ppermute(value, 'sy', SWAP)  66 us
    unnamed x326, local copies, waits for them, and re-layouts  57.2 us
    ppermute x6, waiting for transfers between devices, from_group(): lax.ppermute(pick(rows, (at + r) % 2), ALL, backs[r])  48.2 us
    ppermute x20, starting transfers between devices, swap_y(): return lax.ppermute(value, 'sy', SWAP)  19.4 us
    ppermute x6, starting transfers between devices, from_group(): lax.ppermute(pick(rows, (at + r) % 2), ALL, backs[r])  18.8 us
  transfers between devices with their start and end apart: 121, of which 53 were waited for; matrix products, arithmetic and copies ran while one was open for 9% of the time, Pallas kernels for 18%

profile of v2, /device:TPU:11, one launch (start us, length us, event | category | flops | bytes accessed | tf_op | source)
XLA Modules:
  0.0 757.4 jit_solution(8849662285120342474)
XLA Ops:
  11.8 5.1 collective-permute-start.1
  27.4 4.7 collective-permute-start.2
  33.7 4.2 collective-permute-done.12
  45.5 5.5 collective-permute-done.23
  57.2 10.3 %all-gather.11.cloned.1.call-done = bf16[512,1024]{1,0:T(8,128)(2,1)} async-done(((bf16[128,1024]{1,0:T(8,128)(2,1)}), bf16[512,1024]{1,0:T(8,128)(2,1)}) %all-gather.11.cloned.1.call-update) | async-done | bytes 1048592 | tf_op jit(solution)/shard_map/all_gather | solution.py:770
  80.1 5.5 collective-permute-done.10.refs_2_
  91.7 6.3 collective-permute-done.17
  98.1 10.3 %shard_map.180 = (bf16[1024,256]{1,0:T(8,128)(2,1)S(1)}, bf16[1024,256]{1,0:T(8,128)(2,1)S(1)}, bf16[1024,256]{1,0:T(8,128)(2,1)S(1)}, bf16[1024,256]{1,0:T(8,128)(2,1)S(1)}, f32[1024,256]{1,0:T(8,128)S(1)}) custom-call(s32[5]{0:T(128)S(1)} %pad_add_fusion.scalars_ref, bf16[256,1024]{1,0:T(8,128)(2,1)S(1)} %get-tuple-element.111.refs_1_.refs_0_, ...), custom_call_target="tpu_custom_call" | custom-call | flops 1 | bytes 1 | tf_op jit(solution)/shard_map/pallas_call | solution.py:111
  116.5 4.2 collective-permute-done.19
  133.1 6.8 collective-permute-done.21.refs_3_
  152.3 10.1 %collective-permute-done.27 = bf16[2,2,32,704]{3,2,1,0:T(8,128)(2,1)S(1)} collective-permute-done((bf16[2,2,32,704]{3,2,1,0:T(8,128)(2,1)S(1)}, bf16[2,2,32,704]{3,2,1,0:T(8,128)(2,1)S(1)}, u32[]{:S(2)}, u32[]{:S(2)}) %collective-permute-start.27) | collective-permute-done | bytes 180256 | tf_op jit(solution)/shard_map/ppermute | solution.py:39
  164.6 4.4 all-gather.17.cloned.1.call-done
  181.7 4.4 shard_map.185
  188.0 4.7 shard_map.186
  195.0 7.2 collective-permute-done.36
  205.2 12.3 %collective-permute-done.37.refs_3_ = bf16[256,1024]{1,0:T(8,128)(2,1)S(1)} collective-permute-done((bf16[256,1024]{1,0:T(8,128)(2,1)S(1)}, bf16[256,1024]{1,0:T(8,128)(2,1)S(1)}, u32[]{:S(2)}, u32[]{:S(2)}) %collective-permute-start.37) | collective-permute-done | bytes 524320 | tf_op jit(solution)/shard_map/ppermute | solution.py:39
  224.1 9.1 %collective-permute-done.39.refs_2_ = bf16[256,1024]{1,0:T(8,128)(2,1)} collective-permute-done((bf16[256,1024]{1,0:T(8,128)(2,1)}, bf16[256,1024]{1,0:T(8,128)(2,1)}, u32[]{:S(2)}, u32[]{:S(2)}) %collective-permute-start.39) | collective-permute-done | bytes 524320 | tf_op jit(solution)/shard_map/ppermute | solution.py:39
  244.2 11.6 %shard_map.189 = (bf16[1024,256]{1,0:T(8,128)(2,1)S(1)}, bf16[1024,256]{1,0:T(8,128)(2,1)S(1)}, bf16[1024,256]{1,0:T(8,128)(2,1)S(1)}, bf16[1024,256]{1,0:T(8,128)(2,1)S(1)}) custom-call(s32[5]{0:T(128)S(1)} %pad_add_fusion.scalars_ref, bf16[256,1024]{1,0:T(8,128)(2,1)} %get-tuple-element.126.refs_0_.refs_11_, ...), custom_call_target="tpu_custom_call" | custom-call | flops 1 | bytes 1 | tf_op jit(solution)/shard_map/pallas_call | solution.py:111
  257.1 3.8 collective-permute-start.42
  260.9 8.1 %collective-permute-done.43.refs_2_.refs_3_.refs_5_ = bf16[4,704,256]{2,1,0:T(8,128)(2,1)S(1)} collective-permute-done((bf16[4,704,256]{2,1,0:T(8,128)(2,1)}, bf16[4,704,256]{2,1,0:T(8,128)(2,1)S(1)}, u32[]{:S(2)}, u32[]{:S(2)}) %collective-permute-start.43) | collective-permute-done | bytes 1441824 | tf_op jit(solution)/shard_map/ppermute | solution.py:43
  270.8 10.4 %collective-permute-done.44.refs_3_ = bf16[256,1024]{1,0:T(8,128)(2,1)S(1)} collective-permute-done((bf16[256,1024]{1,0:T(8,128)(2,1)S(1)}, bf16[256,1024]{1,0:T(8,128)(2,1)S(1)}, u32[]{:S(2)}, u32[]{:S(2)}) %collective-permute-start.44) | collective-permute-done | bytes 524320 | tf_op jit(solution)/shard_map/ppermute | solution.py:39
  286.5 6.5 collective-permute-done.47.refs_0_.refs_2_
  293.0 3.8 collective-permute-start.48
  296.8 4.1 shard_map.193
  300.8 4.1 shard_map.194
  309.1 3.2 collective-permute-start.53
  316.8 12.6 %collective-permute-done.53 = bf16[128,1024]{1,0:T(8,128)(2,1)S(1)} collective-permute-done((bf16[128,1024]{1,0:T(8,128)(2,1)S(1)}, bf16[128,1024]{1,0:T(8,128)(2,1)S(1)}, u32[]{:S(2)}, u32[]{:S(2)}) %collective-permute-start.53) | collective-permute-done | bytes 262176 | tf_op jit(solution)/shard_map/ppermute | solution.py:759
  329.3 5.6 collective-permute-done.54
  339.6 7.1 collective-permute-done.57.refs_0_.refs_4_
  346.7 4.1 collective-permute-start.58
  350.8 4.6 shard_map.196
  355.4 4.6 shard_map.197
  364.9 3.2 shard_map.200
  368.1 7.9 %collective-permute-done.60.refs_3_ = bf16[256,1024]{1,0:T(8,128)(2,1)S(1)} collective-permute-done((bf16[256,1024]{1,0:T(8,128)(2,1)S(1)}, bf16[256,1024]{1,0:T(8,128)(2,1)S(1)}, u32[]{:S(2)}, u32[]{:S(2)}) %collective-permute-start.60) | collective-permute-done | bytes 524320 | tf_op jit(solution)/shard_map/ppermute | solution.py:39
  380.9 10.2 %collective-permute-done.62.refs_2_.refs_4_ = bf16[256,1024]{1,0:T(8,128)(2,1)S(1)} collective-permute-done((bf16[256,1024]{1,0:T(8,128)(2,1)S(1)}, bf16[256,1024]{1,0:T(8,128)(2,1)S(1)}, u32[]{:S(2)}, u32[]{:S(2)}) %collective-permute-start.62) | collective-permute-done | bytes 524320 | tf_op jit(solution)/shard_map/ppermute | solution.py:39
  395.2 17.4 %shard_map.203 = (f32[256,1024]{1,0:T(8,128)S(1)}, f32[256,1024]{1,0:T(8,128)S(1)}, bf16[2,256,1024]{2,1,0:T(8,128)(2,1)S(1)}, bf16[1024,768]{1,0:T(8,128)(2,1)S(1)}, f32[1024,256]{1,0:T(8,128)S(1)}) custom-call(s32[5]{0:T(128)S(1)} %pad_add_fusion.scalars_ref, bf16[256,1024]{1,0:T(8,128)(2,1)S(1)} %get-tuple-element.154.refs_0_.refs_2_, ...), custom_call_target="tpu_custom_call" | custom-call | flops 1 | bytes 1 | tf_op jit(solution)/shard_map/pallas_call | solution.py:111
  418.9 3.6 shard_map.205
  423.4 10.0 %collective-permute-done.67.refs_3_ = bf16[4,704,128]{2,1,0:T(8,128)(2,1)S(1)} collective-permute-done((bf16[4,704,128]{2,1,0:T(8,128)(2,1)S(1)}, bf16[4,704,128]{2,1,0:T(8,128)(2,1)S(1)}, u32[]{:S(2)}, u32[]{:S(2)}) %collective-permute-start.67) | collective-permute-done | bytes 720928 | tf_op jit(solution)/shard_map/ppermute | solution.py:43
  446.1 3.5 collective-permute-done.66.refs_3_
  457.3 7.8 %collective-permute-done.71.refs_0_.refs_4_ = bf16[256,1024]{1,0:T(8,128)(2,1)} collective-permute-done((bf16[256,1024]{1,0:T(8,128)(2,1)}, bf16[256,1024]{1,0:T(8,128)(2,1)}, u32[]{:S(2)}, u32[]{:S(2)}) %collective-permute-start.71) | collective-permute-done | bytes 524320 | tf_op jit(solution)/shard_map/ppermute | solution.py:39
  467.6 4.0 collective-permute-done.69.refs_1_
  475.5 5.8 shard_map.210
  482.3 5.4 shard_map.211
  496.1 3.3 shard_map.213
  500.2 8.4 %collective-permute-done.76.refs_1_ = bf16[352,1024]{1,0:T(8,128)(2,1)S(1)} collective-permute-done((bf16[352,1024]{1,0:T(8,128)(2,1)}, bf16[352,1024]{1,0:T(8,128)(2,1)S(1)}, u32[]{:S(2)}, u32[]{:S(2)}) %collective-permute-start.76) | collective-permute-done | bytes 720928 | tf_op jit(solution)/shard_map/ppermute | solution.py:43
  509.3 4.9 collective-permute-done.75.refs_1_
  514.9 4.4 shard_map.216
  526.6 8.8 %collective-permute-done.78.refs_2_.refs_4_ = bf16[256,1024]{1,0:T(8,128)(2,1)S(1)} collective-permute-done((bf16[256,1024]{1,0:T(8,128)(2,1)S(1)}, bf16[256,1024]{1,0:T(8,128)(2,1)S(1)}, u32[]{:S(2)}, u32[]{:S(2)}) %collective-permute-start.78) | collective-permute-done | bytes 524320 | tf_op jit(solution)/shard_map/ppermute | solution.py:39
  541.1 3.4 shard_map.218
  545.4 18.3 %shard_map.219 = (f32[256,1024]{1,0:T(8,128)S(1)}, f32[256,1024]{1,0:T(8,128)S(1)}, bf16[2,256,1024]{2,1,0:T(8,128)(2,1)}, bf16[1024,768]{1,0:T(8,128)(2,1)S(1)}, f32[1024,256]{1,0:T(8,128)S(1)}) custom-call(s32[5]{0:T(128)S(1)} %pad_add_fusion.scalars_ref, bf16[256,1024]{1,0:T(8,128)(2,1)S(1)} %get-tuple-element.190.refs_0_.refs_2_, ...), custom_call_target="tpu_custom_call" | custom-call | flops 1 | bytes 1 | tf_op jit(solution)/shard_map/pallas_call | solution.py:111
  578.6 3.8 collective-permute-start.52
  585.9 3.3 shard_map.221
  606.8 5.6 collective-permute-done.52
  617.8 6.4 collective-permute-start.84
  625.8 5.0 collective-permute-done.93.refs_1_
  632.1 6.7 collective-permute-done.92.refs_1_
  651.4 12.4 %collective-permute-done.85 = bf16[128,1024]{1,0:T(8,128)(2,1)} collective-permute-done((bf16[128,1024]{1,0:T(8,128)(2,1)}, bf16[128,1024]{1,0:T(8,128)(2,1)}, u32[]{:S(2)}, u32[]{:S(2)}) %collective-permute-start.85) | collective-permute-done | bytes 262176 | tf_op jit(solution)/shard_map/ppermute | solution.py:766
  667.7 3.2 collective-permute-start.88
  675.3 8.6 %collective-permute-done.88 = bf16[128,768]{1,0:T(8,128)(2,1)S(1)} collective-permute-done((bf16[128,768]{1,0:T(8,128)(2,1)S(1)}, bf16[128,768]{1,0:T(8,128)(2,1)S(1)}, u32[]{:S(2)}, u32[]{:S(2)}) %collective-permute-start.88) | collective-permute-done | bytes 196640 | tf_op jit(solution)/shard_map/ppermute | solution.py:86
  684.5 3.6 collective-permute-done.89
  700.4 4.1 collective-permute-start.110
  706.8 22.9 %collective-permute-done.109 = bf16[128,1024]{1,0:T(8,128)(2,1)S(1)} collective-permute-done((bf16[128,1024]{1,0:T(8,128)(2,1)S(1)}, bf16[128,1024]{1,0:T(8,128)(2,1)S(1)}, u32[]{:S(2)}, u32[]{:S(2)}) %collective-permute-start.109) | collective-permute-done | bytes 262176 | tf_op jit(solution)/shard_map/ppermute | solution.py:766
  729.8 6.4 collective-permute-done.110
  737.4 3.6 collective-permute-start.104
  (749 shorter events, 305.4 us)
Async XLA Ops:
  7.2 60.3 %all-gather.11.cloned.1.call-start = ((), (), s32[]{:S(2)}) async-start(), calls=%async_computation.10 | async-start | bytes 1310720 | tf_op jit(solution)/shard_map/all_gather | solution.py:770
  8.0 24.1 %collective-permute-start.3 = (f32[4,32]{1,0:T(4,128)S(1)}, f32[4,32]{1,0:T(4,128)S(1)}, u32[]{:S(2)}, u32[]{:S(2)}) collective-permute-start(f32[4,32]{1,0:T(4,128)S(1)} %maximum_convert_fusion.6), channel_id=1, source_target_pairs={{0,8},{8,0},{16,24},{24,16},{1,9},{9,1},{17,25},{25,17},{2,10},{10... | collective-permute-start | bytes 1544 | tf_op jit(solution)/shard_map/ppermute | solution.py:80
  8.2 23.9 %collective-permute-start.4 = (f32[4,32]{1,0:T(4,128)S(1)}, f32[4,32]{1,0:T(4,128)S(1)}, u32[]{:S(2)}, u32[]{:S(2)}) collective-permute-start(f32[4,32]{1,0:T(4,128)S(1)} %maximum_convert_fusion.6), channel_id=1, source_target_pairs={{0,16},{8,24},{16,0},{24,8},{1,17},{9,25},{17,1},{25,9},{2,18},{10... | collective-permute-start | bytes 1544 | tf_op jit(solution)/shard_map/ppermute | solution.py:80
  10.5 21.6 %collective-permute-start.5 = (f32[4,32]{1,0:T(4,128)S(1)}, f32[4,32]{1,0:T(4,128)S(1)}, u32[]{:S(2)}, u32[]{:S(2)}) collective-permute-start(f32[4,32]{1,0:T(4,128)S(1)} %maximum_convert_fusion.6), channel_id=1, source_target_pairs={{0,24},{8,16},{16,8},{24,0},{1,25},{9,17},{17,9},{25,1},{2,26},{10... | collective-permute-start | bytes 1544 | tf_op jit(solution)/shard_map/ppermute | solution.py:80
  11.8 32.1 %collective-permute-start.1 = (bf16[128,1024]{1,0:T(8,128)(2,1)S(1)}, bf16[128,1024]{1,0:T(8,128)(2,1)S(1)}, u32[]{:S(2)}, u32[]{:S(2)}) collective-permute-start(bf16[128,1024]{1,0:T(8,128)(2,1)S(1)} %get-tuple-element.237), channel_id=1, source_target_pairs={{0,0},{1,8},{2,16},{3,24},{4,4},{5,12},{6,20},{7,28},{8,1},{9,9},{... | collective-permute-start | bytes 786440 | tf_op jit(solution)/shard_map/ppermute | solution.py:759
  27.4 16.5 %collective-permute-start.2 = (bf16[128,1024]{1,0:T(8,128)(2,1)S(1)}, bf16[128,1024]{1,0:T(8,128)(2,1)S(1)}, u32[]{:S(2)}, u32[]{:S(2)}) collective-permute-start(bf16[128,1024]{1,0:T(8,128)(2,1)S(1)} %get-tuple-element.238), channel_id=1, source_target_pairs={{0,4},{1,12},{2,20},{3,28},{4,0},{5,8},{6,16},{7,24},{8,5},{9,13},... | collective-permute-start | bytes 786440 | tf_op jit(solution)/shard_map/ppermute | solution.py:759
  40.1 90.7 %all-gather.13.cloned.1.call-start = ((), (), s32[]{:S(2)}) async-start(), calls=%async_computation.11 | async-start | bytes 1802240 | tf_op jit(solution)/shard_map/all_gather | solution.py:770
  55.1 93.4 %all-gather.15.cloned.1.call-start = ((), (), s32[]{:S(2)}) async-start(), calls=%async_computation.12 | async-start | bytes 1802240 | tf_op jit(solution)/shard_map/all_gather | solution.py:770
  56.0 113.0 %all-gather.17.cloned.1.call-start = ((), (), s32[]{:S(2)}) async-start(), calls=%async_computation.13 | async-start | bytes 1310720 | tf_op jit(solution)/shard_map/all_gather | solution.py:770
  74.6 23.5 %collective-permute-start.14 = (bf16[4,128,768]{2,1,0:T(8,128)(2,1)S(1)}, bf16[4,128,768]{2,1,0:T(8,128)(2,1)S(1)}, u32[]{:S(2)}, u32[]{:S(2)}) collective-permute-start(bf16[4,128,768]{2,1,0:T(8,128)(2,1)S(1)} %slice.190), channel_id=1, source_target_pairs={{0,4},{4,0},{1,5},{5,1},{2,6},{6,2},{3,7},{7,3},{8,12},{12,8},{9,1... | collective-permute-start | bytes 2359304 | tf_op jit(solution)/shard_map/ppermute | solution.py:43
  80.0 18.0 %collective-permute-start.9 = (bf16[256,1024]{1,0:T(8,128)(2,1)S(1)}, bf16[256,1024]{1,0:T(8,128)(2,1)S(1)}, u32[]{:S(2)}, u32[]{:S(2)}) collective-permute-start(bf16[256,1024]{1,0:T(8,128)(2,1)S(1)} %get-tuple-element.111.refs_1_.refs_0_), channel_id=1, source_target_pairs={{0,1},{1,0},{2,3},{3,2},{4,5},{5,4},{6,7},{7,6},{8,9},{9,8},{10,11... | collective-permute-start | bytes 1572872 | tf_op jit(solution)/shard_map/ppermute | solution.py:35
  123.3 111.6 %all-gather.19.cloned.1.call-start = ((), (), s32[]{:S(2)}) async-start(), calls=%async_computation.14 | async-start | bytes 1802240 | tf_op jit(solution)/shard_map/all_gather | solution.py:770
  130.8 50.9 %collective-permute-start.25 = (bf16[4,704,256]{2,1,0:T(8,128)(2,1)}, bf16[4,704,256]{2,1,0:T(8,128)(2,1)S(1)}, u32[]{:S(2)}, u32[]{:S(2)}) collective-permute-start(bf16[4,704,256]{2,1,0:T(8,128)(2,1)} %bitcast.291), channel_id=1, source_target_pairs={{0,4},{4,0},{1,5},{5,1},{2,6},{6,2},{3,7},{7,3},{8,12},{12,8},{9,1... | collective-permute-start | bytes 4325384 | tf_op jit(solution)/shard_map/ppermute | solution.py:43
  145.7 26.8 %collective-permute-start.30 = (bf16[256,1024]{1,0:T(8,128)(2,1)}, bf16[256,1024]{1,0:T(8,128)(2,1)}, u32[]{:S(2)}, u32[]{:S(2)}) collective-permute-start(bf16[256,1024]{1,0:T(8,128)(2,1)} %get-tuple-element.118.refs_1_.refs_0_), channel_id=1, source_target_pairs={{0,2},{2,0},{1,3},{3,1},{4,6},{6,4},{5,7},{7,5},{8,10},{10,8},{9,1... | collective-permute-start | bytes 1572872 | tf_op jit(solution)/shard_map/ppermute | solution.py:39
  147.3 15.1 %collective-permute-start.27 = (bf16[2,2,32,704]{3,2,1,0:T(8,128)(2,1)S(1)}, bf16[2,2,32,704]{3,2,1,0:T(8,128)(2,1)S(1)}, u32[]{:S(2)}, u32[]{:S(2)}) collective-permute-start(bf16[2,2,32,704]{3,2,1,0:T(8,128)(2,1)S(1)} %get-tuple-element.250), channel_id=1, source_target_pairs={{0,2},{2,0},{1,3},{3,1},{4,6},{6,4},{5,7},{7,5},{8,10},{10,8},{9,1... | collective-permute-start | bytes 540680 | tf_op jit(solution)/shard_map/ppermute | solution.py:39
  151.1 28.0 %collective-permute-start.26 = (bf16[352,1024]{1,0:T(8,128)(2,1)}, bf16[352,1024]{1,0:T(8,128)(2,1)}, u32[]{:S(2)}, u32[]{:S(2)}) collective-permute-start(bf16[352,1024]{1,0:T(8,128)(2,1)} %bitcast.66.refs_4_.refs_6_), channel_id=1, source_target_pairs={{0,4},{4,0},{1,5},{5,1},{2,6},{6,2},{3,7},{7,3},{8,12},{12,8},{9,1... | collective-permute-start | bytes 2162696 | tf_op jit(solution)/shard_map/ppermute | solution.py:43
  172.5 15.5 %collective-permute-start.31 = (bf16[256,1024]{1,0:T(8,128)(2,1)}, bf16[256,1024]{1,0:T(8,128)(2,1)}, u32[]{:S(2)}, u32[]{:S(2)}) collective-permute-start(bf16[256,1024]{1,0:T(8,128)(2,1)} %collective-permute-done.30.refs_0_.refs_2_), channel_id=1, source_target_pairs={{0,1},{1,0},{2,3},{3,2},{4,5},{5,4},{6,7},{7,6},{8,9},{9,8},{10,11... | collective-permute-start | bytes 1572872 | tf_op jit(solution)/shard_map/ppermute | solution.py:35
  173.6 466.3 %reduce-scatter.8.cloned.1.call-start = ((), (), s32[]{:S(2)}) async-start(), calls=%async_computation.6 | async-start | bytes 1802240 | tf_op jit(solution)/shard_map/reduce_scatter | solution.py:96
  175.4 27.7 %collective-permute-start.33 = (bf16[4,128,768]{2,1,0:T(8,128)(2,1)S(1)}, bf16[4,128,768]{2,1,0:T(8,128)(2,1)S(1)}, u32[]{:S(2)}, u32[]{:S(2)}) collective-permute-start(bf16[4,128,768]{2,1,0:T(8,128)(2,1)S(1)} %slice.194), channel_id=1, source_target_pairs={{0,4},{4,0},{1,5},{5,1},{2,6},{6,2},{3,7},{7,3},{8,12},{12,8},{9,1... | collective-permute-start | bytes 2359304 | tf_op jit(solution)/shard_map/ppermute | solution.py:43
  179.1 14.6 %collective-permute-start.35 = (bf16[2,1,32,1024]{3,2,0,1:T(8,128)(2,1)S(1)}, bf16[2,1,32,1024]{3,2,0,1:T(8,128)(2,1)S(1)}, u32[]{:S(2)}, u32[]{:S(2)}) collective-permute-start(bf16[2,1,32,1024]{3,2,0,1:T(8,128)(2,1)S(1)} %get-tuple-element.272), channel_id=1, source_target_pairs={{0,1},{1,0},{2,3},{3,2},{4,5},{5,4},{6,7},{7,6},{8,9},{9,8},{10,11... | collective-permute-start | bytes 393224 | tf_op jit(solution)/shard_map/ppermute | solution.py:35
  221.4 16.8 %collective-permute-start.41 = (bf16[352,1024]{1,0:T(8,128)(2,1)}, bf16[352,1024]{1,0:T(8,128)(2,1)}, u32[]{:S(2)}, u32[]{:S(2)}) collective-permute-start(bf16[352,1024]{1,0:T(8,128)(2,1)} %bitcast.92.refs_4_.refs_6_), channel_id=1, source_target_pairs={{0,4},{4,0},{1,5},{5,1},{2,6},{6,2},{3,7},{7,3},{8,12},{12,8},{9,1... | collective-permute-start | bytes 2162696 | tf_op jit(solution)/shard_map/ppermute | solution.py:43
  222.6 15.6 %collective-permute-start.38 = (bf16[256,1024]{1,0:T(8,128)(2,1)}, bf16[256,1024]{1,0:T(8,128)(2,1)}, u32[]{:S(2)}, u32[]{:S(2)}) collective-permute-start(bf16[256,1024]{1,0:T(8,128)(2,1)} %get-tuple-element.126.refs_0_.refs_11_), channel_id=1, source_target_pairs={{0,1},{1,0},{2,3},{3,2},{4,5},{5,4},{6,7},{7,6},{8,9},{9,8},{10,11... | collective-permute-start | bytes 1572872 | tf_op jit(solution)/shard_map/ppermute | solution.py:35
  234.9 34.1 %collective-permute-start.43 = (bf16[4,704,256]{2,1,0:T(8,128)(2,1)}, bf16[4,704,256]{2,1,0:T(8,128)(2,1)S(1)}, u32[]{:S(2)}, u32[]{:S(2)}) collective-permute-start(bf16[4,704,256]{2,1,0:T(8,128)(2,1)} %bitcast.285), channel_id=1, source_target_pairs={{0,4},{4,0},{1,5},{5,1},{2,6},{6,2},{3,7},{7,3},{8,12},{12,8},{9,1... | collective-permute-start | bytes 4325384 | tf_op jit(solution)/shard_map/ppermute | solution.py:43
  305.0 30.0 %collective-permute-start.46 = (bf16[256,1024]{1,0:T(8,128)(2,1)S(1)}, bf16[256,1024]{1,0:T(8,128)(2,1)S(1)}, u32[]{:S(2)}, u32[]{:S(2)}) collective-permute-start(bf16[256,1024]{1,0:T(8,128)(2,1)S(1)} %get-tuple-element.134), channel_id=1, source_target_pairs={{0,1},{1,0},{2,3},{3,2},{4,5},{5,4},{6,7},{7,6},{8,9},{9,8},{10,11... | collective-permute-start | bytes 1572872 | tf_op jit(solution)/shard_map/ppermute | solution.py:35
  307.5 27.5 %collective-permute-start.50 = (bf16[256,1024]{1,0:T(8,128)(2,1)S(1)}, bf16[256,1024]{1,0:T(8,128)(2,1)S(1)}, u32[]{:S(2)}, u32[]{:S(2)}) collective-permute-start(bf16[256,1024]{1,0:T(8,128)(2,1)S(1)} %shard_map.195.refs_8_), channel_id=1, source_target_pairs={{0,2},{2,0},{1,3},{3,1},{4,6},{6,4},{5,7},{7,5},{8,10},{10,8},{9,1... | collective-permute-start | bytes 1572872 | tf_op jit(solution)/shard_map/ppermute | solution.py:39
  309.1 20.2 %collective-permute-start.53 = (bf16[128,1024]{1,0:T(8,128)(2,1)S(1)}, bf16[128,1024]{1,0:T(8,128)(2,1)S(1)}, u32[]{:S(2)}, u32[]{:S(2)}) collective-permute-start(bf16[128,1024]{1,0:T(8,128)(2,1)S(1)} %get-tuple-element.233), channel_id=1, source_target_pairs={{0,0},{1,8},{2,16},{3,24},{4,4},{5,12},{6,20},{7,28},{8,1},{9,9},{... | collective-permute-start | bytes 786440 | tf_op jit(solution)/shard_map/ppermute | solution.py:759
  312.3 22.6 %collective-permute-start.54 = (bf16[128,1024]{1,0:T(8,128)(2,1)S(1)}, bf16[128,1024]{1,0:T(8,128)(2,1)S(1)}, u32[]{:S(2)}, u32[]{:S(2)}) collective-permute-start(bf16[128,1024]{1,0:T(8,128)(2,1)S(1)} %get-tuple-element.234), channel_id=1, source_target_pairs={{0,4},{1,12},{2,20},{3,28},{4,0},{5,8},{6,16},{7,24},{8,5},{9,13},... | collective-permute-start | bytes 786440 | tf_op jit(solution)/shard_map/ppermute | solution.py:759
  378.6 16.6 %collective-permute-start.64 = (bf16[4,704,128]{2,1,0:T(8,128)(2,1)S(1)}, bf16[4,704,128]{2,1,0:T(8,128)(2,1)S(1)}, u32[]{:S(2)}, u32[]{:S(2)}) collective-permute-start(bf16[4,704,128]{2,1,0:T(8,128)(2,1)S(1)} %get-tuple-element.151.refs_6_), channel_id=1, source_target_pairs={{0,4},{4,0},{1,5},{5,1},{2,6},{6,2},{3,7},{7,3},{8,12},{12,8},{9,1... | collective-permute-start | bytes 2162696 | tf_op jit(solution)/shard_map/ppermute | solution.py:43
  379.4 15.8 %collective-permute-start.61 = (bf16[256,1024]{1,0:T(8,128)(2,1)S(1)}, bf16[256,1024]{1,0:T(8,128)(2,1)S(1)}, u32[]{:S(2)}, u32[]{:S(2)}) collective-permute-start(bf16[256,1024]{1,0:T(8,128)(2,1)S(1)} %get-tuple-element.154.refs_0_.refs_2_), channel_id=1, source_target_pairs={{0,1},{1,0},{2,3},{3,2},{4,5},{5,4},{6,7},{7,6},{8,9},{9,8},{10,11... | collective-permute-start | bytes 1572872 | tf_op jit(solution)/shard_map/ppermute | solution.py:35
  415.7 17.8 %collective-permute-start.67 = (bf16[4,704,128]{2,1,0:T(8,128)(2,1)S(1)}, bf16[4,704,128]{2,1,0:T(8,128)(2,1)S(1)}, u32[]{:S(2)}, u32[]{:S(2)}) collective-permute-start(bf16[4,704,128]{2,1,0:T(8,128)(2,1)S(1)} %get-tuple-element.159.refs_13_), channel_id=1, source_target_pairs={{0,4},{4,0},{1,5},{5,1},{2,6},{6,2},{3,7},{7,3},{8,12},{12,8},{9,1... | collective-permute-start | bytes 2162696 | tf_op jit(solution)/shard_map/ppermute | solution.py:43
  436.4 205.0 %reduce-scatter.6.cloned.1.call-start = ((), (), s32[]{:S(2)}) async-start(), calls=%async_computation.5 | async-start | bytes 983040 | tf_op jit(solution)/shard_map/reduce_scatter | solution.py:96
  454.4 17.2 %collective-permute-start.69 = (bf16[4,128,768]{2,1,0:T(8,128)(2,1)S(1)}, bf16[4,128,768]{2,1,0:T(8,128)(2,1)S(1)}, u32[]{:S(2)}, u32[]{:S(2)}) collective-permute-start(bf16[4,128,768]{2,1,0:T(8,128)(2,1)S(1)} %copy-done.121), channel_id=1, source_target_pairs={{0,4},{4,0},{1,5},{5,1},{2,6},{6,2},{3,7},{7,3},{8,12},{12,8},{9,1... | collective-permute-start | bytes 2359304 | tf_op jit(solution)/shard_map/ppermute | solution.py:43
  455.2 18.0 %collective-permute-start.68 = (bf16[256,1024]{1,0:T(8,128)(2,1)}, bf16[256,1024]{1,0:T(8,128)(2,1)}, u32[]{:S(2)}, u32[]{:S(2)}) collective-permute-start(bf16[256,1024]{1,0:T(8,128)(2,1)} %get-tuple-element.170.refs_0_.refs_2_), channel_id=1, source_target_pairs={{0,1},{1,0},{2,3},{3,2},{4,5},{5,4},{6,7},{7,6},{8,9},{9,8},{10,11... | collective-permute-start | bytes 1572872 | tf_op jit(solution)/shard_map/ppermute | solution.py:35
  465.1 17.1 %collective-permute-start.72 = (bf16[256,1024]{1,0:T(8,128)(2,1)}, bf16[256,1024]{1,0:T(8,128)(2,1)}, u32[]{:S(2)}, u32[]{:S(2)}) collective-permute-start(bf16[256,1024]{1,0:T(8,128)(2,1)} %collective-permute-done.71.refs_0_.refs_4_), channel_id=1, source_target_pairs={{0,1},{1,0},{2,3},{3,2},{4,5},{5,4},{6,7},{7,6},{8,9},{9,8},{10,11... | collective-permute-start | bytes 1572872 | tf_op jit(solution)/shard_map/ppermute | solution.py:35
  490.6 18.0 %collective-permute-start.76 = (bf16[352,1024]{1,0:T(8,128)(2,1)}, bf16[352,1024]{1,0:T(8,128)(2,1)S(1)}, u32[]{:S(2)}, u32[]{:S(2)}) collective-permute-start(bf16[352,1024]{1,0:T(8,128)(2,1)} %get-tuple-element.152.refs_6_), channel_id=1, source_target_pairs={{0,4},{4,0},{1,5},{5,1},{2,6},{6,2},{3,7},{7,3},{8,12},{12,8},{9,1... | collective-permute-start | bytes 2162696 | tf_op jit(solution)/shard_map/ppermute | solution.py:43
  491.4 27.9 %collective-permute-start.70 = (bf16[256,1024]{1,0:T(8,128)(2,1)}, bf16[256,1024]{1,0:T(8,128)(2,1)S(1)}, u32[]{:S(2)}, u32[]{:S(2)}) collective-permute-start(bf16[256,1024]{1,0:T(8,128)(2,1)} %get-tuple-element.176), channel_id=1, source_target_pairs={{0,1},{1,0},{2,3},{3,2},{4,5},{5,4},{6,7},{7,6},{8,9},{9,8},{10,11... | collective-permute-start | bytes 1572872 | tf_op jit(solution)/shard_map/ppermute | solution.py:35
  493.7 25.6 %collective-permute-start.74 = (bf16[256,1024]{1,0:T(8,128)(2,1)S(1)}, bf16[256,1024]{1,0:T(8,128)(2,1)}, u32[]{:S(2)}, u32[]{:S(2)}) collective-permute-start(bf16[256,1024]{1,0:T(8,128)(2,1)S(1)} %shard_map.212.refs_6_), channel_id=1, source_target_pairs={{0,2},{2,0},{1,3},{3,1},{4,6},{6,4},{5,7},{7,5},{8,10},{10,8},{9,1... | collective-permute-start | bytes 1572872 | tf_op jit(solution)/shard_map/ppermute | solution.py:39
  493.8 149.8 %reduce-scatter.12.cloned.1.call-start = ((), (), s32[]{:S(2)}) async-start(), calls=%async_computation.8 | async-start | bytes 1228800 | tf_op jit(solution)/shard_map/reduce_scatter | solution.py:96
  494.1 20.2 %collective-permute-start.75 = (bf16[128,1024]{1,0:T(8,128)(2,1)S(1)}, bf16[128,1024]{1,0:T(8,128)(2,1)S(1)}, u32[]{:S(2)}, u32[]{:S(2)}) collective-permute-start(bf16[128,1024]{1,0:T(8,128)(2,1)S(1)} %copy-done.139), channel_id=1, source_target_pairs={{0,4},{4,0},{1,5},{5,1},{2,6},{6,2},{3,7},{7,3},{8,12},{12,8},{9,1... | collective-permute-start | bytes 786440 | tf_op jit(solution)/shard_map/ppermute | solution.py:43
  522.8 22.5 %collective-permute-start.80 = (bf16[4,704,128]{2,1,0:T(8,128)(2,1)S(1)}, bf16[4,704,128]{2,1,0:T(8,128)(2,1)S(1)}, u32[]{:S(2)}, u32[]{:S(2)}) collective-permute-start(bf16[4,704,128]{2,1,0:T(8,128)(2,1)S(1)} %get-tuple-element.187.refs_2_), channel_id=1, source_target_pairs={{0,4},{4,0},{1,5},{5,1},{2,6},{6,2},{3,7},{7,3},{8,12},{12,8},{9,1... | collective-permute-start | bytes 2162696 | tf_op jit(solution)/shard_map/ppermute | solution.py:43
  523.6 14.7 %collective-permute-start.101 = (bf16[2,1,32,1024]{3,2,0,1:T(8,128)(2,1)S(1)}, bf16[2,1,32,1024]{3,2,0,1:T(8,128)(2,1)S(1)}, u32[]{:S(2)}, u32[]{:S(2)}) collective-permute-start(bf16[2,1,32,1024]{3,2,0,1:T(8,128)(2,1)S(1)} %get-tuple-element.270), channel_id=1, source_target_pairs={{0,2},{2,0},{1,3},{3,1},{4,6},{6,4},{5,7},{7,5},{8,10},{10,8},{9,1... | collective-permute-start | bytes 393224 | tf_op jit(solution)/shard_map/ppermute | solution.py:39
  525.0 20.3 %collective-permute-start.77 = (bf16[256,1024]{1,0:T(8,128)(2,1)S(1)}, bf16[256,1024]{1,0:T(8,128)(2,1)S(1)}, u32[]{:S(2)}, u32[]{:S(2)}) collective-permute-start(bf16[256,1024]{1,0:T(8,128)(2,1)S(1)} %get-tuple-element.190.refs_0_.refs_2_), channel_id=1, source_target_pairs={{0,1},{1,0},{2,3},{3,2},{4,5},{5,4},{6,7},{7,6},{8,9},{9,8},{10,11... | collective-permute-start | bytes 1572872 | tf_op jit(solution)/shard_map/ppermute | solution.py:35
  568.3 136.3 %reduce-scatter.14.cloned.1.call-start = ((), (), s32[]{:S(2)}) async-start(), calls=%async_computation.9 | async-start | bytes 1802240 | tf_op jit(solution)/shard_map/reduce_scatter | solution.py:96
  568.4 22.4 %collective-permute-start.83 = (bf16[4,704,128]{2,1,0:T(8,128)(2,1)}, bf16[4,704,128]{2,1,0:T(8,128)(2,1)}, u32[]{:S(2)}, u32[]{:S(2)}) collective-permute-start(bf16[4,704,128]{2,1,0:T(8,128)(2,1)} %copy-done.130), channel_id=1, source_target_pairs={{0,4},{4,0},{1,5},{5,1},{2,6},{6,2},{3,7},{7,3},{8,12},{12,8},{9,1... | collective-permute-start | bytes 2162696 | tf_op jit(solution)/shard_map/ppermute | solution.py:43
  573.4 24.3 %collective-permute-start.82 = (bf16[256,1024]{1,0:T(8,128)(2,1)}, bf16[256,1024]{1,0:T(8,128)(2,1)}, u32[]{:S(2)}, u32[]{:S(2)}) collective-permute-start(bf16[256,1024]{1,0:T(8,128)(2,1)} %shard_map.220.refs_5_), channel_id=1, source_target_pairs={{0,2},{2,0},{1,3},{3,1},{4,6},{6,4},{5,7},{7,5},{8,10},{10,8},{9,1... | collective-permute-start | bytes 1572872 | tf_op jit(solution)/shard_map/ppermute | solution.py:39
  576.5 30.3 %collective-permute-start.51 = (bf16[128,1024]{1,0:T(8,128)(2,1)}, bf16[128,1024]{1,0:T(8,128)(2,1)}, u32[]{:S(2)}, u32[]{:S(2)}) collective-permute-start(bf16[128,1024]{1,0:T(8,128)(2,1)} %get-tuple-element.235), channel_id=1, source_target_pairs={{0,0},{8,1},{16,2},{24,3},{4,4},{12,5},{20,6},{28,7},{1,8},{9,9},{... | collective-permute-start | bytes 786440 | tf_op jit(solution)/shard_map/ppermute | solution.py:766
  578.6 33.9 %collective-permute-start.52 = (bf16[128,1024]{1,0:T(8,128)(2,1)}, bf16[128,1024]{1,0:T(8,128)(2,1)}, u32[]{:S(2)}, u32[]{:S(2)}) collective-permute-start(bf16[128,1024]{1,0:T(8,128)(2,1)} %get-tuple-element.236), channel_id=1, source_target_pairs={{4,0},{12,1},{20,2},{28,3},{0,4},{8,5},{16,6},{24,7},{5,8},{13,9},... | collective-permute-start | bytes 786440 | tf_op jit(solution)/shard_map/ppermute | solution.py:766
  590.1 34.0 %collective-permute-start.86 = (bf16[4,128,768]{2,1,0:T(8,128)(2,1)}, bf16[4,128,768]{2,1,0:T(8,128)(2,1)}, u32[]{:S(2)}, u32[]{:S(2)}) collective-permute-start(bf16[4,128,768]{2,1,0:T(8,128)(2,1)} %get-tuple-element.203.refs_4_), channel_id=1, source_target_pairs={{0,4},{4,0},{1,5},{5,1},{2,6},{6,2},{3,7},{7,3},{8,12},{12,8},{9,1... | collective-permute-start | bytes 2359304 | tf_op jit(solution)/shard_map/ppermute | solution.py:43
  602.0 28.8 %collective-permute-start.93 = (bf16[352,1024]{1,0:T(8,128)(2,1)}, bf16[352,1024]{1,0:T(8,128)(2,1)}, u32[]{:S(2)}, u32[]{:S(2)}) collective-permute-start(bf16[352,1024]{1,0:T(8,128)(2,1)} %get-tuple-element.188.refs_6_), channel_id=1, source_target_pairs={{0,4},{4,0},{1,5},{5,1},{2,6},{6,2},{3,7},{7,3},{8,12},{12,8},{9,1... | collective-permute-start | bytes 2162696 | tf_op jit(solution)/shard_map/ppermute | solution.py:43
  614.7 24.1 %collective-permute-start.92 = (bf16[128,1024]{1,0:T(8,128)(2,1)}, bf16[128,1024]{1,0:T(8,128)(2,1)}, u32[]{:S(2)}, u32[]{:S(2)}) collective-permute-start(bf16[128,1024]{1,0:T(8,128)(2,1)} %get-tuple-element.204.refs_6_), channel_id=1, source_target_pairs={{0,4},{4,0},{1,5},{5,1},{2,6},{6,2},{3,7},{7,3},{8,12},{12,8},{9,1... | collective-permute-start | bytes 786440 | tf_op jit(solution)/shard_map/ppermute | solution.py:43
  615.8 125.1 %reduce-scatter.10.cloned.1.call-start = ((), (), s32[]{:S(2)}) async-start(), calls=%async_computation.7 | async-start | bytes 1310720 | tf_op jit(solution)/shard_map/reduce_scatter | solution.py:96
  616.5 29.5 %collective-permute-start.100 = (f32[4,1024]{1,0:T(4,128)}, f32[4,1024]{1,0:T(4,128)}, u32[]{:S(2)}, u32[]{:S(2)}) collective-permute-start(f32[4,1024]{1,0:T(4,128)} %fusion.28), channel_id=1, source_target_pairs={{0,4},{4,0},{1,5},{5,1},{2,6},{6,2},{3,7},{7,3},{8,12},{12,8},{9,1... | collective-permute-start | bytes 49160 | tf_op jit(solution)/shard_map/ppermute | solution.py:43
  617.8 33.6 %collective-permute-start.84 = (bf16[128,1024]{1,0:T(8,128)(2,1)}, bf16[128,1024]{1,0:T(8,128)(2,1)}, u32[]{:S(2)}, u32[]{:S(2)}) collective-permute-start(bf16[128,1024]{1,0:T(8,128)(2,1)} %get-tuple-element.227), channel_id=1, source_target_pairs={{0,0},{8,1},{16,2},{24,3},{4,4},{12,5},{20,6},{28,7},{1,8},{9,9},{... | collective-permute-start | bytes 786440 | tf_op jit(solution)/shard_map/ppermute | solution.py:766
  624.2 39.7 %collective-permute-start.85 = (bf16[128,1024]{1,0:T(8,128)(2,1)}, bf16[128,1024]{1,0:T(8,128)(2,1)}, u32[]{:S(2)}, u32[]{:S(2)}) collective-permute-start(bf16[128,1024]{1,0:T(8,128)(2,1)} %get-tuple-element.228), channel_id=1, source_target_pairs={{4,0},{12,1},{20,2},{28,3},{0,4},{8,5},{16,6},{24,7},{5,8},{13,9},... | collective-permute-start | bytes 786440 | tf_op jit(solution)/shard_map/ppermute | solution.py:766
  648.2 41.8 %collective-permute-start.107 = (bf16[2,256,256]{2,1,0:T(8,128)(2,1)}, bf16[2,256,256]{2,1,0:T(8,128)(2,1)}, u32[]{:S(2)}, u32[]{:S(2)}) collective-permute-start(bf16[2,256,256]{2,1,0:T(8,128)(2,1)} %get-tuple-element.222), channel_id=1, source_target_pairs={{0,2},{2,0},{1,3},{3,1},{4,6},{6,4},{5,7},{7,5},{8,10},{10,8},{9,1... | collective-permute-start | bytes 786440 | tf_op jit(solution)/shard_map/ppermute | solution.py:39
  648.9 22.0 %collective-permute-start.96 = (bf16[2,1,32,1024]{3,2,0,1:T(8,128)(2,1)}, bf16[2,1,32,1024]{3,2,0,1:T(8,128)(2,1)}, u32[]{:S(2)}, u32[]{:S(2)}) collective-permute-start(bf16[2,1,32,1024]{3,2,0,1:T(8,128)(2,1)} %get-tuple-element.266), channel_id=1, source_target_pairs={{0,2},{2,0},{1,3},{3,1},{4,6},{6,4},{5,7},{7,5},{8,10},{10,8},{9,1... | collective-permute-start | bytes 393224 | tf_op jit(solution)/shard_map/ppermute | solution.py:39
  650.6 21.4 %collective-permute-start.105 = (bf16[2,2,32,704]{3,2,1,0:T(8,128)(2,1)S(1)}, bf16[2,2,32,704]{3,2,1,0:T(8,128)(2,1)S(1)}, u32[]{:S(2)}, u32[]{:S(2)}) collective-permute-start(bf16[2,2,32,704]{3,2,1,0:T(8,128)(2,1)S(1)} %bitcast.368), channel_id=1, source_target_pairs={{0,2},{2,0},{1,3},{3,1},{4,6},{6,4},{5,7},{7,5},{8,10},{10,8},{9,1... | collective-permute-start | bytes 540680 | tf_op jit(solution)/shard_map/ppermute | solution.py:39
  651.4 23.8 %collective-permute-start.87 = (bf16[128,768]{1,0:T(8,128)(2,1)S(1)}, bf16[128,768]{1,0:T(8,128)(2,1)S(1)}, u32[]{:S(2)}, u32[]{:S(2)}) collective-permute-start(bf16[128,768]{1,0:T(8,128)(2,1)S(1)} %get-tuple-element.212), channel_id=1, source_target_pairs={{0,8},{8,0},{16,24},{24,16},{1,9},{9,1},{17,25},{25,17},{2,10},{10... | collective-permute-start | bytes 589832 | tf_op jit(solution)/shard_map/ppermute | solution.py:86
  667.7 16.2 %collective-permute-start.88 = (bf16[128,768]{1,0:T(8,128)(2,1)S(1)}, bf16[128,768]{1,0:T(8,128)(2,1)S(1)}, u32[]{:S(2)}, u32[]{:S(2)}) collective-permute-start(bf16[128,768]{1,0:T(8,128)(2,1)S(1)} %get-tuple-element.214), channel_id=1, source_target_pairs={{0,16},{8,24},{16,0},{24,8},{1,17},{9,25},{17,1},{25,9},{2,18},{10... | collective-permute-start | bytes 589832 | tf_op jit(solution)/shard_map/ppermute | solution.py:86
  670.9 17.2 %collective-permute-start.89 = (bf16[128,768]{1,0:T(8,128)(2,1)S(1)}, bf16[128,768]{1,0:T(8,128)(2,1)S(1)}, u32[]{:S(2)}, u32[]{:S(2)}) collective-permute-start(bf16[128,768]{1,0:T(8,128)(2,1)S(1)} %get-tuple-element.213), channel_id=1, source_target_pairs={{0,24},{8,16},{16,8},{24,0},{1,25},{9,17},{17,9},{25,1},{2,26},{10... | collective-permute-start | bytes 589832 | tf_op jit(solution)/shard_map/ppermute | solution.py:86
  672.1 16.3 %collective-permute-start.95 = (bf16[2,32,768]{2,1,0:T(8,128)(2,1)S(1)}, bf16[2,32,768]{2,1,0:T(8,128)(2,1)S(1)}, u32[]{:S(2)}, u32[]{:S(2)}) collective-permute-start(bf16[2,32,768]{2,1,0:T(8,128)(2,1)S(1)} %get-tuple-element.284), channel_id=1, source_target_pairs={{0,1},{1,0},{2,3},{3,2},{4,5},{5,4},{6,7},{7,6},{8,9},{9,8},{10,11... | collective-permute-start | bytes 294920 | tf_op jit(solution)/shard_map/ppermute | solution.py:35
  698.3 31.5 %collective-permute-start.109 = (bf16[128,1024]{1,0:T(8,128)(2,1)S(1)}, bf16[128,1024]{1,0:T(8,128)(2,1)S(1)}, u32[]{:S(2)}, u32[]{:S(2)}) collective-permute-start(bf16[128,1024]{1,0:T(8,128)(2,1)S(1)} %get-tuple-element.217), channel_id=1, source_target_pairs={{0,0},{8,1},{16,2},{24,3},{4,4},{12,5},{20,6},{28,7},{1,8},{9,9},{... | collective-permute-start | bytes 786440 | tf_op jit(solution)/shard_map/ppermute | solution.py:766
  700.4 35.7 %collective-permute-start.110 = (bf16[128,1024]{1,0:T(8,128)(2,1)S(1)}, bf16[128,1024]{1,0:T(8,128)(2,1)S(1)}, u32[]{:S(2)}, u32[]{:S(2)}) collective-permute-start(bf16[128,1024]{1,0:T(8,128)(2,1)S(1)} %get-tuple-element.218), channel_id=1, source_target_pairs={{4,0},{12,1},{20,2},{28,3},{0,4},{8,5},{16,6},{24,7},{5,8},{13,9},... | collective-permute-start | bytes 786440 | tf_op jit(solution)/shard_map/ppermute | solution.py:766
  705.8 31.4 %collective-permute-start.103 = (bf16[2,2,32,704]{3,2,1,0:T(8,128)(2,1)S(1)}, bf16[2,2,32,704]{3,2,1,0:T(8,128)(2,1)S(1)}, u32[]{:S(2)}, u32[]{:S(2)}) collective-permute-start(bf16[2,2,32,704]{3,2,1,0:T(8,128)(2,1)S(1)} %bitcast.369), channel_id=1, source_target_pairs={{0,2},{2,0},{1,3},{3,1},{4,6},{6,4},{5,7},{7,5},{8,10},{10,8},{9,1... | collective-permute-start | bytes 540680 | tf_op jit(solution)/shard_map/ppermute | solution.py:39
  (219 other events, 1640.3 us)
Sparse Core Ops, SparseCore 0:
  40.3 27.2 all-gather.10
  69.7 33.5 all-gather.12
  105.4 33.8 all-gather.14
  141.2 27.6 all-gather.16
  173.7 33.1 all-gather.18
  436.6 32.7 reduce-scatter.7
  493.9 22.3 reduce-scatter.5
  568.4 38.6 reduce-scatter.11
  615.9 48.2 reduce-scatter.13
  690.2 41.7 reduce-scatter.9

commit v3 on v2

--- a/solution.py
+++ b/solution.py
@@ -11,6 +11,7 @@
 LAYERS = 2
 epsilon = 1e-05
 masked_score = -1e30
+SCALE = 0.125 * 1.4426950408889634
 bf16 = jnp.bfloat16
 f32 = jnp.float32
 
@@ -193,6 +194,12 @@
     lowest = jnp.where(query < start, 0, jnp.where(query < end, start, end))
     key = lax.broadcasted_iota(jnp.int32, shape, 1)
     return (key <= query) & (key >= lowest)
+
+
+def weigh_rows(scores, allowed):
+    scores = jnp.where(allowed, scores * SCALE, masked_score)
+    weights = jnp.exp2(scores - jnp.max(scores, axis=-1, keepdims=True))
+    return (weights, 1.0 / jnp.sum(weights, axis=-1, keepdims=True))
 
 
 def softmax_rows(scores, allowed):
@@ -262,8 +269,8 @@
             outs = []
             for h in range(2):
                 one = jnp.where(lane // 64 == h, query, jnp.zeros_like(query))
-                chance = softmax_rows(dot_cols(one, keys), allowed)
-                outs.append(dot(chance.astype(bf16), values))
+                weights, share = weigh_rows(dot_cols(one, keys), allowed)
+                outs.append(dot(weights.astype(bf16), values) * share)
             o_ref[there, columns] = jnp.where(lane < 64, outs[0], outs[1]).astype(bf16)
 
 
@@ -307,16 +314,17 @@
                 mine = lane // 64 == h
                 one = jnp.where(mine, query, jnp.zeros_like(query))
                 one_up = jnp.where(mine, up, jnp.zeros_like(up))
-                chance = softmax_rows(dot_cols(one, keys), allowed)
+                weights, share = weigh_rows(dot_cols(one, keys), allowed)
+                chance = weights * share
                 back = dot_cols(one_up, values)
                 delta = jnp.sum(chance * back, axis=-1, keepdims=True)
-                score = (chance * (back - delta) * 0.125).astype(bf16)
+                score = (chance * (back - delta)).astype(bf16)
                 dq.append(dot(score, keys))
-                dk.append(dot_rows(score, one))
+                dk.append(dot_rows(score, one * 0.125))
                 dv.append(dot_rows(chance.astype(bf16), one_up))
             dk_sum[upto, columns] += dk[0] + dk[1]
             dv_sum[upto, columns] += dv[0] + dv[1]
-            dq = jnp.where(lane < 64, dq[0], dq[1])
+            dq = jnp.where(lane < 64, dq[0], dq[1]) * 0.125
             d_ref[there, columns] = (dq * cosine - partner(dq) * sine).astype(bf16)
     for b in range(4):
         there = pl.ds(pl.multiple_of((me ^ b) * rows, rows), rows)
@@ -800,6 +808,7 @@
     gains = jnp.stack([norm_attn[0], norm_mlp[0], norm_attn[1], norm_mlp[1]])
     sums = (to_group(tokens),)
     first_qkv = exchange(qkv_pieces(0)).reshape(group_rows, 3 * width)
+    first_qkv, sums = lax.optimization_barrier((first_qkv, sums))
     gains = jnp.stack(by_distance(jnp.stack(gather_near(gains.astype(f32)))))
     gains = gains.transpose(1, 0, 2).reshape(4, sz_size, 1, 1, in_rows)
     gains = in_order(lax.axis_index("fx"), gains, swap_x(gains), 2)[:, :, :, 0]
@@ -810,8 +819,8 @@
 
     attention = [attention_weights(0, first_qkv)]
     mlps, downs = [], None
-    upstream = to_group(out_grad)
-
+
+    valid = group.valid()
     saved = []
     first = None
     for layer in range(LAYERS):
@@ -837,16 +846,17 @@
         if layer == 0:
             gates.append(mlp_weights(1))
         mlps.append(gates[layer] + downs[layer])
+        if layer > 0:
+            group.need(*first_up)
         near, far = group.mlp(m, mlps[layer])
+        if layer == 0:
+            upstream = to_group(group.hold(out_grad)).astype(f32) * valid
+            first_up = spread(upstream.astype(bf16))
         if layer == 0:
             group.need(attention[1][1][0], attention[1][2])
         sums = (middle, *group.reduce_pieces((*near[:2], *far[:2])))
         saved.append((entry, a, kept, out, middle, m, near[2:], far[2:]))
-    valid = group.valid()
     hidden_out = from_group(group.plain_sum(sums) * valid)
-
-    upstream = upstream.astype(f32) * valid
-    low = upstream.astype(bf16)
     carry = None
     grads = [None] * LAYERS
     gain_grads = [None] * (2 * LAYERS)
@@ -880,11 +890,13 @@
     for layer in reversed(range(LAYERS)):
         last = layer == 0
         entry, a, kept, out, middle, m, near, far = saved[layer]
-        y = spread(low)
+        y = first_up if waiting is None else spread(low)
         if waiting is not None:
             pair, qkv, down, outs = waiting
             qkv = scattered(group.add(*qkv))
         near_back, far_back = group.mlp_back(y, (near[:2], far[:2]), mlps[layer])
+        if not last:
+            group.need(*sums)
         partial = group.reduce_pieces((*near_back[:2], *far_back[:2]))
         keep, send = group.gate_grads(m, near_back[2], far_back[2])
         gate = (keep, swap_y(send))

time: 765 us -> 757 us (0.990)
  waiting for transfers between devices: 294 us -> 278 us
  starting transfers between devices: 150 us -> 161 us
    ppermute x6, waiting for transfers between devices: 48.2 us -> 38.5 us  [from_group(): lax.ppermute(pick(rows, (at + r) % 2), ALL, backs[r])]
    ppermute x31, waiting for transfers between devices: 124 us -> 132 us  [swap_x(): return lax.ppermute(value, 'fx', SWAP)]
    pallas_call x55 -> x56, Pallas kernels: 164 us -> 161 us  [kernel_call(): pl.pallas_call(whole, out_shape=[shape_of(*one) for one in results], in_s...]
    unnamed x326 -> x352, local copies, waits for them, and re-layouts: 57.2 us -> 58 us
  transfers between devices with their start and end apart: 121 -> 121, of which waited for: 53 -> 55; matrix products, arithmetic and copies ran while one was open for 9% -> 9% of each run, Pallas kernels for 18% -> 18%
where the time goes in v3:
time: 757 us; the launch traced here: 749 us
  waiting for transfers between devices  278 us (37%)
  starting transfers between devices  161 us (21%)
  Pallas kernels  161 us (21%)
  local copies, waits for them, and re-layouts  101 us (13%)
  other arithmetic  30.3 us (4%)
  between operations  17.1 us (2%)
    pallas_call x56, Pallas kernels, kernel_call(): pl.pallas_call(whole, out_shape=[shape_of(*one) for one in results], in_s...  161 us
    ppermute x31, waiting for transfers between devices, swap_x(): return lax.ppermute(value, 'fx', SWAP)  132 us
    ppermute x43, starting transfers between devices, swap_core(): return lax.ppermute(value, 'fc', SWAP)  68.4 us
    ppermute x20, waiting for transfers between devices, swap_y(): return lax.ppermute(value, 'sy', SWAP)  62.5 us
    unnamed x352, local copies, waits for them, and re-layouts  58 us
    ppermute x6, waiting for transfers between devices, from_group(): lax.ppermute(pick(rows, (at + r) % 2), ALL, backs[r])  38.5 us
    ppermute x31, starting transfers between devices, swap_x(): return lax.ppermute(value, 'fx', SWAP)  22.6 us
    ppermute x20, starting transfers between devices, swap_y(): return lax.ppermute(value, 'sy', SWAP)  21.3 us
  transfers between devices with their start and end apart: 121, of which 55 were waited for; matrix products, arithmetic and copies ran while one was open for 9% of the time, Pallas kernels for 18%

profile of v3, /device:TPU:11, one launch (start us, length us, event | category | flops | bytes accessed | tf_op | source)
XLA Modules:
  0.0 748.6 jit_solution(6949401368551655685)
XLA Ops:
  12.6 5.1 collective-permute-start.3
  28.1 4.7 collective-permute-start.4
  33.0 5.6 collective-permute-done.1
  52.2 5.0 collective-permute-done.23
  63.6 9.0 %all-gather.11.cloned.1.call-done = bf16[512,1024]{1,0:T(8,128)(2,1)} async-done(((bf16[128,1024]{1,0:T(8,128)(2,1)}), bf16[512,1024]{1,0:T(8,128)(2,1)}) %all-gather.11.cloned.1.call-update) | async-done | bytes 1048592 | tf_op jit(solution)/shard_map/all_gather | solution.py:778
  85.0 5.6 collective-permute-done.12.refs_2_
  96.7 6.1 collective-permute-done.17
  103.1 8.9 %shard_map.180 = (bf16[1024,256]{1,0:T(8,128)(2,1)S(1)}, bf16[1024,256]{1,0:T(8,128)(2,1)S(1)}, bf16[1024,256]{1,0:T(8,128)(2,1)S(1)}, bf16[1024,256]{1,0:T(8,128)(2,1)S(1)}, f32[1024,256]{1,0:T(8,128)S(1)}) custom-call(s32[5]{0:T(128)S(1)} %pad_add_fusion.scalars_ref, bf16[256,1024]{1,0:T(8,128)(2,1)S(1)} %get-tuple-element.114.refs_1_.refs_0_, ...), custom_call_target="tpu_custom_call" | custom-call | flops 1 | bytes 1 | tf_op jit(solution)/shard_map/pallas_call | solution.py:112
  120.1 4.3 collective-permute-done.19
  136.6 6.8 collective-permute-done.21.refs_3_
  155.8 10.2 %collective-permute-done.27 = bf16[2,2,32,704]{3,2,1,0:T(8,128)(2,1)S(1)} collective-permute-done((bf16[2,2,32,704]{3,2,1,0:T(8,128)(2,1)S(1)}, bf16[2,2,32,704]{3,2,1,0:T(8,128)(2,1)S(1)}, u32[]{:S(2)}, u32[]{:S(2)}) %collective-permute-start.27) | collective-permute-done | bytes 180256 | tf_op jit(solution)/shard_map/ppermute | solution.py:40
  168.1 5.9 all-gather.17.cloned.1.call-done
  184.9 4.5 shard_map.185
  190.4 5.0 shard_map.186
  197.3 7.6 %collective-permute-done.36 = bf16[1,4,32,1024]{3,2,1,0:T(8,128)(2,1)S(1)} collective-permute-done((bf16[1,4,32,1024]{3,2,1,0:T(8,128)(2,1)S(1)}, bf16[1,4,32,1024]{3,2,1,0:T(8,128)(2,1)S(1)}, u32[]{:S(2)}, u32[]{:S(2)}) %collective-permute-start.36) | collective-permute-done | bytes 262176 | tf_op jit(solution)/shard_map/ppermute | solution.py:44
  209.5 12.3 %collective-permute-done.37.refs_3_ = bf16[256,1024]{1,0:T(8,128)(2,1)S(1)} collective-permute-done((bf16[256,1024]{1,0:T(8,128)(2,1)S(1)}, bf16[256,1024]{1,0:T(8,128)(2,1)S(1)}, u32[]{:S(2)}, u32[]{:S(2)}) %collective-permute-start.37) | collective-permute-done | bytes 524320 | tf_op jit(solution)/shard_map/ppermute | solution.py:40
  228.4 9.2 %collective-permute-done.39.refs_2_ = bf16[256,1024]{1,0:T(8,128)(2,1)} collective-permute-done((bf16[256,1024]{1,0:T(8,128)(2,1)}, bf16[256,1024]{1,0:T(8,128)(2,1)}, u32[]{:S(2)}, u32[]{:S(2)}) %collective-permute-start.39) | collective-permute-done | bytes 524320 | tf_op jit(solution)/shard_map/ppermute | solution.py:40
  248.7 9.8 %shard_map.190 = (bf16[1024,256]{1,0:T(8,128)(2,1)S(1)}, bf16[1024,256]{1,0:T(8,128)(2,1)S(1)}, bf16[1024,256]{1,0:T(8,128)(2,1)S(1)}, bf16[1024,256]{1,0:T(8,128)(2,1)S(1)}) custom-call(s32[5]{0:T(128)S(1)} %pad_add_fusion.scalars_ref, bf16[256,1024]{1,0:T(8,128)(2,1)} %get-tuple-element.130.refs_0_.refs_11_, ...), custom_call_target="tpu_custom_call" | custom-call | flops 1 | bytes 1 | tf_op jit(solution)/shard_map/pallas_call | solution.py:112
  259.7 3.7 collective-permute-start.42
  265.8 3.8 collective-permute-start.47
  269.6 3.9 collective-permute-done.43.refs_2_.refs_3_.refs_5_
  274.2 3.8 collective-permute-start.44
  279.3 3.4 collective-permute-done.46
  282.7 5.6 collective-permute-done.47
  288.7 5.6 collective-permute-done.44.refs_3_
  295.4 3.8 collective-permute-start.48
  299.1 6.4 collective-permute-done.49.refs_8_.refs_0_.refs_4_
  305.5 3.7 collective-permute-start.50
  309.2 7.5 %collective-permute-done.52.refs_0_.refs_2_ = bf16[256,1024]{1,0:T(8,128)(2,1)S(1)} collective-permute-done((bf16[256,1024]{1,0:T(8,128)(2,1)S(1)}, bf16[256,1024]{1,0:T(8,128)(2,1)S(1)}, u32[]{:S(2)}, u32[]{:S(2)}) %collective-permute-start.52) | collective-permute-done | bytes 524320 | tf_op jit(solution)/shard_map/ppermute | solution.py:40
  318.8 4.1 shard_map.194
  322.9 4.4 shard_map.195
  330.0 4.6 shard_map.197
  334.6 4.6 shard_map.198
  341.1 11.8 %collective-permute-done.55.refs_5_ = bf16[256,1024]{1,0:T(8,128)(2,1)S(1)} collective-permute-done((bf16[256,1024]{1,0:T(8,128)(2,1)S(1)}, bf16[256,1024]{1,0:T(8,128)(2,1)S(1)}, u32[]{:S(2)}, u32[]{:S(2)}) %collective-permute-start.55) | collective-permute-done | bytes 524320 | tf_op jit(solution)/shard_map/ppermute | solution.py:40
  360.3 5.6 collective-permute-done.60.refs_3_
  371.8 7.1 collective-permute-done.62.refs_2_.refs_4_
  384.2 17.1 %shard_map.204 = (f32[256,1024]{1,0:T(8,128)S(1)}, f32[256,1024]{1,0:T(8,128)S(1)}, bf16[2,256,1024]{2,1,0:T(8,128)(2,1)S(1)}, bf16[1024,768]{1,0:T(8,128)(2,1)S(1)}, f32[1024,256]{1,0:T(8,128)S(1)}) custom-call(s32[5]{0:T(128)S(1)} %pad_add_fusion.scalars_ref, bf16[256,1024]{1,0:T(8,128)(2,1)S(1)} %get-tuple-element.158.refs_0_.refs_2_, ...), custom_call_target="tpu_custom_call" | custom-call | flops 1 | bytes 1 | tf_op jit(solution)/shard_map/pallas_call | solution.py:112
  408.2 3.6 shard_map.206
  412.7 10.0 %collective-permute-done.67.refs_3_ = bf16[4,704,128]{2,1,0:T(8,128)(2,1)S(1)} collective-permute-done((bf16[4,704,128]{2,1,0:T(8,128)(2,1)S(1)}, bf16[4,704,128]{2,1,0:T(8,128)(2,1)S(1)}, u32[]{:S(2)}, u32[]{:S(2)}) %collective-permute-start.67) | collective-permute-done | bytes 720928 | tf_op jit(solution)/shard_map/ppermute | solution.py:44
  434.9 4.1 collective-permute-done.66.refs_3_
  446.4 8.1 %collective-permute-done.71.refs_0_.refs_4_ = bf16[256,1024]{1,0:T(8,128)(2,1)} collective-permute-done((bf16[256,1024]{1,0:T(8,128)(2,1)}, bf16[256,1024]{1,0:T(8,128)(2,1)}, u32[]{:S(2)}, u32[]{:S(2)}) %collective-permute-start.71) | collective-permute-done | bytes 524320 | tf_op jit(solution)/shard_map/ppermute | solution.py:40
  457.0 3.3 collective-permute-done.69.refs_1_
  465.4 5.0 shard_map.211
  473.2 6.0 shard_map.212
  491.4 3.4 shard_map.214
  494.8 8.0 %collective-permute-done.76.refs_1_ = bf16[352,1024]{1,0:T(8,128)(2,1)S(1)} collective-permute-done((bf16[352,1024]{1,0:T(8,128)(2,1)}, bf16[352,1024]{1,0:T(8,128)(2,1)S(1)}, u32[]{:S(2)}, u32[]{:S(2)}) %collective-permute-start.76) | collective-permute-done | bytes 720928 | tf_op jit(solution)/shard_map/ppermute | solution.py:44
  503.5 4.8 collective-permute-done.75.refs_1_
  509.0 4.4 shard_map.217
  518.6 13.1 %collective-permute-done.101 = bf16[2,1,32,1024]{3,2,0,1:T(8,128)(2,1)S(1)} collective-permute-done((bf16[2,1,32,1024]{3,2,0,1:T(8,128)(2,1)S(1)}, bf16[2,1,32,1024]{3,2,0,1:T(8,128)(2,1)S(1)}, u32[]{:S(2)}, u32[]{:S(2)}) %collective-permute-start.101) | collective-permute-done | bytes 131104 | tf_op jit(solution)/shard_map/ppermute | solution.py:40
  537.0 3.5 shard_map.219
  543.6 19.1 %shard_map.220 = (f32[256,1024]{1,0:T(8,128)S(1)}, f32[256,1024]{1,0:T(8,128)S(1)}, bf16[2,256,1024]{2,1,0:T(8,128)(2,1)}, bf16[1024,768]{1,0:T(8,128)(2,1)S(1)}, f32[1024,256]{1,0:T(8,128)S(1)}) custom-call(s32[5]{0:T(128)S(1)} %pad_add_fusion.scalars_ref, bf16[256,1024]{1,0:T(8,128)(2,1)} %get-tuple-element.194.refs_0_.refs_2_, ...), custom_call_target="tpu_custom_call" | custom-call | flops 1 | bytes 1 | tf_op jit(solution)/shard_map/pallas_call | solution.py:112
  575.8 3.5 collective-permute-start.57
  579.3 3.3 shard_map.222
  606.2 3.8 collective-permute-start.84
  614.6 8.7 %collective-permute-done.93.refs_1_ = bf16[352,1024]{1,0:T(8,128)(2,1)} collective-permute-done((bf16[352,1024]{1,0:T(8,128)(2,1)}, bf16[352,1024]{1,0:T(8,128)(2,1)}, u32[]{:S(2)}, u32[]{:S(2)}) %collective-permute-start.93) | collective-permute-done | bytes 720928 | tf_op jit(solution)/shard_map/ppermute | solution.py:44
  624.6 5.9 collective-permute-done.92.refs_1_
  642.7 4.0 collective-permute-start.87
  646.8 4.3 collective-permute-done.85
  654.9 6.7 collective-permute-start.89
  663.9 5.1 collective-permute-done.89
  684.3 26.2 %collective-permute-done.109 = bf16[128,1024]{1,0:T(8,128)(2,1)S(1)} collective-permute-done((bf16[128,1024]{1,0:T(8,128)(2,1)S(1)}, bf16[128,1024]{1,0:T(8,128)(2,1)S(1)}, u32[]{:S(2)}, u32[]{:S(2)}) %collective-permute-start.109) | collective-permute-done | bytes 262176 | tf_op jit(solution)/shard_map/ppermute | solution.py:774
  710.5 8.0 %collective-permute-done.110 = bf16[128,1024]{1,0:T(8,128)(2,1)} collective-permute-done((bf16[128,1024]{1,0:T(8,128)(2,1)S(1)}, bf16[128,1024]{1,0:T(8,128)(2,1)}, u32[]{:S(2)}, u32[]{:S(2)}) %collective-permute-start.110) | collective-permute-done | bytes 262176 | tf_op jit(solution)/shard_map/ppermute | solution.py:774
  720.8 3.4 collective-permute-start.104
  725.3 4.5 collective-permute-start.106
  (778 shorter events, 312.2 us)
Async XLA Ops:
  7.2 65.3 %all-gather.11.cloned.1.call-start = ((), (), s32[]{:S(2)}) async-start(), calls=%async_computation.10 | async-start | bytes 1310720 | tf_op jit(solution)/shard_map/all_gather | solution.py:778
  8.7 24.1 %collective-permute-start.5 = (f32[4,32]{1,0:T(4,128)S(1)}, f32[4,32]{1,0:T(4,128)S(1)}, u32[]{:S(2)}, u32[]{:S(2)}) collective-permute-start(f32[4,32]{1,0:T(4,128)S(1)} %maximum_convert_fusion.6), channel_id=1, source_target_pairs={{0,8},{8,0},{16,24},{24,16},{1,9},{9,1},{17,25},{25,17},{2,10},{10... | collective-permute-start | bytes 1544 | tf_op jit(solution)/shard_map/ppermute | solution.py:81
  9.0 24.0 %collective-permute-start.6 = (f32[4,32]{1,0:T(4,128)S(1)}, f32[4,32]{1,0:T(4,128)S(1)}, u32[]{:S(2)}, u32[]{:S(2)}) collective-permute-start(f32[4,32]{1,0:T(4,128)S(1)} %maximum_convert_fusion.6), channel_id=1, source_target_pairs={{0,16},{8,24},{16,0},{24,8},{1,17},{9,25},{17,1},{25,9},{2,18},{10... | collective-permute-start | bytes 1544 | tf_op jit(solution)/shard_map/ppermute | solution.py:81
  11.3 21.7 %collective-permute-start.7 = (f32[4,32]{1,0:T(4,128)S(1)}, f32[4,32]{1,0:T(4,128)S(1)}, u32[]{:S(2)}, u32[]{:S(2)}) collective-permute-start(f32[4,32]{1,0:T(4,128)S(1)} %maximum_convert_fusion.6), channel_id=1, source_target_pairs={{0,24},{8,16},{16,8},{24,0},{1,25},{9,17},{17,9},{25,1},{2,26},{10... | collective-permute-start | bytes 1544 | tf_op jit(solution)/shard_map/ppermute | solution.py:81
  12.6 27.5 %collective-permute-start.3 = (bf16[128,1024]{1,0:T(8,128)(2,1)S(1)}, bf16[128,1024]{1,0:T(8,128)(2,1)S(1)}, u32[]{:S(2)}, u32[]{:S(2)}) collective-permute-start(bf16[128,1024]{1,0:T(8,128)(2,1)S(1)} %get-tuple-element.241), channel_id=1, source_target_pairs={{0,0},{1,8},{2,16},{3,24},{4,4},{5,12},{6,20},{7,28},{8,1},{9,9},{... | collective-permute-start | bytes 786440 | tf_op jit(solution)/shard_map/ppermute | solution.py:767
  28.1 14.7 %collective-permute-start.4 = (bf16[128,1024]{1,0:T(8,128)(2,1)S(1)}, bf16[128,1024]{1,0:T(8,128)(2,1)S(1)}, u32[]{:S(2)}, u32[]{:S(2)}) collective-permute-start(bf16[128,1024]{1,0:T(8,128)(2,1)S(1)} %get-tuple-element.242), channel_id=1, source_target_pairs={{0,4},{1,12},{2,20},{3,28},{4,0},{5,8},{6,16},{7,24},{8,5},{9,13},... | collective-permute-start | bytes 786440 | tf_op jit(solution)/shard_map/ppermute | solution.py:767
  43.6 90.7 %all-gather.13.cloned.1.call-start = ((), (), s32[]{:S(2)}) async-start(), calls=%async_computation.11 | async-start | bytes 1802240 | tf_op jit(solution)/shard_map/all_gather | solution.py:778
  61.8 90.2 %all-gather.15.cloned.1.call-start = ((), (), s32[]{:S(2)}) async-start(), calls=%async_computation.12 | async-start | bytes 1802240 | tf_op jit(solution)/shard_map/all_gather | solution.py:778
  62.7 111.3 %all-gather.17.cloned.1.call-start = ((), (), s32[]{:S(2)}) async-start(), calls=%async_computation.13 | async-start | bytes 1310720 | tf_op jit(solution)/shard_map/all_gather | solution.py:778
  79.5 23.5 %collective-permute-start.14 = (bf16[4,128,768]{2,1,0:T(8,128)(2,1)S(1)}, bf16[4,128,768]{2,1,0:T(8,128)(2,1)S(1)}, u32[]{:S(2)}, u32[]{:S(2)}) collective-permute-start(bf16[4,128,768]{2,1,0:T(8,128)(2,1)S(1)} %slice.190), channel_id=1, source_target_pairs={{0,4},{4,0},{1,5},{5,1},{2,6},{6,2},{3,7},{7,3},{8,12},{12,8},{9,1... | collective-permute-start | bytes 2359304 | tf_op jit(solution)/shard_map/ppermute | solution.py:44
  84.9 18.0 %collective-permute-start.11 = (bf16[256,1024]{1,0:T(8,128)(2,1)S(1)}, bf16[256,1024]{1,0:T(8,128)(2,1)S(1)}, u32[]{:S(2)}, u32[]{:S(2)}) collective-permute-start(bf16[256,1024]{1,0:T(8,128)(2,1)S(1)} %get-tuple-element.114.refs_1_.refs_0_), channel_id=1, source_target_pairs={{0,1},{1,0},{2,3},{3,2},{4,5},{5,4},{6,7},{7,6},{8,9},{9,8},{10,11... | collective-permute-start | bytes 1572872 | tf_op jit(solution)/shard_map/ppermute | solution.py:36
  126.9 112.4 %all-gather.19.cloned.1.call-start = ((), (), s32[]{:S(2)}) async-start(), calls=%async_computation.14 | async-start | bytes 1802240 | tf_op jit(solution)/shard_map/all_gather | solution.py:778
  134.4 50.5 %collective-permute-start.25 = (bf16[4,704,256]{2,1,0:T(8,128)(2,1)}, bf16[4,704,256]{2,1,0:T(8,128)(2,1)S(1)}, u32[]{:S(2)}, u32[]{:S(2)}) collective-permute-start(bf16[4,704,256]{2,1,0:T(8,128)(2,1)} %bitcast.291), channel_id=1, source_target_pairs={{0,4},{4,0},{1,5},{5,1},{2,6},{6,2},{3,7},{7,3},{8,12},{12,8},{9,1... | collective-permute-start | bytes 4325384 | tf_op jit(solution)/shard_map/ppermute | solution.py:44
  149.2 28.3 %collective-permute-start.30 = (bf16[256,1024]{1,0:T(8,128)(2,1)}, bf16[256,1024]{1,0:T(8,128)(2,1)}, u32[]{:S(2)}, u32[]{:S(2)}) collective-permute-start(bf16[256,1024]{1,0:T(8,128)(2,1)} %get-tuple-element.122.refs_1_.refs_0_), channel_id=1, source_target_pairs={{0,2},{2,0},{1,3},{3,1},{4,6},{6,4},{5,7},{7,5},{8,10},{10,8},{9,1... | collective-permute-start | bytes 1572872 | tf_op jit(solution)/shard_map/ppermute | solution.py:40
  150.8 15.1 %collective-permute-start.27 = (bf16[2,2,32,704]{3,2,1,0:T(8,128)(2,1)S(1)}, bf16[2,2,32,704]{3,2,1,0:T(8,128)(2,1)S(1)}, u32[]{:S(2)}, u32[]{:S(2)}) collective-permute-start(bf16[2,2,32,704]{3,2,1,0:T(8,128)(2,1)S(1)} %get-tuple-element.254), channel_id=1, source_target_pairs={{0,2},{2,0},{1,3},{3,1},{4,6},{6,4},{5,7},{7,5},{8,10},{10,8},{9,1... | collective-permute-start | bytes 540680 | tf_op jit(solution)/shard_map/ppermute | solution.py:40
  154.6 28.2 %collective-permute-start.26 = (bf16[352,1024]{1,0:T(8,128)(2,1)}, bf16[352,1024]{1,0:T(8,128)(2,1)}, u32[]{:S(2)}, u32[]{:S(2)}) collective-permute-start(bf16[352,1024]{1,0:T(8,128)(2,1)} %bitcast.66.refs_4_.refs_6_), channel_id=1, source_target_pairs={{0,4},{4,0},{1,5},{5,1},{2,6},{6,2},{3,7},{7,3},{8,12},{12,8},{9,1... | collective-permute-start | bytes 2162696 | tf_op jit(solution)/shard_map/ppermute | solution.py:44
  178.6 452.5 %reduce-scatter.8.cloned.1.call-start = ((), (), s32[]{:S(2)}) async-start(), calls=%async_computation.6 | async-start | bytes 1802240 | tf_op jit(solution)/shard_map/reduce_scatter | solution.py:97
  180.5 26.8 %collective-permute-start.33 = (bf16[4,128,768]{2,1,0:T(8,128)(2,1)S(1)}, bf16[4,128,768]{2,1,0:T(8,128)(2,1)S(1)}, u32[]{:S(2)}, u32[]{:S(2)}) collective-permute-start(bf16[4,128,768]{2,1,0:T(8,128)(2,1)S(1)} %slice.194), channel_id=1, source_target_pairs={{0,4},{4,0},{1,5},{5,1},{2,6},{6,2},{3,7},{7,3},{8,12},{12,8},{9,1... | collective-permute-start | bytes 2359304 | tf_op jit(solution)/shard_map/ppermute | solution.py:44
  225.8 16.8 %collective-permute-start.41 = (bf16[352,1024]{1,0:T(8,128)(2,1)}, bf16[352,1024]{1,0:T(8,128)(2,1)}, u32[]{:S(2)}, u32[]{:S(2)}) collective-permute-start(bf16[352,1024]{1,0:T(8,128)(2,1)} %bitcast.92.refs_4_.refs_6_), channel_id=1, source_target_pairs={{0,4},{4,0},{1,5},{5,1},{2,6},{6,2},{3,7},{7,3},{8,12},{12,8},{9,1... | collective-permute-start | bytes 2162696 | tf_op jit(solution)/shard_map/ppermute | solution.py:44
  227.0 15.7 %collective-permute-start.38 = (bf16[256,1024]{1,0:T(8,128)(2,1)}, bf16[256,1024]{1,0:T(8,128)(2,1)}, u32[]{:S(2)}, u32[]{:S(2)}) collective-permute-start(bf16[256,1024]{1,0:T(8,128)(2,1)} %get-tuple-element.130.refs_0_.refs_11_), channel_id=1, source_target_pairs={{0,1},{1,0},{2,3},{3,2},{4,5},{5,4},{6,7},{7,6},{8,9},{9,8},{10,11... | collective-permute-start | bytes 1572872 | tf_op jit(solution)/shard_map/ppermute | solution.py:36
  239.3 34.2 %collective-permute-start.43 = (bf16[4,704,256]{2,1,0:T(8,128)(2,1)}, bf16[4,704,256]{2,1,0:T(8,128)(2,1)S(1)}, u32[]{:S(2)}, u32[]{:S(2)}) collective-permute-start(bf16[4,704,256]{2,1,0:T(8,128)(2,1)} %bitcast.285), channel_id=1, source_target_pairs={{0,4},{4,0},{1,5},{5,1},{2,6},{6,2},{3,7},{7,3},{8,12},{12,8},{9,1... | collective-permute-start | bytes 4325384 | tf_op jit(solution)/shard_map/ppermute | solution.py:44
  263.5 19.2 %collective-permute-start.46 = (bf16[128,1024]{1,0:T(8,128)(2,1)S(1)}, bf16[128,1024]{1,0:T(8,128)(2,1)S(1)}, u32[]{:S(2)}, u32[]{:S(2)}) collective-permute-start(bf16[128,1024]{1,0:T(8,128)(2,1)S(1)} %get-tuple-element.239), channel_id=1, source_target_pairs={{0,0},{1,8},{2,16},{3,24},{4,4},{5,12},{6,20},{7,28},{8,1},{9,9},{... | collective-permute-start | bytes 786440 | tf_op jit(solution)/shard_map/ppermute | solution.py:767
  265.8 22.5 %collective-permute-start.47 = (bf16[128,1024]{1,0:T(8,128)(2,1)S(1)}, bf16[128,1024]{1,0:T(8,128)(2,1)S(1)}, u32[]{:S(2)}, u32[]{:S(2)}) collective-permute-start(bf16[128,1024]{1,0:T(8,128)(2,1)S(1)} %get-tuple-element.240), channel_id=1, source_target_pairs={{0,4},{1,12},{2,20},{3,28},{4,0},{5,8},{6,16},{7,24},{8,5},{9,13},... | collective-permute-start | bytes 786440 | tf_op jit(solution)/shard_map/ppermute | solution.py:767
  274.2 20.1 %collective-permute-start.44 = (bf16[256,1024]{1,0:T(8,128)(2,1)S(1)}, bf16[256,1024]{1,0:T(8,128)(2,1)S(1)}, u32[]{:S(2)}, u32[]{:S(2)}) collective-permute-start(bf16[256,1024]{1,0:T(8,128)(2,1)S(1)} %shard_map.192.refs_5_), channel_id=1, source_target_pairs={{0,2},{2,0},{1,3},{3,1},{4,6},{6,4},{5,7},{7,5},{8,10},{10,8},{9,1... | collective-permute-start | bytes 1572872 | tf_op jit(solution)/shard_map/ppermute | solution.py:40
  288.6 16.9 %collective-permute-start.49 = (bf16[256,1024]{1,0:T(8,128)(2,1)S(1)}, bf16[256,1024]{1,0:T(8,128)(2,1)S(1)}, u32[]{:S(2)}, u32[]{:S(2)}) collective-permute-start(bf16[256,1024]{1,0:T(8,128)(2,1)S(1)} %get-tuple-element.220.refs_6_.refs_0_.refs_2_), channel_id=1, source_target_pairs={{0,2},{2,0},{1,3},{3,1},{4,6},{6,4},{5,7},{7,5},{8,10},{10,8},{9,1... | collective-permute-start | bytes 1572872 | tf_op jit(solution)/shard_map/ppermute | solution.py:40
  295.3 21.4 %collective-permute-start.52 = (bf16[256,1024]{1,0:T(8,128)(2,1)S(1)}, bf16[256,1024]{1,0:T(8,128)(2,1)S(1)}, u32[]{:S(2)}, u32[]{:S(2)}) collective-permute-start(bf16[256,1024]{1,0:T(8,128)(2,1)S(1)} %get-tuple-element.136.refs_0_.refs_10_), channel_id=1, source_target_pairs={{0,2},{2,0},{1,3},{3,1},{4,6},{6,4},{5,7},{7,5},{8,10},{10,8},{9,1... | collective-permute-start | bytes 1572872 | tf_op jit(solution)/shard_map/ppermute | solution.py:40
  295.4 23.4 %collective-permute-start.48 = (bf16[256,1024]{1,0:T(8,128)(2,1)S(1)}, bf16[256,1024]{1,0:T(8,128)(2,1)S(1)}, u32[]{:S(2)}, u32[]{:S(2)}) collective-permute-start(bf16[256,1024]{1,0:T(8,128)(2,1)S(1)} %get-tuple-element.220.refs_6_.refs_0_.refs_2_), channel_id=1, source_target_pairs={{0,1},{1,0},{2,3},{3,2},{4,5},{5,4},{6,7},{7,6},{8,9},{9,8},{10,11... | collective-permute-start | bytes 1572872 | tf_op jit(solution)/shard_map/ppermute | solution.py:36
  339.8 20.6 %collective-permute-start.58 = (bf16[256,1024]{1,0:T(8,128)(2,1)S(1)}, bf16[256,1024]{1,0:T(8,128)(2,1)S(1)}, u32[]{:S(2)}, u32[]{:S(2)}) collective-permute-start(bf16[256,1024]{1,0:T(8,128)(2,1)S(1)} %get-tuple-element.146), channel_id=1, source_target_pairs={{0,1},{1,0},{2,3},{3,2},{4,5},{5,4},{6,7},{7,6},{8,9},{9,8},{10,11... | collective-permute-start | bytes 1572872 | tf_op jit(solution)/shard_map/ppermute | solution.py:36
  368.2 15.9 %collective-permute-start.64 = (bf16[4,704,128]{2,1,0:T(8,128)(2,1)S(1)}, bf16[4,704,128]{2,1,0:T(8,128)(2,1)S(1)}, u32[]{:S(2)}, u32[]{:S(2)}) collective-permute-start(bf16[4,704,128]{2,1,0:T(8,128)(2,1)S(1)} %get-tuple-element.155.refs_6_), channel_id=1, source_target_pairs={{0,4},{4,0},{1,5},{5,1},{2,6},{6,2},{3,7},{7,3},{8,12},{12,8},{9,1... | collective-permute-start | bytes 2162696 | tf_op jit(solution)/shard_map/ppermute | solution.py:44
  369.4 14.8 %collective-permute-start.61 = (bf16[256,1024]{1,0:T(8,128)(2,1)S(1)}, bf16[256,1024]{1,0:T(8,128)(2,1)S(1)}, u32[]{:S(2)}, u32[]{:S(2)}) collective-permute-start(bf16[256,1024]{1,0:T(8,128)(2,1)S(1)} %get-tuple-element.158.refs_0_.refs_2_), channel_id=1, source_target_pairs={{0,1},{1,0},{2,3},{3,2},{4,5},{5,4},{6,7},{7,6},{8,9},{9,8},{10,11... | collective-permute-start | bytes 1572872 | tf_op jit(solution)/shard_map/ppermute | solution.py:36
  404.9 17.8 %collective-permute-start.67 = (bf16[4,704,128]{2,1,0:T(8,128)(2,1)S(1)}, bf16[4,704,128]{2,1,0:T(8,128)(2,1)S(1)}, u32[]{:S(2)}, u32[]{:S(2)}) collective-permute-start(bf16[4,704,128]{2,1,0:T(8,128)(2,1)S(1)} %get-tuple-element.163.refs_13_), channel_id=1, source_target_pairs={{0,4},{4,0},{1,5},{5,1},{2,6},{6,2},{3,7},{7,3},{8,12},{12,8},{9,1... | collective-permute-start | bytes 2162696 | tf_op jit(solution)/shard_map/ppermute | solution.py:44
  425.6 207.1 %reduce-scatter.6.cloned.1.call-start = ((), (), s32[]{:S(2)}) async-start(), calls=%async_computation.5 | async-start | bytes 983040 | tf_op jit(solution)/shard_map/reduce_scatter | solution.py:97
  443.2 17.2 %collective-permute-start.69 = (bf16[4,128,768]{2,1,0:T(8,128)(2,1)S(1)}, bf16[4,128,768]{2,1,0:T(8,128)(2,1)S(1)}, u32[]{:S(2)}, u32[]{:S(2)}) collective-permute-start(bf16[4,128,768]{2,1,0:T(8,128)(2,1)S(1)} %copy-done.128), channel_id=1, source_target_pairs={{0,4},{4,0},{1,5},{5,1},{2,6},{6,2},{3,7},{7,3},{8,12},{12,8},{9,1... | collective-permute-start | bytes 2359304 | tf_op jit(solution)/shard_map/ppermute | solution.py:44
  444.3 17.6 %collective-permute-start.68 = (bf16[256,1024]{1,0:T(8,128)(2,1)}, bf16[256,1024]{1,0:T(8,128)(2,1)}, u32[]{:S(2)}, u32[]{:S(2)}) collective-permute-start(bf16[256,1024]{1,0:T(8,128)(2,1)} %get-tuple-element.174.refs_0_.refs_2_), channel_id=1, source_target_pairs={{0,1},{1,0},{2,3},{3,2},{4,5},{5,4},{6,7},{7,6},{8,9},{9,8},{10,11... | collective-permute-start | bytes 1572872 | tf_op jit(solution)/shard_map/ppermute | solution.py:36
  454.5 18.6 %collective-permute-start.72 = (bf16[256,1024]{1,0:T(8,128)(2,1)}, bf16[256,1024]{1,0:T(8,128)(2,1)}, u32[]{:S(2)}, u32[]{:S(2)}) collective-permute-start(bf16[256,1024]{1,0:T(8,128)(2,1)} %collective-permute-done.71.refs_0_.refs_4_), channel_id=1, source_target_pairs={{0,1},{1,0},{2,3},{3,2},{4,5},{5,4},{6,7},{7,6},{8,9},{9,8},{10,11... | collective-permute-start | bytes 1572872 | tf_op jit(solution)/shard_map/ppermute | solution.py:36
  484.7 18.1 %collective-permute-start.76 = (bf16[352,1024]{1,0:T(8,128)(2,1)}, bf16[352,1024]{1,0:T(8,128)(2,1)S(1)}, u32[]{:S(2)}, u32[]{:S(2)}) collective-permute-start(bf16[352,1024]{1,0:T(8,128)(2,1)} %get-tuple-element.156.refs_6_), channel_id=1, source_target_pairs={{0,4},{4,0},{1,5},{5,1},{2,6},{6,2},{3,7},{7,3},{8,12},{12,8},{9,1... | collective-permute-start | bytes 2162696 | tf_op jit(solution)/shard_map/ppermute | solution.py:44
  485.9 149.0 %reduce-scatter.12.cloned.1.call-start = ((), (), s32[]{:S(2)}) async-start(), calls=%async_computation.8 | async-start | bytes 1228800 | tf_op jit(solution)/shard_map/reduce_scatter | solution.py:97
  486.0 27.4 %collective-permute-start.70 = (bf16[256,1024]{1,0:T(8,128)(2,1)}, bf16[256,1024]{1,0:T(8,128)(2,1)S(1)}, u32[]{:S(2)}, u32[]{:S(2)}) collective-permute-start(bf16[256,1024]{1,0:T(8,128)(2,1)} %copy-done.164), channel_id=1, source_target_pairs={{0,1},{1,0},{2,3},{3,2},{4,5},{5,4},{6,7},{7,6},{8,9},{9,8},{10,11... | collective-permute-start | bytes 1572872 | tf_op jit(solution)/shard_map/ppermute | solution.py:36
  489.5 23.9 %collective-permute-start.74 = (bf16[256,1024]{1,0:T(8,128)(2,1)S(1)}, bf16[256,1024]{1,0:T(8,128)(2,1)S(1)}, u32[]{:S(2)}, u32[]{:S(2)}) collective-permute-start(bf16[256,1024]{1,0:T(8,128)(2,1)S(1)} %shard_map.213.refs_6_), channel_id=1, source_target_pairs={{0,2},{2,0},{1,3},{3,1},{4,6},{6,4},{5,7},{7,5},{8,10},{10,8},{9,1... | collective-permute-start | bytes 1572872 | tf_op jit(solution)/shard_map/ppermute | solution.py:40
  490.2 18.1 %collective-permute-start.75 = (bf16[128,1024]{1,0:T(8,128)(2,1)S(1)}, bf16[128,1024]{1,0:T(8,128)(2,1)S(1)}, u32[]{:S(2)}, u32[]{:S(2)}) collective-permute-start(bf16[128,1024]{1,0:T(8,128)(2,1)S(1)} %copy-done.146), channel_id=1, source_target_pairs={{0,4},{4,0},{1,5},{5,1},{2,6},{6,2},{3,7},{7,3},{8,12},{12,8},{9,1... | collective-permute-start | bytes 786440 | tf_op jit(solution)/shard_map/ppermute | solution.py:44
  515.9 17.5 %collective-permute-start.78 = (bf16[256,1024]{1,0:T(8,128)(2,1)}, bf16[256,1024]{1,0:T(8,128)(2,1)}, u32[]{:S(2)}, u32[]{:S(2)}) collective-permute-start(bf16[256,1024]{1,0:T(8,128)(2,1)} %get-tuple-element.194.refs_0_.refs_2_), channel_id=1, source_target_pairs={{0,2},{2,0},{1,3},{3,1},{4,6},{6,4},{5,7},{7,5},{8,10},{10,8},{9,1... | collective-permute-start | bytes 1572872 | tf_op jit(solution)/shard_map/ppermute | solution.py:40
  516.5 15.1 %collective-permute-start.101 = (bf16[2,1,32,1024]{3,2,0,1:T(8,128)(2,1)S(1)}, bf16[2,1,32,1024]{3,2,0,1:T(8,128)(2,1)S(1)}, u32[]{:S(2)}, u32[]{:S(2)}) collective-permute-start(bf16[2,1,32,1024]{3,2,0,1:T(8,128)(2,1)S(1)} %get-tuple-element.274), channel_id=1, source_target_pairs={{0,2},{2,0},{1,3},{3,1},{4,6},{6,4},{5,7},{7,5},{8,10},{10,8},{9,1... | collective-permute-start | bytes 393224 | tf_op jit(solution)/shard_map/ppermute | solution.py:40
  517.4 24.0 %collective-permute-start.80 = (bf16[4,704,128]{2,1,0:T(8,128)(2,1)}, bf16[4,704,128]{2,1,0:T(8,128)(2,1)}, u32[]{:S(2)}, u32[]{:S(2)}) collective-permute-start(bf16[4,704,128]{2,1,0:T(8,128)(2,1)} %get-tuple-element.191.refs_2_), channel_id=1, source_target_pairs={{0,4},{4,0},{1,5},{5,1},{2,6},{6,2},{3,7},{7,3},{8,12},{12,8},{9,1... | collective-permute-start | bytes 2162696 | tf_op jit(solution)/shard_map/ppermute | solution.py:44
  536.4 145.6 %reduce-scatter.14.cloned.1.call-start = ((), (), s32[]{:S(2)}) async-start(), calls=%async_computation.9 | async-start | bytes 1802240 | tf_op jit(solution)/shard_map/reduce_scatter | solution.py:97
  566.2 17.9 %collective-permute-start.83 = (bf16[4,704,128]{2,1,0:T(8,128)(2,1)}, bf16[4,704,128]{2,1,0:T(8,128)(2,1)}, u32[]{:S(2)}, u32[]{:S(2)}) collective-permute-start(bf16[4,704,128]{2,1,0:T(8,128)(2,1)} %get-tuple-element.199.refs_14_), channel_id=1, source_target_pairs={{0,4},{4,0},{1,5},{5,1},{2,6},{6,2},{3,7},{7,3},{8,12},{12,8},{9,1... | collective-permute-start | bytes 2162696 | tf_op jit(solution)/shard_map/ppermute | solution.py:44
  570.6 19.7 %collective-permute-start.82 = (bf16[256,1024]{1,0:T(8,128)(2,1)S(1)}, bf16[256,1024]{1,0:T(8,128)(2,1)}, u32[]{:S(2)}, u32[]{:S(2)}) collective-permute-start(bf16[256,1024]{1,0:T(8,128)(2,1)S(1)} %shard_map.221.refs_5_), channel_id=1, source_target_pairs={{0,2},{2,0},{1,3},{3,1},{4,6},{6,4},{5,7},{7,5},{8,10},{10,8},{9,1... | collective-permute-start | bytes 1572872 | tf_op jit(solution)/shard_map/ppermute | solution.py:40
  573.0 27.8 %collective-permute-start.56 = (bf16[128,1024]{1,0:T(8,128)(2,1)}, bf16[128,1024]{1,0:T(8,128)(2,1)}, u32[]{:S(2)}, u32[]{:S(2)}) collective-permute-start(bf16[128,1024]{1,0:T(8,128)(2,1)} %get-tuple-element.237), channel_id=1, source_target_pairs={{0,0},{8,1},{16,2},{24,3},{4,4},{12,5},{20,6},{28,7},{1,8},{9,9},{... | collective-permute-start | bytes 786440 | tf_op jit(solution)/shard_map/ppermute | solution.py:774
  575.8 25.1 %collective-permute-start.57 = (bf16[128,1024]{1,0:T(8,128)(2,1)}, bf16[128,1024]{1,0:T(8,128)(2,1)}, u32[]{:S(2)}, u32[]{:S(2)}) collective-permute-start(bf16[128,1024]{1,0:T(8,128)(2,1)} %get-tuple-element.238), channel_id=1, source_target_pairs={{4,0},{12,1},{20,2},{28,3},{0,4},{8,5},{16,6},{24,7},{5,8},{13,9},... | collective-permute-start | bytes 786440 | tf_op jit(solution)/shard_map/ppermute | solution.py:774
  583.6 26.4 %collective-permute-start.86 = (bf16[4,128,768]{2,1,0:T(8,128)(2,1)}, bf16[4,128,768]{2,1,0:T(8,128)(2,1)}, u32[]{:S(2)}, u32[]{:S(2)}) collective-permute-start(bf16[4,128,768]{2,1,0:T(8,128)(2,1)} %get-tuple-element.207.refs_4_), channel_id=1, source_target_pairs={{0,4},{4,0},{1,5},{5,1},{2,6},{6,2},{3,7},{7,3},{8,12},{12,8},{9,1... | collective-permute-start | bytes 2359304 | tf_op jit(solution)/shard_map/ppermute | solution.py:44
  597.1 26.2 %collective-permute-start.93 = (bf16[352,1024]{1,0:T(8,128)(2,1)}, bf16[352,1024]{1,0:T(8,128)(2,1)}, u32[]{:S(2)}, u32[]{:S(2)}) collective-permute-start(bf16[352,1024]{1,0:T(8,128)(2,1)} %get-tuple-element.192.refs_6_), channel_id=1, source_target_pairs={{0,4},{4,0},{1,5},{5,1},{2,6},{6,2},{3,7},{7,3},{8,12},{12,8},{9,1... | collective-permute-start | bytes 2162696 | tf_op jit(solution)/shard_map/ppermute | solution.py:44
  598.3 131.6 %reduce-scatter.10.cloned.1.call-start = ((), (), s32[]{:S(2)}) async-start(), calls=%async_computation.7 | async-start | bytes 1310720 | tf_op jit(solution)/shard_map/reduce_scatter | solution.py:97
  603.1 27.4 %collective-permute-start.92 = (bf16[128,1024]{1,0:T(8,128)(2,1)S(1)}, bf16[128,1024]{1,0:T(8,128)(2,1)S(1)}, u32[]{:S(2)}, u32[]{:S(2)}) collective-permute-start(bf16[128,1024]{1,0:T(8,128)(2,1)S(1)} %copy-done.148), channel_id=1, source_target_pairs={{0,4},{4,0},{1,5},{5,1},{2,6},{6,2},{3,7},{7,3},{8,12},{12,8},{9,1... | collective-permute-start | bytes 786440 | tf_op jit(solution)/shard_map/ppermute | solution.py:44
  605.0 32.3 %collective-permute-start.100 = (f32[4,1024]{1,0:T(4,128)}, f32[4,1024]{1,0:T(4,128)}, u32[]{:S(2)}, u32[]{:S(2)}) collective-permute-start(f32[4,1024]{1,0:T(4,128)} %fusion.28), channel_id=1, source_target_pairs={{0,4},{4,0},{1,5},{5,1},{2,6},{6,2},{3,7},{7,3},{8,12},{12,8},{9,1... | collective-permute-start | bytes 49160 | tf_op jit(solution)/shard_map/ppermute | solution.py:44
  606.2 40.5 %collective-permute-start.84 = (bf16[128,1024]{1,0:T(8,128)(2,1)}, bf16[128,1024]{1,0:T(8,128)(2,1)}, u32[]{:S(2)}, u32[]{:S(2)}) collective-permute-start(bf16[128,1024]{1,0:T(8,128)(2,1)} %get-tuple-element.231), channel_id=1, source_target_pairs={{0,0},{8,1},{16,2},{24,3},{4,4},{12,5},{20,6},{28,7},{1,8},{9,9},{... | collective-permute-start | bytes 786440 | tf_op jit(solution)/shard_map/ppermute | solution.py:774
  610.0 41.1 %collective-permute-start.85 = (bf16[128,1024]{1,0:T(8,128)(2,1)}, bf16[128,1024]{1,0:T(8,128)(2,1)}, u32[]{:S(2)}, u32[]{:S(2)}) collective-permute-start(bf16[128,1024]{1,0:T(8,128)(2,1)} %get-tuple-element.232), channel_id=1, source_target_pairs={{4,0},{12,1},{20,2},{28,3},{0,4},{8,5},{16,6},{24,7},{5,8},{13,9},... | collective-permute-start | bytes 786440 | tf_op jit(solution)/shard_map/ppermute | solution.py:774
  639.5 31.4 %collective-permute-start.107 = (bf16[2,256,256]{2,1,0:T(8,128)(2,1)}, bf16[2,256,256]{2,1,0:T(8,128)(2,1)}, u32[]{:S(2)}, u32[]{:S(2)}) collective-permute-start(bf16[2,256,256]{2,1,0:T(8,128)(2,1)} %get-tuple-element.226), channel_id=1, source_target_pairs={{0,2},{2,0},{1,3},{3,1},{4,6},{6,4},{5,7},{7,5},{8,10},{10,8},{9,1... | collective-permute-start | bytes 786440 | tf_op jit(solution)/shard_map/ppermute | solution.py:40
  641.5 20.1 %collective-permute-start.96 = (bf16[2,1,32,1024]{3,2,0,1:T(8,128)(2,1)}, bf16[2,1,32,1024]{3,2,0,1:T(8,128)(2,1)}, u32[]{:S(2)}, u32[]{:S(2)}) collective-permute-start(bf16[2,1,32,1024]{3,2,0,1:T(8,128)(2,1)} %get-tuple-element.270), channel_id=1, source_target_pairs={{0,2},{2,0},{1,3},{3,1},{4,6},{6,4},{5,7},{7,5},{8,10},{10,8},{9,1... | collective-permute-start | bytes 393224 | tf_op jit(solution)/shard_map/ppermute | solution.py:40
  642.7 21.1 %collective-permute-start.87 = (bf16[128,768]{1,0:T(8,128)(2,1)}, bf16[128,768]{1,0:T(8,128)(2,1)S(1)}, u32[]{:S(2)}, u32[]{:S(2)}) collective-permute-start(bf16[128,768]{1,0:T(8,128)(2,1)} %get-tuple-element.216), channel_id=1, source_target_pairs={{0,8},{8,0},{16,24},{24,16},{1,9},{9,1},{17,25},{25,17},{2,10},{10... | collective-permute-start | bytes 589832 | tf_op jit(solution)/shard_map/ppermute | solution.py:87
  646.7 17.2 %collective-permute-start.88 = (bf16[128,768]{1,0:T(8,128)(2,1)}, bf16[128,768]{1,0:T(8,128)(2,1)S(1)}, u32[]{:S(2)}, u32[]{:S(2)}) collective-permute-start(bf16[128,768]{1,0:T(8,128)(2,1)} %get-tuple-element.218), channel_id=1, source_target_pairs={{0,16},{8,24},{16,0},{24,8},{1,17},{9,25},{17,1},{25,9},{2,18},{10... | collective-permute-start | bytes 589832 | tf_op jit(solution)/shard_map/ppermute | solution.py:87
  661.6 14.4 %collective-permute-start.95 = (bf16[2,32,768]{2,1,0:T(8,128)(2,1)S(1)}, bf16[2,32,768]{2,1,0:T(8,128)(2,1)S(1)}, u32[]{:S(2)}, u32[]{:S(2)}) collective-permute-start(bf16[2,32,768]{2,1,0:T(8,128)(2,1)S(1)} %get-tuple-element.288), channel_id=1, source_target_pairs={{0,1},{1,0},{2,3},{3,2},{4,5},{5,4},{6,7},{7,6},{8,9},{9,8},{10,11... | collective-permute-start | bytes 294920 | tf_op jit(solution)/shard_map/ppermute | solution.py:36
  678.3 32.2 %collective-permute-start.109 = (bf16[128,1024]{1,0:T(8,128)(2,1)S(1)}, bf16[128,1024]{1,0:T(8,128)(2,1)S(1)}, u32[]{:S(2)}, u32[]{:S(2)}) collective-permute-start(bf16[128,1024]{1,0:T(8,128)(2,1)S(1)} %get-tuple-element.221), channel_id=1, source_target_pairs={{0,0},{8,1},{16,2},{24,3},{4,4},{12,5},{20,6},{28,7},{1,8},{9,9},{... | collective-permute-start | bytes 786440 | tf_op jit(solution)/shard_map/ppermute | solution.py:774
  680.2 38.2 %collective-permute-start.110 = (bf16[128,1024]{1,0:T(8,128)(2,1)S(1)}, bf16[128,1024]{1,0:T(8,128)(2,1)}, u32[]{:S(2)}, u32[]{:S(2)}) collective-permute-start(bf16[128,1024]{1,0:T(8,128)(2,1)S(1)} %get-tuple-element.222), channel_id=1, source_target_pairs={{4,0},{12,1},{20,2},{28,3},{0,4},{8,5},{16,6},{24,7},{5,8},{13,9},... | collective-permute-start | bytes 786440 | tf_op jit(solution)/shard_map/ppermute | solution.py:774
  683.3 37.4 %collective-permute-start.103 = (bf16[2,2,32,704]{3,2,1,0:T(8,128)(2,1)S(1)}, bf16[2,2,32,704]{3,2,1,0:T(8,128)(2,1)S(1)}, u32[]{:S(2)}, u32[]{:S(2)}) collective-permute-start(bf16[2,2,32,704]{3,2,1,0:T(8,128)(2,1)S(1)} %bitcast.367), channel_id=1, source_target_pairs={{0,2},{2,0},{1,3},{3,1},{4,6},{6,4},{5,7},{7,5},{8,10},{10,8},{9,1... | collective-permute-start | bytes 540680 | tf_op jit(solution)/shard_map/ppermute | solution.py:40
  720.8 14.4 %collective-permute-start.104 = (bf16[2,2,32,704]{3,2,1,0:T(8,128)(2,1)S(1)}, bf16[2,2,32,704]{3,2,1,0:T(8,128)(2,1)S(1)}, u32[]{:S(2)}, u32[]{:S(2)}) collective-permute-start(bf16[2,2,32,704]{3,2,1,0:T(8,128)(2,1)S(1)} %get-tuple-element.244), channel_id=1, source_target_pairs={{0,1},{1,0},{2,3},{3,2},{4,5},{5,4},{6,7},{7,6},{8,9},{9,8},{10,11... | collective-permute-start | bytes 540680 | tf_op jit(solution)/shard_map/ppermute | solution.py:36
  (232 other events, 1665.5 us)
Sparse Core Ops, SparseCore 0:
  43.8 28.7 all-gather.10
  74.7 33.5 all-gather.12
  110.4 33.8 all-gather.14
  146.3 27.6 all-gather.16
  178.7 33.1 all-gather.18
  425.8 31.6 reduce-scatter.7
  486.0 20.0 reduce-scatter.5
  536.5 23.9 reduce-scatter.11
  598.4 50.1 reduce-scatter.13
  673.3 42.5 reduce-scatter.9

commit v4 on v3

--- a/solution.py
+++ b/solution.py
@@ -938,7 +938,6 @@
     gain_sums = rows[in_rows : in_rows + 2 * LAYERS].astype(f32)
     gain_sums = lax.dynamic_slice(gain_sums, (0, me * in_rows), (2 * LAYERS, in_rows))
     pair_1, qkv_1, rows_1 = [group.hold(one) for one in done]
-    value_grad = group.hold(value_grad)
     hand_out(1, pair_1, rows_1[:hidden_rows], qkv_1, rows_1[hidden_rows:])
     hand_out(0, pair, down, qkv, rows[:in_rows])
     pieces = value_grad.astype(bf16).reshape(group_size, local, width)

time: 757 us -> 780 us (1.030)
  waiting for transfers between devices: 278 us -> 297 us
  starting transfers between devices: 161 us -> 171 us
    ppermute x3, waiting for transfers between devices: 5.1 us -> 27.8 us  [scatter_near(): total = total + lax.ppermute(blocks[d], 'sz', pairs).astype(f32)]
    ppermute x43, starting transfers between devices: 68.4 us -> 88.6 us  [swap_core(): return lax.ppermute(value, 'fc', SWAP)]
    ppermute x3, starting transfers between devices: 10.7 us -> 0.97 us  [scatter_near(): total = total + lax.ppermute(blocks[d], 'sz', pairs).astype(f32)]
    pallas_call x56 -> x55, Pallas kernels: 161 us -> 157 us  [kernel_call(): pl.pallas_call(whole, out_shape=[shape_of(*one) for one in results], in_s...]
    unnamed x352 -> x342, local copies, waits for them, and re-layouts: 58 us -> 54.3 us
  transfers between devices with their start and end apart: 121 -> 121, of which waited for: 55 -> 52; matrix products, arithmetic and copies ran while one was open for 9% -> 9% of each run, Pallas kernels for 18% -> 17%
where the time goes in v4:
time: 780 us; the launch traced here: 773 us
  waiting for transfers between devices  297 us (38%)
  starting transfers between devices  171 us (22%)
  Pallas kernels  157 us (20%)
  local copies, waits for them, and re-layouts  99.1 us (13%)
  other arithmetic  31.9 us (4%)
  between operations  17.2 us (2%)
    pallas_call x55, Pallas kernels, kernel_call(): pl.pallas_call(whole, out_shape=[shape_of(*one) for one in results], in_s...  157 us
    ppermute x31, waiting for transfers between devices, swap_x(): return lax.ppermute(value, 'fx', SWAP)  138 us
    ppermute x43, starting transfers between devices, swap_core(): return lax.ppermute(value, 'fc', SWAP)  88.6 us
    ppermute x20, waiting for transfers between devices, swap_y(): return lax.ppermute(value, 'sy', SWAP)  59 us
    unnamed x342, local copies, waits for them, and re-layouts  54.3 us
    ppermute x6, waiting for transfers between devices, from_group(): lax.ppermute(pick(rows, (at + r) % 2), ALL, backs[r])  34.7 us
    ppermute x3, waiting for transfers between devices, scatter_near(): total = total + lax.ppermute(blocks[d], 'sz', pairs).astype(f32)  27.8 us
    ppermute x20, starting transfers between devices, swap_y(): return lax.ppermute(value, 'sy', SWAP)  21.4 us
  transfers between devices with their start and end apart: 121, of which 52 were waited for; matrix products, arithmetic and copies ran while one was open for 9% of the time, Pallas kernels for 17%

profile of v4, /device:TPU:11, one launch (start us, length us, event | category | flops | bytes accessed | tf_op | source)
XLA Modules:
  0.0 772.9 jit_solution(13064460714529460460)
XLA Ops:
  12.6 5.1 collective-permute-start.3
  28.1 4.7 collective-permute-start.4
  33.0 5.6 collective-permute-done.1
  52.2 5.0 collective-permute-done.23
  63.6 9.0 %all-gather.11.cloned.1.call-done = bf16[512,1024]{1,0:T(8,128)(2,1)} async-done(((bf16[128,1024]{1,0:T(8,128)(2,1)}), bf16[512,1024]{1,0:T(8,128)(2,1)}) %all-gather.11.cloned.1.call-update) | async-done | bytes 1048592 | tf_op jit(solution)/shard_map/all_gather | solution.py:778
  85.1 5.6 collective-permute-done.12.refs_2_
  96.7 6.2 collective-permute-done.17
  103.1 8.9 %shard_map.180 = (bf16[1024,256]{1,0:T(8,128)(2,1)S(1)}, bf16[1024,256]{1,0:T(8,128)(2,1)S(1)}, bf16[1024,256]{1,0:T(8,128)(2,1)S(1)}, bf16[1024,256]{1,0:T(8,128)(2,1)S(1)}, f32[1024,256]{1,0:T(8,128)S(1)}) custom-call(s32[5]{0:T(128)S(1)} %pad_add_fusion.scalars_ref, bf16[256,1024]{1,0:T(8,128)(2,1)S(1)} %get-tuple-element.114.refs_1_.refs_0_, ...), custom_call_target="tpu_custom_call" | custom-call | flops 1 | bytes 1 | tf_op jit(solution)/shard_map/pallas_call | solution.py:112
  120.1 4.3 collective-permute-done.19
  136.7 6.8 collective-permute-done.21.refs_3_
  155.8 10.2 %collective-permute-done.27 = bf16[2,2,32,704]{3,2,1,0:T(8,128)(2,1)S(1)} collective-permute-done((bf16[2,2,32,704]{3,2,1,0:T(8,128)(2,1)S(1)}, bf16[2,2,32,704]{3,2,1,0:T(8,128)(2,1)S(1)}, u32[]{:S(2)}, u32[]{:S(2)}) %collective-permute-start.27) | collective-permute-done | bytes 180256 | tf_op jit(solution)/shard_map/ppermute | solution.py:40
  168.2 5.9 all-gather.17.cloned.1.call-done
  185.0 4.5 shard_map.185
  190.5 5.0 shard_map.186
  197.3 7.7 collective-permute-done.36
  209.6 12.3 %collective-permute-done.37.refs_3_ = bf16[256,1024]{1,0:T(8,128)(2,1)S(1)} collective-permute-done((bf16[256,1024]{1,0:T(8,128)(2,1)S(1)}, bf16[256,1024]{1,0:T(8,128)(2,1)S(1)}, u32[]{:S(2)}, u32[]{:S(2)}) %collective-permute-start.37) | collective-permute-done | bytes 524320 | tf_op jit(solution)/shard_map/ppermute | solution.py:40
  228.5 9.2 %collective-permute-done.39.refs_2_ = bf16[256,1024]{1,0:T(8,128)(2,1)} collective-permute-done((bf16[256,1024]{1,0:T(8,128)(2,1)}, bf16[256,1024]{1,0:T(8,128)(2,1)}, u32[]{:S(2)}, u32[]{:S(2)}) %collective-permute-start.39) | collective-permute-done | bytes 524320 | tf_op jit(solution)/shard_map/ppermute | solution.py:40
  248.7 9.7 %shard_map.190 = (bf16[1024,256]{1,0:T(8,128)(2,1)S(1)}, bf16[1024,256]{1,0:T(8,128)(2,1)S(1)}, bf16[1024,256]{1,0:T(8,128)(2,1)S(1)}, bf16[1024,256]{1,0:T(8,128)(2,1)S(1)}) custom-call(s32[5]{0:T(128)S(1)} %pad_add_fusion.scalars_ref, bf16[256,1024]{1,0:T(8,128)(2,1)} %get-tuple-element.130.refs_0_.refs_11_, ...), custom_call_target="tpu_custom_call" | custom-call | flops 1 | bytes 1 | tf_op jit(solution)/shard_map/pallas_call | solution.py:112
  259.8 3.7 collective-permute-start.42
  265.9 3.8 collective-permute-start.47
  269.7 3.9 collective-permute-done.43.refs_2_.refs_3_.refs_5_
  274.2 3.8 collective-permute-start.44
  279.3 3.5 collective-permute-done.46
  282.8 5.6 collective-permute-done.47
  288.8 5.5 collective-permute-done.44.refs_3_
  295.4 3.7 collective-permute-start.48
  299.2 6.4 collective-permute-done.49.refs_8_.refs_0_.refs_4_
  305.6 3.7 collective-permute-start.50
  309.2 7.6 collective-permute-done.52.refs_0_.refs_2_
  318.8 4.1 shard_map.194
  322.9 4.4 shard_map.195
  330.0 4.6 shard_map.197
  334.6 4.6 shard_map.198
  341.1 11.8 %collective-permute-done.55.refs_5_ = bf16[256,1024]{1,0:T(8,128)(2,1)S(1)} collective-permute-done((bf16[256,1024]{1,0:T(8,128)(2,1)S(1)}, bf16[256,1024]{1,0:T(8,128)(2,1)S(1)}, u32[]{:S(2)}, u32[]{:S(2)}) %collective-permute-start.55) | collective-permute-done | bytes 524320 | tf_op jit(solution)/shard_map/ppermute | solution.py:40
  356.3 3.2 shard_map.201
  360.4 5.6 collective-permute-done.60.refs_3_
  371.8 7.1 collective-permute-done.62.refs_2_.refs_4_
  378.9 3.0 collective-permute-start.63
  384.3 17.1 %shard_map.204 = (f32[256,1024]{1,0:T(8,128)S(1)}, f32[256,1024]{1,0:T(8,128)S(1)}, bf16[2,256,1024]{2,1,0:T(8,128)(2,1)S(1)}, bf16[1024,768]{1,0:T(8,128)(2,1)S(1)}, f32[1024,256]{1,0:T(8,128)S(1)}) custom-call(s32[5]{0:T(128)S(1)} %pad_add_fusion.scalars_ref, bf16[256,1024]{1,0:T(8,128)(2,1)S(1)} %get-tuple-element.158.refs_0_.refs_2_, ...), custom_call_target="tpu_custom_call" | custom-call | flops 1 | bytes 1 | tf_op jit(solution)/shard_map/pallas_call | solution.py:112
  408.2 3.6 shard_map.206
  412.7 10.0 %collective-permute-done.67.refs_3_ = bf16[4,704,128]{2,1,0:T(8,128)(2,1)S(1)} collective-permute-done((bf16[4,704,128]{2,1,0:T(8,128)(2,1)S(1)}, bf16[4,704,128]{2,1,0:T(8,128)(2,1)S(1)}, u32[]{:S(2)}, u32[]{:S(2)}) %collective-permute-start.67) | collective-permute-done | bytes 720928 | tf_op jit(solution)/shard_map/ppermute | solution.py:44
  434.9 4.1 collective-permute-done.66.refs_3_
  446.5 8.1 %collective-permute-done.71.refs_0_.refs_4_ = bf16[256,1024]{1,0:T(8,128)(2,1)} collective-permute-done((bf16[256,1024]{1,0:T(8,128)(2,1)}, bf16[256,1024]{1,0:T(8,128)(2,1)}, u32[]{:S(2)}, u32[]{:S(2)}) %collective-permute-start.71) | collective-permute-done | bytes 524320 | tf_op jit(solution)/shard_map/ppermute | solution.py:40
  457.1 3.3 collective-permute-done.69.refs_1_
  465.4 5.0 shard_map.211
  473.2 6.0 shard_map.212
  491.4 3.4 shard_map.214
  494.8 8.0 %collective-permute-done.76.refs_1_ = bf16[352,1024]{1,0:T(8,128)(2,1)S(1)} collective-permute-done((bf16[352,1024]{1,0:T(8,128)(2,1)}, bf16[352,1024]{1,0:T(8,128)(2,1)S(1)}, u32[]{:S(2)}, u32[]{:S(2)}) %collective-permute-start.76) | collective-permute-done | bytes 720928 | tf_op jit(solution)/shard_map/ppermute | solution.py:44
  503.6 4.8 collective-permute-done.75.refs_1_
  509.8 3.5 shard_map.217
  519.7 9.1 %collective-permute-done.78.refs_2_.refs_4_ = bf16[256,1024]{1,0:T(8,128)(2,1)} collective-permute-done((bf16[256,1024]{1,0:T(8,128)(2,1)}, bf16[256,1024]{1,0:T(8,128)(2,1)}, u32[]{:S(2)}, u32[]{:S(2)}) %collective-permute-start.78) | collective-permute-done | bytes 524320 | tf_op jit(solution)/shard_map/ppermute | solution.py:40
  532.2 3.5 shard_map.219
  538.7 19.1 %shard_map.220 = (f32[256,1024]{1,0:T(8,128)S(1)}, f32[256,1024]{1,0:T(8,128)S(1)}, bf16[2,256,1024]{2,1,0:T(8,128)(2,1)}, bf16[1024,768]{1,0:T(8,128)(2,1)S(1)}, f32[1024,256]{1,0:T(8,128)S(1)}) custom-call(s32[5]{0:T(128)S(1)} %pad_add_fusion.scalars_ref, bf16[256,1024]{1,0:T(8,128)(2,1)} %get-tuple-element.194.refs_0_.refs_2_, ...), custom_call_target="tpu_custom_call" | custom-call | flops 1 | bytes 1 | tf_op jit(solution)/shard_map/pallas_call | solution.py:112
  563.9 6.2 collective-permute-done.107
  578.6 3.4 collective-permute-start.57
  601.7 26.3 %collective-permute-done.57 = bf16[128,1024]{1,0:T(8,128)(2,1)} collective-permute-done((bf16[128,1024]{1,0:T(8,128)(2,1)}, bf16[128,1024]{1,0:T(8,128)(2,1)}, u32[]{:S(2)}, u32[]{:S(2)}) %collective-permute-start.57) | collective-permute-done | bytes 262176 | tf_op jit(solution)/shard_map/ppermute | solution.py:774
  631.7 6.3 collective-permute-start.99
  640.6 5.9 collective-permute-done.110
  650.0 6.6 collective-permute-start.84
  656.6 11.3 %collective-permute-done.100 = f32[4,1024]{1,0:T(4,128)S(1)} collective-permute-done((f32[4,1024]{1,0:T(4,128)S(1)}, f32[4,1024]{1,0:T(4,128)S(1)}, u32[]{:S(2)}, u32[]{:S(2)}) %collective-permute-start.100) | collective-permute-done | bytes 16416 | tf_op jit(solution)/shard_map/ppermute | solution.py:44
  679.3 17.8 %collective-permute-start.97 = (bf16[2,1,32,1024]{3,2,0,1:T(8,128)(2,1)}, bf16[2,1,32,1024]{3,2,0,1:T(8,128)(2,1)}, u32[]{:S(2)}, u32[]{:S(2)}) collective-permute-start(bf16[2,1,32,1024]{3,2,0,1:T(8,128)(2,1)} %get-tuple-element.268), channel_id=1, source_target_pairs={{0,1},{1,0},{2,3},{3,2},{4,5},{5,4},{6,7},{7,6},{8,9},{9,8},{10,11... | collective-permute-start | bytes 393224 | tf_op jit(solution)/shard_map/ppermute | solution.py:36
  704.4 10.3 %collective-permute-done.88 = bf16[128,768]{1,0:T(8,128)(2,1)} collective-permute-done((bf16[128,768]{1,0:T(8,128)(2,1)S(1)}, bf16[128,768]{1,0:T(8,128)(2,1)}, u32[]{:S(2)}, u32[]{:S(2)}) %collective-permute-start.88) | collective-permute-done | bytes 196640 | tf_op jit(solution)/shard_map/ppermute | solution.py:87
  714.6 17.5 %collective-permute-done.89 = bf16[128,768]{1,0:T(8,128)(2,1)} collective-permute-done((bf16[128,768]{1,0:T(8,128)(2,1)S(1)}, bf16[128,768]{1,0:T(8,128)(2,1)}, u32[]{:S(2)}, u32[]{:S(2)}) %collective-permute-start.89) | collective-permute-done | bytes 196640 | tf_op jit(solution)/shard_map/ppermute | solution.py:87
  744.9 3.7 collective-permute-done.103
  (767 shorter events, 307.1 us)
Async XLA Ops:
  7.2 65.3 %all-gather.11.cloned.1.call-start = ((), (), s32[]{:S(2)}) async-start(), calls=%async_computation.10 | async-start | bytes 1310720 | tf_op jit(solution)/shard_map/all_gather | solution.py:778
  8.7 24.1 %collective-permute-start.5 = (f32[4,32]{1,0:T(4,128)S(1)}, f32[4,32]{1,0:T(4,128)S(1)}, u32[]{:S(2)}, u32[]{:S(2)}) collective-permute-start(f32[4,32]{1,0:T(4,128)S(1)} %maximum_convert_fusion.6), channel_id=1, source_target_pairs={{0,8},{8,0},{16,24},{24,16},{1,9},{9,1},{17,25},{25,17},{2,10},{10... | collective-permute-start | bytes 1544 | tf_op jit(solution)/shard_map/ppermute | solution.py:81
  9.0 24.0 %collective-permute-start.6 = (f32[4,32]{1,0:T(4,128)S(1)}, f32[4,32]{1,0:T(4,128)S(1)}, u32[]{:S(2)}, u32[]{:S(2)}) collective-permute-start(f32[4,32]{1,0:T(4,128)S(1)} %maximum_convert_fusion.6), channel_id=1, source_target_pairs={{0,16},{8,24},{16,0},{24,8},{1,17},{9,25},{17,1},{25,9},{2,18},{10... | collective-permute-start | bytes 1544 | tf_op jit(solution)/shard_map/ppermute | solution.py:81
  11.3 21.7 %collective-permute-start.7 = (f32[4,32]{1,0:T(4,128)S(1)}, f32[4,32]{1,0:T(4,128)S(1)}, u32[]{:S(2)}, u32[]{:S(2)}) collective-permute-start(f32[4,32]{1,0:T(4,128)S(1)} %maximum_convert_fusion.6), channel_id=1, source_target_pairs={{0,24},{8,16},{16,8},{24,0},{1,25},{9,17},{17,9},{25,1},{2,26},{10... | collective-permute-start | bytes 1544 | tf_op jit(solution)/shard_map/ppermute | solution.py:81
  12.6 27.5 %collective-permute-start.3 = (bf16[128,1024]{1,0:T(8,128)(2,1)S(1)}, bf16[128,1024]{1,0:T(8,128)(2,1)S(1)}, u32[]{:S(2)}, u32[]{:S(2)}) collective-permute-start(bf16[128,1024]{1,0:T(8,128)(2,1)S(1)} %get-tuple-element.241), channel_id=1, source_target_pairs={{0,0},{1,8},{2,16},{3,24},{4,4},{5,12},{6,20},{7,28},{8,1},{9,9},{... | collective-permute-start | bytes 786440 | tf_op jit(solution)/shard_map/ppermute | solution.py:767
  28.1 14.7 %collective-permute-start.4 = (bf16[128,1024]{1,0:T(8,128)(2,1)S(1)}, bf16[128,1024]{1,0:T(8,128)(2,1)S(1)}, u32[]{:S(2)}, u32[]{:S(2)}) collective-permute-start(bf16[128,1024]{1,0:T(8,128)(2,1)S(1)} %get-tuple-element.242), channel_id=1, source_target_pairs={{0,4},{1,12},{2,20},{3,28},{4,0},{5,8},{6,16},{7,24},{8,5},{9,13},... | collective-permute-start | bytes 786440 | tf_op jit(solution)/shard_map/ppermute | solution.py:767
  43.6 90.8 %all-gather.13.cloned.1.call-start = ((), (), s32[]{:S(2)}) async-start(), calls=%async_computation.11 | async-start | bytes 1802240 | tf_op jit(solution)/shard_map/all_gather | solution.py:778
  61.8 90.3 %all-gather.15.cloned.1.call-start = ((), (), s32[]{:S(2)}) async-start(), calls=%async_computation.12 | async-start | bytes 1802240 | tf_op jit(solution)/shard_map/all_gather | solution.py:778
  62.7 111.4 %all-gather.17.cloned.1.call-start = ((), (), s32[]{:S(2)}) async-start(), calls=%async_computation.13 | async-start | bytes 1310720 | tf_op jit(solution)/shard_map/all_gather | solution.py:778
  79.5 23.5 %collective-permute-start.14 = (bf16[4,128,768]{2,1,0:T(8,128)(2,1)S(1)}, bf16[4,128,768]{2,1,0:T(8,128)(2,1)S(1)}, u32[]{:S(2)}, u32[]{:S(2)}) collective-permute-start(bf16[4,128,768]{2,1,0:T(8,128)(2,1)S(1)} %slice.190), channel_id=1, source_target_pairs={{0,4},{4,0},{1,5},{5,1},{2,6},{6,2},{3,7},{7,3},{8,12},{12,8},{9,1... | collective-permute-start | bytes 2359304 | tf_op jit(solution)/shard_map/ppermute | solution.py:44
  85.0 18.0 %collective-permute-start.11 = (bf16[256,1024]{1,0:T(8,128)(2,1)S(1)}, bf16[256,1024]{1,0:T(8,128)(2,1)S(1)}, u32[]{:S(2)}, u32[]{:S(2)}) collective-permute-start(bf16[256,1024]{1,0:T(8,128)(2,1)S(1)} %get-tuple-element.114.refs_1_.refs_0_), channel_id=1, source_target_pairs={{0,1},{1,0},{2,3},{3,2},{4,5},{5,4},{6,7},{7,6},{8,9},{9,8},{10,11... | collective-permute-start | bytes 1572872 | tf_op jit(solution)/shard_map/ppermute | solution.py:36
  126.9 112.4 %all-gather.19.cloned.1.call-start = ((), (), s32[]{:S(2)}) async-start(), calls=%async_computation.14 | async-start | bytes 1802240 | tf_op jit(solution)/shard_map/all_gather | solution.py:778
  134.4 50.5 %collective-permute-start.25 = (bf16[4,704,256]{2,1,0:T(8,128)(2,1)}, bf16[4,704,256]{2,1,0:T(8,128)(2,1)S(1)}, u32[]{:S(2)}, u32[]{:S(2)}) collective-permute-start(bf16[4,704,256]{2,1,0:T(8,128)(2,1)} %bitcast.291), channel_id=1, source_target_pairs={{0,4},{4,0},{1,5},{5,1},{2,6},{6,2},{3,7},{7,3},{8,12},{12,8},{9,1... | collective-permute-start | bytes 4325384 | tf_op jit(solution)/shard_map/ppermute | solution.py:44
  149.3 28.3 %collective-permute-start.30 = (bf16[256,1024]{1,0:T(8,128)(2,1)}, bf16[256,1024]{1,0:T(8,128)(2,1)}, u32[]{:S(2)}, u32[]{:S(2)}) collective-permute-start(bf16[256,1024]{1,0:T(8,128)(2,1)} %get-tuple-element.122.refs_1_.refs_0_), channel_id=1, source_target_pairs={{0,2},{2,0},{1,3},{3,1},{4,6},{6,4},{5,7},{7,5},{8,10},{10,8},{9,1... | collective-permute-start | bytes 1572872 | tf_op jit(solution)/shard_map/ppermute | solution.py:40
  150.9 15.1 %collective-permute-start.27 = (bf16[2,2,32,704]{3,2,1,0:T(8,128)(2,1)S(1)}, bf16[2,2,32,704]{3,2,1,0:T(8,128)(2,1)S(1)}, u32[]{:S(2)}, u32[]{:S(2)}) collective-permute-start(bf16[2,2,32,704]{3,2,1,0:T(8,128)(2,1)S(1)} %get-tuple-element.254), channel_id=1, source_target_pairs={{0,2},{2,0},{1,3},{3,1},{4,6},{6,4},{5,7},{7,5},{8,10},{10,8},{9,1... | collective-permute-start | bytes 540680 | tf_op jit(solution)/shard_map/ppermute | solution.py:40
  154.6 28.2 %collective-permute-start.26 = (bf16[352,1024]{1,0:T(8,128)(2,1)}, bf16[352,1024]{1,0:T(8,128)(2,1)}, u32[]{:S(2)}, u32[]{:S(2)}) collective-permute-start(bf16[352,1024]{1,0:T(8,128)(2,1)} %bitcast.66.refs_4_.refs_6_), channel_id=1, source_target_pairs={{0,4},{4,0},{1,5},{5,1},{2,6},{6,2},{3,7},{7,3},{8,12},{12,8},{9,1... | collective-permute-start | bytes 2162696 | tf_op jit(solution)/shard_map/ppermute | solution.py:44
  178.7 492.0 %reduce-scatter.8.cloned.1.call-start = ((), (), s32[]{:S(2)}) async-start(), calls=%async_computation.6 | async-start | bytes 1802240 | tf_op jit(solution)/shard_map/reduce_scatter | solution.py:97
  180.5 26.8 %collective-permute-start.33 = (bf16[4,128,768]{2,1,0:T(8,128)(2,1)S(1)}, bf16[4,128,768]{2,1,0:T(8,128)(2,1)S(1)}, u32[]{:S(2)}, u32[]{:S(2)}) collective-permute-start(bf16[4,128,768]{2,1,0:T(8,128)(2,1)S(1)} %slice.194), channel_id=1, source_target_pairs={{0,4},{4,0},{1,5},{5,1},{2,6},{6,2},{3,7},{7,3},{8,12},{12,8},{9,1... | collective-permute-start | bytes 2359304 | tf_op jit(solution)/shard_map/ppermute | solution.py:44
  225.9 16.8 %collective-permute-start.41 = (bf16[352,1024]{1,0:T(8,128)(2,1)}, bf16[352,1024]{1,0:T(8,128)(2,1)}, u32[]{:S(2)}, u32[]{:S(2)}) collective-permute-start(bf16[352,1024]{1,0:T(8,128)(2,1)} %bitcast.92.refs_4_.refs_6_), channel_id=1, source_target_pairs={{0,4},{4,0},{1,5},{5,1},{2,6},{6,2},{3,7},{7,3},{8,12},{12,8},{9,1... | collective-permute-start | bytes 2162696 | tf_op jit(solution)/shard_map/ppermute | solution.py:44
  227.1 15.7 %collective-permute-start.38 = (bf16[256,1024]{1,0:T(8,128)(2,1)}, bf16[256,1024]{1,0:T(8,128)(2,1)}, u32[]{:S(2)}, u32[]{:S(2)}) collective-permute-start(bf16[256,1024]{1,0:T(8,128)(2,1)} %get-tuple-element.130.refs_0_.refs_11_), channel_id=1, source_target_pairs={{0,1},{1,0},{2,3},{3,2},{4,5},{5,4},{6,7},{7,6},{8,9},{9,8},{10,11... | collective-permute-start | bytes 1572872 | tf_op jit(solution)/shard_map/ppermute | solution.py:36
  239.3 34.2 %collective-permute-start.43 = (bf16[4,704,256]{2,1,0:T(8,128)(2,1)}, bf16[4,704,256]{2,1,0:T(8,128)(2,1)S(1)}, u32[]{:S(2)}, u32[]{:S(2)}) collective-permute-start(bf16[4,704,256]{2,1,0:T(8,128)(2,1)} %bitcast.285), channel_id=1, source_target_pairs={{0,4},{4,0},{1,5},{5,1},{2,6},{6,2},{3,7},{7,3},{8,12},{12,8},{9,1... | collective-permute-start | bytes 4325384 | tf_op jit(solution)/shard_map/ppermute | solution.py:44
  263.5 19.3 %collective-permute-start.46 = (bf16[128,1024]{1,0:T(8,128)(2,1)S(1)}, bf16[128,1024]{1,0:T(8,128)(2,1)S(1)}, u32[]{:S(2)}, u32[]{:S(2)}) collective-permute-start(bf16[128,1024]{1,0:T(8,128)(2,1)S(1)} %get-tuple-element.239), channel_id=1, source_target_pairs={{0,0},{1,8},{2,16},{3,24},{4,4},{5,12},{6,20},{7,28},{8,1},{9,9},{... | collective-permute-start | bytes 786440 | tf_op jit(solution)/shard_map/ppermute | solution.py:767
  265.9 22.6 %collective-permute-start.47 = (bf16[128,1024]{1,0:T(8,128)(2,1)S(1)}, bf16[128,1024]{1,0:T(8,128)(2,1)S(1)}, u32[]{:S(2)}, u32[]{:S(2)}) collective-permute-start(bf16[128,1024]{1,0:T(8,128)(2,1)S(1)} %get-tuple-element.240), channel_id=1, source_target_pairs={{0,4},{1,12},{2,20},{3,28},{4,0},{5,8},{6,16},{7,24},{8,5},{9,13},... | collective-permute-start | bytes 786440 | tf_op jit(solution)/shard_map/ppermute | solution.py:767
  274.2 20.1 %collective-permute-start.44 = (bf16[256,1024]{1,0:T(8,128)(2,1)S(1)}, bf16[256,1024]{1,0:T(8,128)(2,1)S(1)}, u32[]{:S(2)}, u32[]{:S(2)}) collective-permute-start(bf16[256,1024]{1,0:T(8,128)(2,1)S(1)} %shard_map.192.refs_5_), channel_id=1, source_target_pairs={{0,2},{2,0},{1,3},{3,1},{4,6},{6,4},{5,7},{7,5},{8,10},{10,8},{9,1... | collective-permute-start | bytes 1572872 | tf_op jit(solution)/shard_map/ppermute | solution.py:40
  288.7 16.9 %collective-permute-start.49 = (bf16[256,1024]{1,0:T(8,128)(2,1)S(1)}, bf16[256,1024]{1,0:T(8,128)(2,1)S(1)}, u32[]{:S(2)}, u32[]{:S(2)}) collective-permute-start(bf16[256,1024]{1,0:T(8,128)(2,1)S(1)} %get-tuple-element.220.refs_6_.refs_0_.refs_2_), channel_id=1, source_target_pairs={{0,2},{2,0},{1,3},{3,1},{4,6},{6,4},{5,7},{7,5},{8,10},{10,8},{9,1... | collective-permute-start | bytes 1572872 | tf_op jit(solution)/shard_map/ppermute | solution.py:40
  295.3 21.4 %collective-permute-start.52 = (bf16[256,1024]{1,0:T(8,128)(2,1)S(1)}, bf16[256,1024]{1,0:T(8,128)(2,1)S(1)}, u32[]{:S(2)}, u32[]{:S(2)}) collective-permute-start(bf16[256,1024]{1,0:T(8,128)(2,1)S(1)} %get-tuple-element.136.refs_0_.refs_10_), channel_id=1, source_target_pairs={{0,2},{2,0},{1,3},{3,1},{4,6},{6,4},{5,7},{7,5},{8,10},{10,8},{9,1... | collective-permute-start | bytes 1572872 | tf_op jit(solution)/shard_map/ppermute | solution.py:40
  295.4 23.4 %collective-permute-start.48 = (bf16[256,1024]{1,0:T(8,128)(2,1)S(1)}, bf16[256,1024]{1,0:T(8,128)(2,1)S(1)}, u32[]{:S(2)}, u32[]{:S(2)}) collective-permute-start(bf16[256,1024]{1,0:T(8,128)(2,1)S(1)} %get-tuple-element.220.refs_6_.refs_0_.refs_2_), channel_id=1, source_target_pairs={{0,1},{1,0},{2,3},{3,2},{4,5},{5,4},{6,7},{7,6},{8,9},{9,8},{10,11... | collective-permute-start | bytes 1572872 | tf_op jit(solution)/shard_map/ppermute | solution.py:36
  339.8 20.6 %collective-permute-start.58 = (bf16[256,1024]{1,0:T(8,128)(2,1)S(1)}, bf16[256,1024]{1,0:T(8,128)(2,1)S(1)}, u32[]{:S(2)}, u32[]{:S(2)}) collective-permute-start(bf16[256,1024]{1,0:T(8,128)(2,1)S(1)} %get-tuple-element.146), channel_id=1, source_target_pairs={{0,1},{1,0},{2,3},{3,2},{4,5},{5,4},{6,7},{7,6},{8,9},{9,8},{10,11... | collective-permute-start | bytes 1572872 | tf_op jit(solution)/shard_map/ppermute | solution.py:36
  368.2 15.9 %collective-permute-start.64 = (bf16[4,704,128]{2,1,0:T(8,128)(2,1)S(1)}, bf16[4,704,128]{2,1,0:T(8,128)(2,1)S(1)}, u32[]{:S(2)}, u32[]{:S(2)}) collective-permute-start(bf16[4,704,128]{2,1,0:T(8,128)(2,1)S(1)} %get-tuple-element.155.refs_6_), channel_id=1, source_target_pairs={{0,4},{4,0},{1,5},{5,1},{2,6},{6,2},{3,7},{7,3},{8,12},{12,8},{9,1... | collective-permute-start | bytes 2162696 | tf_op jit(solution)/shard_map/ppermute | solution.py:44
  369.4 14.7 %collective-permute-start.61 = (bf16[256,1024]{1,0:T(8,128)(2,1)S(1)}, bf16[256,1024]{1,0:T(8,128)(2,1)S(1)}, u32[]{:S(2)}, u32[]{:S(2)}) collective-permute-start(bf16[256,1024]{1,0:T(8,128)(2,1)S(1)} %get-tuple-element.158.refs_0_.refs_2_), channel_id=1, source_target_pairs={{0,1},{1,0},{2,3},{3,2},{4,5},{5,4},{6,7},{7,6},{8,9},{9,8},{10,11... | collective-permute-start | bytes 1572872 | tf_op jit(solution)/shard_map/ppermute | solution.py:36
  405.0 17.8 %collective-permute-start.67 = (bf16[4,704,128]{2,1,0:T(8,128)(2,1)S(1)}, bf16[4,704,128]{2,1,0:T(8,128)(2,1)S(1)}, u32[]{:S(2)}, u32[]{:S(2)}) collective-permute-start(bf16[4,704,128]{2,1,0:T(8,128)(2,1)S(1)} %get-tuple-element.163.refs_13_), channel_id=1, source_target_pairs={{0,4},{4,0},{1,5},{5,1},{2,6},{6,2},{3,7},{7,3},{8,12},{12,8},{9,1... | collective-permute-start | bytes 2162696 | tf_op jit(solution)/shard_map/ppermute | solution.py:44
  425.7 246.6 %reduce-scatter.6.cloned.1.call-start = ((), (), s32[]{:S(2)}) async-start(), calls=%async_computation.5 | async-start | bytes 983040 | tf_op jit(solution)/shard_map/reduce_scatter | solution.py:97
  443.2 17.2 %collective-permute-start.69 = (bf16[4,128,768]{2,1,0:T(8,128)(2,1)S(1)}, bf16[4,128,768]{2,1,0:T(8,128)(2,1)S(1)}, u32[]{:S(2)}, u32[]{:S(2)}) collective-permute-start(bf16[4,128,768]{2,1,0:T(8,128)(2,1)S(1)} %copy-done.126), channel_id=1, source_target_pairs={{0,4},{4,0},{1,5},{5,1},{2,6},{6,2},{3,7},{7,3},{8,12},{12,8},{9,1... | collective-permute-start | bytes 2359304 | tf_op jit(solution)/shard_map/ppermute | solution.py:44
  444.4 17.6 %collective-permute-start.68 = (bf16[256,1024]{1,0:T(8,128)(2,1)}, bf16[256,1024]{1,0:T(8,128)(2,1)}, u32[]{:S(2)}, u32[]{:S(2)}) collective-permute-start(bf16[256,1024]{1,0:T(8,128)(2,1)} %get-tuple-element.174.refs_0_.refs_2_), channel_id=1, source_target_pairs={{0,1},{1,0},{2,3},{3,2},{4,5},{5,4},{6,7},{7,6},{8,9},{9,8},{10,11... | collective-permute-start | bytes 1572872 | tf_op jit(solution)/shard_map/ppermute | solution.py:36
  454.6 18.6 %collective-permute-start.72 = (bf16[256,1024]{1,0:T(8,128)(2,1)}, bf16[256,1024]{1,0:T(8,128)(2,1)}, u32[]{:S(2)}, u32[]{:S(2)}) collective-permute-start(bf16[256,1024]{1,0:T(8,128)(2,1)} %collective-permute-done.71.refs_0_.refs_4_), channel_id=1, source_target_pairs={{0,1},{1,0},{2,3},{3,2},{4,5},{5,4},{6,7},{7,6},{8,9},{9,8},{10,11... | collective-permute-start | bytes 1572872 | tf_op jit(solution)/shard_map/ppermute | solution.py:36
  484.7 18.1 %collective-permute-start.76 = (bf16[352,1024]{1,0:T(8,128)(2,1)}, bf16[352,1024]{1,0:T(8,128)(2,1)S(1)}, u32[]{:S(2)}, u32[]{:S(2)}) collective-permute-start(bf16[352,1024]{1,0:T(8,128)(2,1)} %get-tuple-element.156.refs_6_), channel_id=1, source_target_pairs={{0,4},{4,0},{1,5},{5,1},{2,6},{6,2},{3,7},{7,3},{8,12},{12,8},{9,1... | collective-permute-start | bytes 2162696 | tf_op jit(solution)/shard_map/ppermute | solution.py:44
  485.9 187.9 %reduce-scatter.12.cloned.1.call-start = ((), (), s32[]{:S(2)}) async-start(), calls=%async_computation.8 | async-start | bytes 1228800 | tf_op jit(solution)/shard_map/reduce_scatter | solution.py:97
  486.0 27.3 %collective-permute-start.70 = (bf16[256,1024]{1,0:T(8,128)(2,1)}, bf16[256,1024]{1,0:T(8,128)(2,1)S(1)}, u32[]{:S(2)}, u32[]{:S(2)}) collective-permute-start(bf16[256,1024]{1,0:T(8,128)(2,1)} %copy-done.158), channel_id=1, source_target_pairs={{0,1},{1,0},{2,3},{3,2},{4,5},{5,4},{6,7},{7,6},{8,9},{9,8},{10,11... | collective-permute-start | bytes 1572872 | tf_op jit(solution)/shard_map/ppermute | solution.py:36
  489.5 23.9 %collective-permute-start.74 = (bf16[256,1024]{1,0:T(8,128)(2,1)S(1)}, bf16[256,1024]{1,0:T(8,128)(2,1)S(1)}, u32[]{:S(2)}, u32[]{:S(2)}) collective-permute-start(bf16[256,1024]{1,0:T(8,128)(2,1)S(1)} %shard_map.213.refs_6_), channel_id=1, source_target_pairs={{0,2},{2,0},{1,3},{3,1},{4,6},{6,4},{5,7},{7,5},{8,10},{10,8},{9,1... | collective-permute-start | bytes 1572872 | tf_op jit(solution)/shard_map/ppermute | solution.py:40
  490.2 18.1 %collective-permute-start.75 = (bf16[128,1024]{1,0:T(8,128)(2,1)S(1)}, bf16[128,1024]{1,0:T(8,128)(2,1)S(1)}, u32[]{:S(2)}, u32[]{:S(2)}) collective-permute-start(bf16[128,1024]{1,0:T(8,128)(2,1)S(1)} %copy-done.146), channel_id=1, source_target_pairs={{0,4},{4,0},{1,5},{5,1},{2,6},{6,2},{3,7},{7,3},{8,12},{12,8},{9,1... | collective-permute-start | bytes 786440 | tf_op jit(solution)/shard_map/ppermute | solution.py:44
  518.0 18.6 %collective-permute-start.80 = (bf16[4,704,128]{2,1,0:T(8,128)(2,1)}, bf16[4,704,128]{2,1,0:T(8,128)(2,1)}, u32[]{:S(2)}, u32[]{:S(2)}) collective-permute-start(bf16[4,704,128]{2,1,0:T(8,128)(2,1)} %get-tuple-element.191.refs_2_), channel_id=1, source_target_pairs={{0,4},{4,0},{1,5},{5,1},{2,6},{6,2},{3,7},{7,3},{8,12},{12,8},{9,1... | collective-permute-start | bytes 2162696 | tf_op jit(solution)/shard_map/ppermute | solution.py:44
  519.2 17.3 %collective-permute-start.77 = (bf16[256,1024]{1,0:T(8,128)(2,1)}, bf16[256,1024]{1,0:T(8,128)(2,1)}, u32[]{:S(2)}, u32[]{:S(2)}) collective-permute-start(bf16[256,1024]{1,0:T(8,128)(2,1)} %get-tuple-element.194.refs_0_.refs_2_), channel_id=1, source_target_pairs={{0,1},{1,0},{2,3},{3,2},{4,5},{5,4},{6,7},{7,6},{8,9},{9,8},{10,11... | collective-permute-start | bytes 1572872 | tf_op jit(solution)/shard_map/ppermute | solution.py:36
  531.6 209.4 %reduce-scatter.14.cloned.1.call-start = ((), (), s32[]{:S(2)}) async-start(), calls=%async_computation.9 | async-start | bytes 1802240 | tf_op jit(solution)/shard_map/reduce_scatter | solution.py:97
  562.7 22.7 %collective-permute-start.83 = (bf16[4,704,128]{2,1,0:T(8,128)(2,1)}, bf16[4,704,128]{2,1,0:T(8,128)(2,1)S(1)}, u32[]{:S(2)}, u32[]{:S(2)}) collective-permute-start(bf16[4,704,128]{2,1,0:T(8,128)(2,1)} %get-tuple-element.199.refs_14_), channel_id=1, source_target_pairs={{0,4},{4,0},{1,5},{5,1},{2,6},{6,2},{3,7},{7,3},{8,12},{12,8},{9,1... | collective-permute-start | bytes 2162696 | tf_op jit(solution)/shard_map/ppermute | solution.py:44
  572.0 17.0 %collective-permute-start.108 = (bf16[2,256,256]{2,1,0:T(8,128)(2,1)}, bf16[2,256,256]{2,1,0:T(8,128)(2,1)}, u32[]{:S(2)}, u32[]{:S(2)}) collective-permute-start(bf16[2,256,256]{2,1,0:T(8,128)(2,1)} %get-tuple-element.224), channel_id=1, source_target_pairs={{0,1},{1,0},{2,3},{3,2},{4,5},{5,4},{6,7},{7,6},{8,9},{9,8},{10,11... | collective-permute-start | bytes 786440 | tf_op jit(solution)/shard_map/ppermute | solution.py:36
  573.7 25.0 %collective-permute-start.82 = (bf16[256,1024]{1,0:T(8,128)(2,1)S(1)}, bf16[256,1024]{1,0:T(8,128)(2,1)}, u32[]{:S(2)}, u32[]{:S(2)}) collective-permute-start(bf16[256,1024]{1,0:T(8,128)(2,1)S(1)} %shard_map.221.refs_5_), channel_id=1, source_target_pairs={{0,2},{2,0},{1,3},{3,1},{4,6},{6,4},{5,7},{7,5},{8,10},{10,8},{9,1... | collective-permute-start | bytes 1572872 | tf_op jit(solution)/shard_map/ppermute | solution.py:40
  575.9 25.9 %collective-permute-start.56 = (bf16[128,1024]{1,0:T(8,128)(2,1)}, bf16[128,1024]{1,0:T(8,128)(2,1)}, u32[]{:S(2)}, u32[]{:S(2)}) collective-permute-start(bf16[128,1024]{1,0:T(8,128)(2,1)} %get-tuple-element.237), channel_id=1, source_target_pairs={{0,0},{8,1},{16,2},{24,3},{4,4},{12,5},{20,6},{28,7},{1,8},{9,9},{... | collective-permute-start | bytes 786440 | tf_op jit(solution)/shard_map/ppermute | solution.py:774
  578.6 49.4 %collective-permute-start.57 = (bf16[128,1024]{1,0:T(8,128)(2,1)}, bf16[128,1024]{1,0:T(8,128)(2,1)}, u32[]{:S(2)}, u32[]{:S(2)}) collective-permute-start(bf16[128,1024]{1,0:T(8,128)(2,1)} %get-tuple-element.238), channel_id=1, source_target_pairs={{4,0},{12,1},{20,2},{28,3},{0,4},{8,5},{16,6},{24,7},{5,8},{13,9},... | collective-permute-start | bytes 786440 | tf_op jit(solution)/shard_map/ppermute | solution.py:774
  588.9 165.2 %reduce-scatter.10.cloned.1.call-start = ((), (), s32[]{:S(2)}) async-start(), calls=%async_computation.7 | async-start | bytes 1310720 | tf_op jit(solution)/shard_map/reduce_scatter | solution.py:97
  591.0 49.6 %collective-permute-start.109 = (bf16[128,1024]{1,0:T(8,128)(2,1)S(1)}, bf16[128,1024]{1,0:T(8,128)(2,1)S(1)}, u32[]{:S(2)}, u32[]{:S(2)}) collective-permute-start(bf16[128,1024]{1,0:T(8,128)(2,1)S(1)} %get-tuple-element.221), channel_id=1, source_target_pairs={{0,0},{8,1},{16,2},{24,3},{4,4},{12,5},{20,6},{28,7},{1,8},{9,9},{... | collective-permute-start | bytes 786440 | tf_op jit(solution)/shard_map/ppermute | solution.py:774
  593.7 52.8 %collective-permute-start.110 = (bf16[128,1024]{1,0:T(8,128)(2,1)S(1)}, bf16[128,1024]{1,0:T(8,128)(2,1)S(1)}, u32[]{:S(2)}, u32[]{:S(2)}) collective-permute-start(bf16[128,1024]{1,0:T(8,128)(2,1)S(1)} %get-tuple-element.222), channel_id=1, source_target_pairs={{4,0},{12,1},{20,2},{28,3},{0,4},{8,5},{16,6},{24,7},{5,8},{13,9},... | collective-permute-start | bytes 786440 | tf_op jit(solution)/shard_map/ppermute | solution.py:774
  601.6 30.1 %collective-permute-start.98 = (f32[4,1024]{1,0:T(4,128)S(1)}, f32[4,1024]{1,0:T(4,128)S(1)}, u32[]{:S(2)}, u32[]{:S(2)}) collective-permute-start(f32[4,1024]{1,0:T(4,128)S(1)} %pad_maximum_fusion.8), channel_id=1, source_target_pairs={{0,2},{2,0},{1,3},{3,1},{4,6},{6,4},{5,7},{7,5},{8,10},{10,8},{9,1... | collective-permute-start | bytes 49160 | tf_op jit(solution)/shard_map/ppermute | solution.py:40
  630.2 38.4 %collective-permute-start.93 = (bf16[352,1024]{1,0:T(8,128)(2,1)S(1)}, bf16[352,1024]{1,0:T(8,128)(2,1)S(1)}, u32[]{:S(2)}, u32[]{:S(2)}) collective-permute-start(bf16[352,1024]{1,0:T(8,128)(2,1)S(1)} %copy-done.130), channel_id=1, source_target_pairs={{0,4},{4,0},{1,5},{5,1},{2,6},{6,2},{3,7},{7,3},{8,12},{12,8},{9,1... | collective-permute-start | bytes 2162696 | tf_op jit(solution)/shard_map/ppermute | solution.py:44
  630.5 37.4 %collective-permute-start.86 = (bf16[4,128,768]{2,1,0:T(8,128)(2,1)S(1)}, bf16[4,128,768]{2,1,0:T(8,128)(2,1)S(1)}, u32[]{:S(2)}, u32[]{:S(2)}) collective-permute-start(bf16[4,128,768]{2,1,0:T(8,128)(2,1)S(1)} %copy-done.124), channel_id=1, source_target_pairs={{0,4},{4,0},{1,5},{5,1},{2,6},{6,2},{3,7},{7,3},{8,12},{12,8},{9,1... | collective-permute-start | bytes 2359304 | tf_op jit(solution)/shard_map/ppermute | solution.py:44
  631.7 17.0 %collective-permute-start.99 = (f32[4,1024]{1,0:T(4,128)S(1)}, f32[4,1024]{1,0:T(4,128)S(1)}, u32[]{:S(2)}, u32[]{:S(2)}) collective-permute-start(f32[4,1024]{1,0:T(4,128)S(1)} %fusion.15), channel_id=1, source_target_pairs={{0,1},{1,0},{2,3},{3,2},{4,5},{5,4},{6,7},{7,6},{8,9},{9,8},{10,11... | collective-permute-start | bytes 49160 | tf_op jit(solution)/shard_map/ppermute | solution.py:36
  647.5 21.9 %collective-permute-start.92 = (bf16[128,1024]{1,0:T(8,128)(2,1)S(1)}, bf16[128,1024]{1,0:T(8,128)(2,1)S(1)}, u32[]{:S(2)}, u32[]{:S(2)}) collective-permute-start(bf16[128,1024]{1,0:T(8,128)(2,1)S(1)} %get-tuple-element.208.refs_6_), channel_id=1, source_target_pairs={{0,4},{4,0},{1,5},{5,1},{2,6},{6,2},{3,7},{7,3},{8,12},{12,8},{9,1... | collective-permute-start | bytes 786440 | tf_op jit(solution)/shard_map/ppermute | solution.py:44
  648.7 19.2 %collective-permute-start.100 = (f32[4,1024]{1,0:T(4,128)S(1)}, f32[4,1024]{1,0:T(4,128)S(1)}, u32[]{:S(2)}, u32[]{:S(2)}) collective-permute-start(f32[4,1024]{1,0:T(4,128)S(1)} %fusion.28), channel_id=1, source_target_pairs={{0,4},{4,0},{1,5},{5,1},{2,6},{6,2},{3,7},{7,3},{8,12},{12,8},{9,1... | collective-permute-start | bytes 49160 | tf_op jit(solution)/shard_map/ppermute | solution.py:44
  650.0 47.1 %collective-permute-start.84 = (bf16[128,1024]{1,0:T(8,128)(2,1)}, bf16[128,1024]{1,0:T(8,128)(2,1)}, u32[]{:S(2)}, u32[]{:S(2)}) collective-permute-start(bf16[128,1024]{1,0:T(8,128)(2,1)} %get-tuple-element.231), channel_id=1, source_target_pairs={{0,0},{8,1},{16,2},{24,3},{4,4},{12,5},{20,6},{28,7},{1,8},{9,9},{... | collective-permute-start | bytes 786440 | tf_op jit(solution)/shard_map/ppermute | solution.py:774
  667.9 29.2 %collective-permute-start.85 = (bf16[128,1024]{1,0:T(8,128)(2,1)}, bf16[128,1024]{1,0:T(8,128)(2,1)}, u32[]{:S(2)}, u32[]{:S(2)}) collective-permute-start(bf16[128,1024]{1,0:T(8,128)(2,1)} %get-tuple-element.232), channel_id=1, source_target_pairs={{4,0},{12,1},{20,2},{28,3},{0,4},{8,5},{16,6},{24,7},{5,8},{13,9},... | collective-permute-start | bytes 786440 | tf_op jit(solution)/shard_map/ppermute | solution.py:774
  676.1 28.3 %collective-permute-start.87 = (bf16[128,768]{1,0:T(8,128)(2,1)}, bf16[128,768]{1,0:T(8,128)(2,1)S(1)}, u32[]{:S(2)}, u32[]{:S(2)}) collective-permute-start(bf16[128,768]{1,0:T(8,128)(2,1)} %get-tuple-element.216), channel_id=1, source_target_pairs={{0,8},{8,0},{16,24},{24,16},{1,9},{9,1},{17,25},{25,17},{2,10},{10... | collective-permute-start | bytes 589832 | tf_op jit(solution)/shard_map/ppermute | solution.py:87
  676.1 24.4 %collective-permute-start.94 = (bf16[2,32,768]{2,1,0:T(8,128)(2,1)S(1)}, bf16[2,32,768]{2,1,0:T(8,128)(2,1)S(1)}, u32[]{:S(2)}, u32[]{:S(2)}) collective-permute-start(bf16[2,32,768]{2,1,0:T(8,128)(2,1)S(1)} %get-tuple-element.290), channel_id=1, source_target_pairs={{0,2},{2,0},{1,3},{3,1},{4,6},{6,4},{5,7},{7,5},{8,10},{10,8},{9,1... | collective-permute-start | bytes 294920 | tf_op jit(solution)/shard_map/ppermute | solution.py:40
  679.3 22.8 %collective-permute-start.97 = (bf16[2,1,32,1024]{3,2,0,1:T(8,128)(2,1)}, bf16[2,1,32,1024]{3,2,0,1:T(8,128)(2,1)}, u32[]{:S(2)}, u32[]{:S(2)}) collective-permute-start(bf16[2,1,32,1024]{3,2,0,1:T(8,128)(2,1)} %get-tuple-element.268), channel_id=1, source_target_pairs={{0,1},{1,0},{2,3},{3,2},{4,5},{5,4},{6,7},{7,6},{8,9},{9,8},{10,11... | collective-permute-start | bytes 393224 | tf_op jit(solution)/shard_map/ppermute | solution.py:36
  699.6 15.1 %collective-permute-start.88 = (bf16[128,768]{1,0:T(8,128)(2,1)S(1)}, bf16[128,768]{1,0:T(8,128)(2,1)}, u32[]{:S(2)}, u32[]{:S(2)}) collective-permute-start(bf16[128,768]{1,0:T(8,128)(2,1)S(1)} %get-tuple-element.218), channel_id=1, source_target_pairs={{0,16},{8,24},{16,0},{24,8},{1,17},{9,25},{17,1},{25,9},{2,18},{10... | collective-permute-start | bytes 589832 | tf_op jit(solution)/shard_map/ppermute | solution.py:87
  699.7 32.4 %collective-permute-start.89 = (bf16[128,768]{1,0:T(8,128)(2,1)S(1)}, bf16[128,768]{1,0:T(8,128)(2,1)}, u32[]{:S(2)}, u32[]{:S(2)}) collective-permute-start(bf16[128,768]{1,0:T(8,128)(2,1)S(1)} %get-tuple-element.217), channel_id=1, source_target_pairs={{0,24},{8,16},{16,8},{24,0},{1,25},{9,17},{17,9},{25,1},{2,26},{10... | collective-permute-start | bytes 589832 | tf_op jit(solution)/shard_map/ppermute | solution.py:87
  (227 other events, 1865.0 us)
Sparse Core Ops, SparseCore 0:
  43.8 28.7 all-gather.10
  74.7 33.6 all-gather.12
  110.5 33.8 all-gather.14
  146.3 27.6 all-gather.16
  178.8 33.1 all-gather.18
  425.8 31.6 reduce-scatter.7
  486.1 19.9 reduce-scatter.5
  531.7 23.6 reduce-scatter.11
  589.0 53.1 reduce-scatter.13
  704.5 31.9 reduce-scatter.9
